TPU v7x, 32 devices: a whole 2x2x4 slice. The times are simulated.
32 devices in a mesh: lat: 4 (over y, x), lon: 4 (over z), mem: 2 (over core).
Axes of the slice: x: 2, y: 2, z: 4, core: 2. Of those that a mesh axis runs over, the one named last changes fastest.
Arguments:
- velo: float32 [2, 4, 128, 2048], P(None, None, 'lat', 'lon'), may hold values from -6 to 6
- temp: float32 [4, 128, 2048], P(None, 'lat', 'lon'), may hold values from -6 to 6
- land: int32 [128, 2048], P('lat', 'lon'), may hold values 0 or 1
- target: bfloat16 [2, 4, 32, 512], P(None, None, 'lat', 'lon'), may hold values from -3 to 3
- w_first: bfloat16 [4, 9, 64, 3], P('mem'), may hold values from -1.25 to 1.25
- w_middle: bfloat16 [4, 9, 64, 64], P('mem'), may hold values from -0.25 to 0.25
- w_last: bfloat16 [4, 9, 2, 64], P('mem'), may hold values from -0.25 to 0.25
Outputs:
- velo_next: float32 [2, 4, 128, 2048], P(None, None, 'lat', 'lon')
- temp_next: float32 [4, 128, 2048], P(None, 'lat', 'lon')
- grad_first: float32 [4, 9, 64, 3], P('mem')
- grad_middle: float32 [4, 9, 64, 64], P('mem')
- grad_last: float32 [4, 9, 2, 64], P('mem')
All inputs are finite; a program needn't handle non-finite values. No bound on the sum of `land` on one device may be relied on, other than what follows from the above.
Results may differ from a plain program's by a relative error of at most 0.0003.
Values may be sent and summed in bfloat16 or wider, within the bound.
No kernel may reach another device: no remote copies, remote signals or barrier semaphores. Data moves between devices by JAX's collectives and lax.ppermute only.
A program may use at most 128 MiB of HBM per device.

v0:
```python
import functools
import itertools
import math

import jax
import jax.numpy as jnp
from jax import lax
from jax.experimental import pallas as pl
from jax.experimental.pallas import tpu as pltpu
from jax.sharding import PartitionSpec as P

COARSE = 4
HALO = 5
SIDE = 16
F32 = jnp.float32
BF16 = jnp.bfloat16
HIGH = lax.Precision.HIGHEST
VMEM_LIMIT = 48 * 1024 * 1024


def dot(a, b, **kw):
    return jnp.dot(a, b, preferred_element_type=F32, **kw)


def dot_nt(a, b):
    return lax.dot_general(a, b, (((1,), (1,)), ((), ())), preferred_element_type=F32)


def lanes_of(shape):
    return lax.broadcasted_iota(jnp.int32, shape, len(shape) - 1)


def subs_of(shape):
    return lax.broadcasted_iota(jnp.int32, shape, len(shape) - 2)


def heads_up(axis):
    return (lax.axis_index(axis) + lax.axis_index("mem")) % 2 == 0


def coarse_kernel(velo, temp, target, own, message, fine):
    levels, rows, cols = temp.shape
    height, width = rows // COARSE, cols // COARSE
    vregs = levels + 1
    pool_r = subs_of((cols, width)) // COARSE
    pool = jnp.where(pool_r == lanes_of((cols, width)), F32(1.0 / COARSE**2), F32(0.0))

    def field(f):
        return temp if f == 2 else velo.at[f]

    means = []
    for f in range(3):
        ref = field(f)
        pieces = []
        for j in range(cols // 128):
            fine[j] = ref[:, :, 128 * j : 128 * (j + 1)].reshape(levels * rows, 128)
            part = None
            for s in range(COARSE):
                piece = fine[j, pl.ds(s, levels * height, stride=COARSE), :]
                part = piece if part is None else part + piece
            pieces.append(part)
        means.append(jnp.concatenate(pieces, 1))
    mean = dot(jnp.concatenate(means, 0), pool, precision=HIGH)
    mean = mean.astype(BF16).astype(F32)

    lane = lanes_of((height, 128))

    def place(tiles):
        pieces = []
        for j in range(vregs):
            value = jnp.zeros((height, 128), F32)
            if j < levels:
                moved = pltpu.roll(tiles[j], 32 * j + SIDE, 1)
                value = jnp.where(lane >= 32 * j + SIDE, moved, value)
            if j > 0:
                moved = pltpu.roll(tiles[j - 1], 32 * (j - 1) + SIDE, 1)
                value = jnp.where(lane < 32 * (j - 1) + SIDE, moved, value)
            pieces.append(value)
        return pieces

    for ch in range(8):
        if ch < 4:
            tiles = [target[ch % 2, l].astype(F32) for l in range(levels)]
        elif ch < 7:
            base = (ch - 4) * levels * height
            tiles = [mean[base + l * height : base + (l + 1) * height] for l in range(levels)]
        if ch < 7:
            pieces = place(tiles)
        else:
            pieces = [jnp.zeros((height, 128), F32)] * vregs
        for j in range(vregs):
            own[j, pl.ds(ch, height, stride=8), :] = pieces[j]
    lane = lanes_of((8 * height, 128))
    to_west = jnp.zeros((8 * height, 128), F32)
    to_east = jnp.zeros((8 * height, 128), F32)
    for l in range(levels):
        here = (lane >= 32 * l) & (lane < 32 * (l + 1))
        to_west = jnp.where(here, own[l], to_west)
        to_east = jnp.where(here, own[l + 1], to_east)
    lane = lanes_of((rows, 128))
    first = jnp.zeros((rows, 128), F32)
    last = jnp.zeros((rows, 128), F32)
    for f in range(3):
        ref = field(f)
        for l in range(levels):
            n = f * levels + l
            first = jnp.where(lane == n, pltpu.roll(ref[l, :, 0:128], n, 1), first)
            last = jnp.where(lane == n, pltpu.roll(ref[l, :, cols - 128 :], n + 1, 1), last)
    to_east = jnp.concatenate([to_east, last], 0)
    to_west = jnp.concatenate([to_west, first], 0)
    message[...] = jnp.where(heads_up("lon"), to_east, to_west)


def merge_kernel(velo, temp, own, got, other, full, message):
    levels, rows, cols = temp.shape
    vregs, tall = own.shape[:2]
    ahead = heads_up("lon")
    right = jnp.where(ahead, got[0:tall, :], other[0:tall, :])
    left = jnp.where(ahead, other[0:tall, :], got[0:tall, :])
    lane = lanes_of((tall, 128))
    for j in range(vregs):
        value = own[j]
        if j < levels:
            at = 32 * j + SIDE
            value = jnp.where((lane >= at - HALO) & (lane < at), left, value)
        if j > 0:
            at = 32 * (j - 1) + SIDE
            value = jnp.where((lane >= at) & (lane < at + HALO), right, value)
        full[j] = value
    deep = 8 * HALO
    ahead = heads_up("lat")
    for j in range(vregs):
        message[deep * j : deep * (j + 1), :] = jnp.where(ahead, full[j, tall - deep :, :], full[j, :deep, :])
    for f in range(3):
        ref = temp if f == 2 else velo.at[f]
        edge = jnp.where(ahead, ref[:, rows - 1, :], ref[:, 0, :])
        for j in range(cols // 128):
            at = deep * vregs + 16 * j + levels * f
            message[at : at + levels, :] = edge[:, 128 * j : 128 * (j + 1)]


def closure_kernel(
    scale, total_rows,
    full, got, other, wf, wm, wb, wl, wlt,
    force, *rest,
):
    nlat = lax.axis_size("lat")
    sends, (mine, xf, xb, h1, h2, yl, gb, d2, pf, gm, gf, gl, packed) = rest[: nlat - 1], rest[nlat - 1 :]
    vregs = full.shape[0]
    height = full.shape[1] // 8
    wide = 128 * vregs
    span = height + 2 * HALO
    first_row = lax.axis_index("lat") * height

    def inside(row):
        at = first_row + row
        return jnp.where((at >= 0) & (at < total_rows), F32(1.0), F32(0.0))

    ahead = heads_up("lat")
    deep = 8 * HALO
    for j in range(vregs):
        cols = slice(128 * j, 128 * (j + 1))
        near, far = got[deep * j : deep * (j + 1), :], other[deep * j : deep * (j + 1), :]
        xf[0:deep, cols] = jnp.where(ahead, far, near)
        xf[deep : deep + 8 * height, cols] = full[j]
        xf[deep + 8 * height :, cols] = jnp.where(ahead, near, far)

    sub = subs_of((8, wide))
    lane = lanes_of((1, wide))
    within = lane % (128 + 2 * SIDE)
    tile = (within >= SIDE) & (within < SIDE + 128)
    tile_f = jnp.where(tile, F32(1.0), F32(0.0))
    tile_b = tile_f.astype(BF16)

    def rows_of(ref, start, size, step):
        return ref[pl.ds(pl.multiple_of(start * step, step), size), :]

    def build(r, _):
        x = rows_of(xf, r, 8, 8)
        one = jnp.where(sub < 4, pltpu.roll(pltpu.roll(x, 1, 1), 4, 0), x)
        two = pltpu.roll(pltpu.roll(x, wide - 1, 1), 4, 0)
        xb[pl.ds(pl.multiple_of(16 * r, 16), 16), :] = jnp.concatenate([one, two], 0).astype(BF16)
        return 0

    lax.fori_loop(0, span, build, 0, unroll=2)

    def stage_one(q, _):
        pre = dot(wf[...], rows_of(xb, q, 48, 16))
        h = jnp.tanh(pre) * inside(q - 4)
        h1[pl.ds(pl.multiple_of(128 * q, 128), 128), :] = h.astype(BF16)
        return 0

    lax.fori_loop(0, height + 8, stage_one, 0)

    def stack(ref, r, m):
        return jnp.concatenate(
            [ref[pl.ds(pl.multiple_of(128 * (r + a) + 64 * m, 64), 64), :] for a in range(3)], 0
        )

    def stage_two(p, _):
        ok = inside(p - 3)
        halves = []
        for m in range(2):
            y = dot(wm[m], stack(h1, p, m))
            pre = pltpu.roll(y[0:64], 1, 1) + y[64:128] + pltpu.roll(y[128:192], wide - 1, 1)
            halves.append((jnp.tanh(pre) * ok).astype(BF16))
        row = jnp.concatenate(halves, 0)
        h2[pl.ds(pl.multiple_of(128 * p, 128), 128), :] = row
        yl[pl.ds(pl.multiple_of(72 * p, 8), 72), :] = dot(wl[...], row)
        return 0

    lax.fori_loop(0, height + 6, stage_two, 0)

    def stage_three(s, _):
        def part(a):
            return yl[pl.ds(pl.multiple_of(72 * (s + a) + 24 * a, 8), 24), :]

        z = part(0) + part(1) + part(2)
        pred = pltpu.roll(z[0:8], 1, 1) + z[8:16] + pltpu.roll(z[16:24], wide - 1, 1)
        goal = rows_of(xf, s + 3, 8, 8)
        g = ((pred - goal) * scale * inside(s - 2)).astype(BF16).astype(F32)
        one = jnp.where(sub < 4, pltpu.roll(g, wide - 1, 1), pltpu.roll(g, 4, 0))
        two = pltpu.roll(g, 1, 1)
        gb[pl.ds(pl.multiple_of(16 * s, 16), 16), :] = jnp.concatenate([one, two], 0).astype(BF16)
        both = pred + pltpu.roll(pred, 6, 0)
        pf[pl.ds(pl.multiple_of(8 * s, 8), 8), :] = both
        return 0

    lax.fori_loop(0, height + 4, stage_three, 0)
    force[...] = jnp.concatenate(
        [pf[8 * (r + 2) : 8 * (r + 2) + 2, :] for r in range(height)], 0
    ).astype(BF16)

    gl[...] = jnp.zeros_like(gl)
    gf[...] = jnp.zeros_like(gf)
    gm[...] = jnp.zeros_like(gm)

    def stage_four(u, _):
        g48 = rows_of(gb, u, 48, 16)
        hidden = rows_of(h2, u + 2, 128, 128).astype(F32)
        d = dot(wlt[...], g48) * (1.0 - hidden * hidden) * inside(u - 1)
        d2[pl.ds(pl.multiple_of(128 * u, 128), 128), :] = d.astype(BF16)
        return 0

    lax.fori_loop(0, height + 2, stage_four, 0)

    def stage_five(j, _):
        g48 = rows_of(gb, j + 1, 48, 16) * tile_b
        gl[...] += dot_nt(g48, rows_of(h2, j + 3, 128, 128))
        halves = []
        for m in range(2):
            y = dot(wb[m], stack(d2, j, m))
            pre = pltpu.roll(y[0:64], wide - 1, 1) + y[64:128] + pltpu.roll(y[128:192], 1, 1)
            hidden = h1[pl.ds(pl.multiple_of(128 * (j + 4) + 64 * m, 64), 64), :].astype(F32)
            halves.append((pre * (1.0 - hidden * hidden) * tile_f).astype(BF16))
            d = d2[pl.ds(pl.multiple_of(128 * (j + 1) + 64 * m, 64), 64), :] * tile_b
            moved = jnp.concatenate([pltpu.roll(d, wide - 1, 1), d, pltpu.roll(d, 1, 1)], 0)
            gm[m] += dot_nt(moved, stack(h1, j + 3, m))
        gf[...] += dot_nt(rows_of(xb, j + 4, 48, 16), jnp.concatenate(halves, 0))
        return 0

    lax.fori_loop(0, height, stage_five, 0)
    for m in range(2):
        packed[192 * m : 192 * (m + 1), :] = gm[m, :, 0:128]
    packed[384:576, :] = jnp.concatenate([gm[0, :, 128:192], gm[1, :, 128:192]], 1)
    pieces = [gf[16 * a : 16 * a + 12, :] for a in range(3)]
    last = gl[...]
    last = jnp.where(lanes_of(last.shape) < 64, last, pltpu.roll(last, 46, 0))
    pieces += [last[16 * s + 4 * b : 16 * s + 4 * b + 2] for s in range(3) for b in range(3)]
    pieces.append(jnp.zeros((packed.shape[0] - 576 - 54, 128), F32))
    packed[576:, :] = jnp.concatenate(pieces, 0)
    part = packed.shape[0] // nlat
    me = lax.axis_index("lat")
    for k, ref in enumerate((mine, *sends)):
        ref[...] = packed[pl.ds(pl.multiple_of((me ^ k) * part, 8), part), :]


def finish_kernel(*refs):
    nlat = lax.axis_size("lat")
    parts, (first, middle, last, packed) = refs[:nlat], refs[nlat:]
    part = parts[0].shape[0]
    me = lax.axis_index("lat")
    for k, ref in enumerate(parts):
        packed[pl.ds(pl.multiple_of((me ^ k) * part, 8), part), :] = ref[...]
    for m in range(2):
        for b in range(3):
            two = packed[192 * m + 64 * b : 192 * m + 64 * (b + 1), :]
            third = packed[384 + 64 * b : 384 + 64 * (b + 1), :]
            middle[m, b] = two[:, 0:64]
            middle[m, 3 + b] = two[:, 64:128]
            middle[m, 6 + b] = third[:, 64 * m : 64 * (m + 1)]
    rows = packed[576:640, :]
    turned = rows.T
    for m in range(2):
        for k in range(9):
            first[m, k] = turned[64 * m : 64 * (m + 1), 4 * k : 4 * k + 3]
            at = 36 + 2 * (3 * (2 - k // 3) + k % 3)
            last[m, k] = rows[at : at + 2, 64 * m : 64 * (m + 1)]


def ocean_kernel(
    total_rows, members,
    velo, temp, land, mine, other, got_lon, other_lon, got_lat, other_lat,
    velo_next, temp_next,
):
    levels, rows, cols = temp.shape
    at = got_lon.shape[0] - rows
    ahead = heads_up("lon")
    ceast = jnp.where(ahead, got_lon[at:, :], other_lon[at:, :])
    cwest = jnp.where(ahead, other_lon[at:, :], got_lon[at:, :])
    ahead = heads_up("lat")
    at = got_lat.shape[0] - 16 * (cols // 128)
    near, far = (
        jnp.concatenate([ref[at + 16 * j : at + 16 * (j + 1), :] for j in range(cols // 128)], 1)
        for ref in (got_lat, other_lat)
    )
    rnorth, rsouth = jnp.where(ahead, near, far), jnp.where(ahead, far, near)
    height, width = rows // COARSE, cols // COARSE
    row = subs_of((rows, cols))
    lane = lanes_of((rows, cols))
    ids = (lax.axis_index("lat") * rows + subs_of((rows, 128))).astype(F32)
    coriolis = jnp.sin(F32(-math.pi / 2) + F32(math.pi) * (ids + 0.5) / F32(total_rows))
    coriolis = jnp.concatenate([coriolis] * (cols // 128), 1)
    wet = land[...].astype(F32) * 0.1
    up = [
        jnp.where(lanes_of((rows, 2 * height)) == subs_of((rows, 2 * height)) // COARSE * 2 + o, F32(1.0), F32(0.0)).astype(BF16)
        for o in range(2)
    ]
    tall = [[dot(u, ref[...]).astype(BF16) for ref in (mine, other)] for u in up]
    spread_k = subs_of((256, cols))
    spread_i = lanes_of((256, cols)) // COARSE

    def neighbours(q, n):
        east = jnp.where(lane == cols - 1, ceast[:, n : n + 1], pltpu.roll(q, cols - 1, 1))
        west = jnp.where(lane == 0, cwest[:, n : n + 1], pltpu.roll(q, 1, 1))
        north = jnp.where(row == rows - 1, rnorth[n : n + 1, :], pltpu.roll(q, rows - 1, 0))
        south = jnp.where(row == 0, rsouth[n : n + 1, :], pltpu.roll(q, 1, 0))
        return east, west, north, south

    cum_x = cum_y = None
    for l in range(levels):
        u, v, t = velo[0, l], velo[1, l], temp[l]
        ue, uw, un, us = neighbours(u, l)
        ve, vw, vn, vs = neighbours(v, levels + l)
        te, tw, tn, ts = neighbours(t, 2 * levels + l)
        dx, dy = te - tw, tn - ts
        cum_x = dx if cum_x is None else cum_x + dx
        cum_y = dy if cum_y is None else cum_y + dy
        spread = jnp.where(spread_k == spread_i + (32 * l + SIDE), F32(1.0), F32(0.0)).astype(BF16)
        f = []
        for o in range(2):
            total = None
            for part in tall[o]:
                term = dot(part[:, 128 * l : 128 * (l + 2)], spread)
                total = term if total is None else total + term
            f.append(total * (1.0 / members))
        lap_u = ue + uw + un + us - 4.0 * u
        lap_v = ve + vw + vn + vs - 4.0 * v
        lap_t = te + tw + tn + ts - 4.0 * t
        velo_next[0, l] = u + wet * (coriolis * v + 0.25 * cum_x + 0.5 * lap_u + f[0])
        velo_next[1, l] = v + wet * (0.25 * cum_y - coriolis * u + 0.5 * lap_v + f[1])
        temp_next[l] = t + wet * (0.3 * lap_t - 0.5 * (u * dx + v * dy))


def prepare(w_first, w_middle, w_last):
    m = w_first.shape[0]
    hid = w_middle.shape[-1]
    eye = jnp.eye(m, dtype=BF16)
    wf = w_first.reshape(m, 3, 3, hid, 3)
    wf = jnp.transpose(wf, (0, 3, 1, 2, 4)).reshape(m * hid, 3, 3, 3)
    wf = jnp.pad(wf, ((0, 0), (0, 0), (0, 0), (0, 1))).reshape(m * hid, 3, 12)
    wf = jnp.pad(wf, ((0, 0), (0, 0), (0, 4))).reshape(m * hid, 48)
    mid = w_middle.reshape(m, 3, 3, hid, hid)
    wm = jnp.transpose(mid, (0, 2, 3, 1, 4)).reshape(m, 3 * hid, 3 * hid)
    wb = jnp.transpose(mid[:, ::-1], (0, 2, 4, 1, 3)).reshape(m, 3 * hid, 3 * hid)
    last = w_last.reshape(m, 3, 3, 2, hid)
    wl = jnp.einsum("mn,maboc->abmonc", eye, last).reshape(3, 3, 2 * m, m * hid)
    wl = jnp.pad(wl, ((0, 0), (0, 0), (0, 8 - 2 * m), (0, 0))).reshape(72, m * hid)
    wlt = jnp.einsum("mn,maboc->mcabno", eye, last[:, ::-1]).reshape(m * hid, 3, 6 * m)
    wlt = jnp.pad(wlt, ((0, 0), (0, 0), (0, 16 - 6 * m))).reshape(m * hid, 48)
    return wf, wm, wb, wl, wlt


def swap_pairs(axis, wrap):
    names = ("lat", "lon", "mem")
    sizes = [lax.axis_size(name) for name in names]
    where = names.index(axis)
    pairs = []
    for index in itertools.product(*(range(n) for n in sizes)):
        place = list(index)
        place[where] += 1 if (index[where] + index[2]) % 2 == 0 else -1
        if wrap:
            place[where] %= sizes[where]
        if 0 <= place[where] < sizes[where]:
            flat = [(i[0] * sizes[1] + i[1]) * sizes[2] + i[2] for i in (index, place)]
            pairs.append(tuple(flat))
    return pairs


def swap(value, axis, wrap):
    got = lax.ppermute(value, ("lat", "lon", "mem"), swap_pairs(axis, wrap))
    return got, swap_cores(got)


def swap_cores(value):
    return lax.ppermute(value, "mem", [(i, i ^ 1) for i in range(lax.axis_size("mem"))])


def partner(value, axis, k):
    return lax.ppermute(value, axis, [(i, i ^ k) for i in range(lax.axis_size(axis))])


def tree_sum(values):
    while len(values) > 1:
        values = [sum(values[i : i + 2][1:], values[i]) for i in range(0, len(values), 2)]
    return values[0]


def per_device(velo, temp, land, target, w_first, w_middle, w_last):
    levels, rows, cols = temp.shape
    height, width = rows // COARSE, cols // COARSE
    wide = levels * (width + 2 * SIDE)
    vregs = wide // 128
    members = w_first.shape[0] * lax.axis_size("mem")
    nlat, nlon = lax.axis_size("lat"), lax.axis_size("lon")
    total_coarse = height * nlat
    count = 2.0 * levels * total_coarse * width * nlon
    params = pltpu.CompilerParams(vmem_limit_bytes=VMEM_LIMIT)
    vm = pltpu.VMEM

    def f32(*shape):
        return jax.ShapeDtypeStruct(shape, F32)

    own, message = pl.pallas_call(
        coarse_kernel,
        out_shape=(f32(vregs, 8 * height, 128), f32(8 * height + rows, 128)),
        scratch_shapes=[vm((cols // 128, levels * rows, 128), F32)],
        compiler_params=params,
        name="coarse",
    )(velo, temp, target)
    got_lon, other_lon = swap(message, "lon", True)
    full, message = pl.pallas_call(
        merge_kernel,
        out_shape=(f32(vregs, 8 * height, 128), f32(8 * HALO * vregs + 16 * (cols // 128), 128)),
        compiler_params=params,
        name="merge",
    )(velo, temp, own, got_lon, other_lon)
    got_lat, other_lat = swap(message, "lat", False)

    weights = prepare(w_first, w_middle, w_last)
    total = 640
    part = total // nlat
    force, *sends, mine = pl.pallas_call(
        functools.partial(closure_kernel, 2.0 / count, total_coarse),
        out_shape=(jax.ShapeDtypeStruct((2 * height, wide), BF16), *[f32(part, 128)] * nlat),
        scratch_shapes=[
            vm((8 * (height + 2 * HALO), wide), F32),
            vm((16 * (height + 2 * HALO), wide), BF16),
            vm((128 * (height + 8), wide), BF16),
            vm((128 * (height + 6), wide), BF16),
            vm((72 * (height + 6), wide), F32),
            vm((16 * (height + 4), wide), BF16),
            vm((128 * (height + 2), wide), BF16),
            vm((8 * (height + 4), wide), F32),
            vm((2, 192, 192), F32),
            vm((48, 128), F32),
            vm((48, 128), F32),
            vm((total, 128), F32),
        ],
        compiler_params=params,
        name="closure",
    )(full, got_lat, other_lat, *weights)

    parts = [partner(value, "lat", k + 1) for k, value in enumerate(sends)]
    other = swap_cores(force)
    velo_next, temp_next = pl.pallas_call(
        functools.partial(ocean_kernel, rows * nlat, members),
        out_shape=(jax.ShapeDtypeStruct(velo.shape, F32), jax.ShapeDtypeStruct(temp.shape, F32)),
        cost_estimate=pl.CostEstimate(flops=10**8, bytes_accessed=4 * 10**6, transcendentals=0),
        compiler_params=params,
        name="ocean",
    )(velo, temp, land, force, other, got_lon, other_lon, got_lat, other_lat)

    summed = tree_sum([mine, *parts])
    summed = tree_sum([summed] + [partner(summed, "lon", k) for k in range(1, nlon)])
    parts = [summed] + [partner(summed, "lat", k) for k in range(1, nlat)]
    grads = pl.pallas_call(
        finish_kernel,
        out_shape=tuple(f32(*w.shape) for w in (w_first, w_middle, w_last)),
        scratch_shapes=[vm((total, 128), F32)],
        compiler_params=params,
        name="finish",
    )(*parts)
    return (velo_next, temp_next, *grads)


def solution(mesh):
    return jax.shard_map(
        per_device,
        mesh=mesh,
        in_specs=(
            P(None, None, "lat", "lon"),
            P(None, "lat", "lon"),
            P("lat", "lon"),
            P(None, None, "lat", "lon"),
            P("mem", None, None, None),
            P("mem", None, None, None),
            P("mem", None, None, None),
        ),
        out_specs=(
            P(None, None, "lat", "lon"),
            P(None, "lat", "lon"),
            P("mem", None, None, None),
            P("mem", None, None, None),
            P("mem", None, None, None),
        ),
        check_vma=False,
    )
```

profile of v0, /device:TPU:0, one launch (start us, length us, event | category | flops | bytes accessed | tf_op | source)
XLA Modules:
  0.0 70.3 jit_solution(1720811835683463436)
XLA Ops:
  0.6 0.0 copy-start
  0.6 1.0 %copy-done = f32[2,4,32,512]{3,2,1,0:T(8,128)S(1)} copy-done((f32[2,4,32,512]{3,2,1,0:T(8,128)S(1)}, f32[2,4,32,512]{3,2,1,0:T(8,128)}, u32[]{:S(2)}) %copy-start) | copy-done | bytes 524312
  1.7 0.9 %copy-done.2 = f32[4,32,512]{2,1,0:T(8,128)S(1)} copy-done((f32[4,32,512]{2,1,0:T(8,128)S(1)}, f32[4,32,512]{2,1,0:T(8,128)}, u32[]{:S(2)}) %copy-start.2) | copy-done | bytes 262168
  2.6 0.7 %copy-done.5 = bf16[2,4,8,128]{3,2,1,0:T(8,128)(2,1)S(1)} copy-done((bf16[2,4,8,128]{3,2,1,0:T(8,128)(2,1)S(1)}, bf16[2,4,8,128]{3,2,1,0:T(8,128)(2,1)}, u32[]{:S(2)}) %copy-start.5) | copy-done | bytes 16408
  3.3 0.5 coarse.1
  3.8 3.1 %collective-permute-start = (f32[96,128]{1,0:T(8,128)S(1)}, f32[96,128]{1,0:T(8,128)S(1)}, u32[]{:S(2)}, u32[]{:S(2)}) collective-permute-start(f32[96,128]{1,0:T(8,128)S(1)} %get-tuple-element.20), channel_id=1, source_target_pairs={{0,2},{1,7},{2,0},{3,5},{4,6},{5,3},{6,4},{7,1},{8,10},{9,15},{10,... | collective-permute-start | bytes 147464 | tf_op jit(solution)/shard_map/ppermute | solution.py:401
  6.9 2.1 %collective-permute-done.got.got_lon = f32[96,128]{1,0:T(8,128)S(1)} collective-permute-done((f32[96,128]{1,0:T(8,128)S(1)}, f32[96,128]{1,0:T(8,128)S(1)}, u32[]{:S(2)}, u32[]{:S(2)}) %collective-permute-start) | collective-permute-done | bytes 49184 | tf_op jit(solution)/shard_map/ppermute | solution.py:401
  9.0 1.0 %collective-permute-start.1 = (f32[96,128]{1,0:T(8,128)S(1)}, f32[96,128]{1,0:T(8,128)S(1)}, u32[]{:S(2)}, u32[]{:S(2)}) collective-permute-start(f32[96,128]{1,0:T(8,128)S(1)} %collective-permute-done.got.got_lon), channel_id=1, source_target_pairs={{0,1},{1,0},{2,3},{3,2},{4,5},{5,4},{6,7},{7,6},{8,9},{9,8},{10,11... | collective-permute-start | bytes 147464 | tf_op jit(solution)/shard_map/ppermute | solution.py:406
  10.0 0.9 %collective-permute-done.1.other.other_lon = f32[96,128]{1,0:T(8,128)S(1)} collective-permute-done((f32[96,128]{1,0:T(8,128)S(1)}, f32[96,128]{1,0:T(8,128)S(1)}, u32[]{:S(2)}, u32[]{:S(2)}) %collective-permute-start.1) | collective-permute-done | bytes 49184 | tf_op jit(solution)/shard_map/ppermute | solution.py:406
  10.9 3.5 %collective-permute-start.2 = (f32[264,128]{1,0:T(8,128)S(1)}, f32[264,128]{1,0:T(8,128)S(1)}, u32[]{:S(2)}, u32[]{:S(2)}) collective-permute-start(f32[264,128]{1,0:T(8,128)S(1)} %get-tuple-element.22), channel_id=1, source_target_pairs={{0,8},{2,10},{4,12},{6,14},{8,0},{9,17},{10,2},{11,19},{12,4},{13,... | collective-permute-start | bytes 405512 | tf_op jit(solution)/shard_map/ppermute | solution.py:401
  14.5 0.3 copy.27
  14.8 0.3 copy.35
  15.0 4.0 %collective-permute-done.2.got.got_lat = f32[264,128]{1,0:T(8,128)S(1)} collective-permute-done((f32[264,128]{1,0:T(8,128)S(1)}, f32[264,128]{1,0:T(8,128)S(1)}, u32[]{:S(2)}, u32[]{:S(2)}) %collective-permute-start.2) | collective-permute-done | bytes 135200 | tf_op jit(solution)/shard_map/ppermute | solution.py:401
  19.1 0.1 multiply_bitcast_fusion
  19.2 0.1 reshape.56
  19.3 0.1 copy.32.wlt
  19.4 0.1 reshape.54
  19.5 1.5 %rev.6 = bf16[2,3,3,64,64]{3,1,4,2,0:T(4,128)(2,1)S(1)} reverse(bf16[2,3,3,64,64]{3,1,4,2,0:T(4,128)(2,1)S(1)} %copy.27), dimensions={1} | reverse | bytes 294912 | tf_op jit(solution)/shard_map/rev | solution.py:375
  21.0 0.3 reshape.52.wb
  21.2 0.0 copy-start.8
  21.2 0.3 reshape.51.wm
  21.5 0.5 copy-done.8
  22.0 0.1 reshape.47
  22.1 0.1 copy.31.wf
  22.2 0.0 collective-permute-done.3.other.other_lat
  22.2 0.0 copy-start.4
  22.2 21.6 %closure.1 = (bf16[16,640]{1,0:T(8,128)(2,1)S(1)}, f32[160,128]{1,0:T(8,128)S(1)}, f32[160,128]{1,0:T(8,128)S(1)}, f32[160,128]{1,0:T(8,128)S(1)}, f32[160,128]{1,0:T(8,128)S(1)}) custom-call(f32[5,64,128]{2,1,0:T(8,128)S(1)} %get-tuple-element.21.full, f32[264,128]{1,0:T(8,128)S(1)} %collective-permute-done.2.got.got_lat, ...), custom_call_target="tpu_custom_call" | custom-call | tf_op jit(solution)/shard_map/closure/pallas_call | solution.py:453
  43.8 0.0 copy-start.1
  43.8 1.4 %collective-permute-start.5 = (f32[160,128]{1,0:T(8,128)S(1)}, f32[160,128]{1,0:T(8,128)S(1)}, u32[]{:S(2)}, u32[]{:S(2)}) collective-permute-start(f32[160,128]{1,0:T(8,128)S(1)} %get-tuple-element.27), channel_id=1, source_target_pairs={{0,8},{8,0},{16,24},{24,16},{1,9},{9,1},{17,25},{25,17},{2,10},{10... | collective-permute-start | bytes 245768 | tf_op jit(solution)/shard_map/ppermute | solution.py:410
  45.2 1.4 %collective-permute-start.6 = (f32[160,128]{1,0:T(8,128)S(1)}, f32[160,128]{1,0:T(8,128)S(1)}, u32[]{:S(2)}, u32[]{:S(2)}) collective-permute-start(f32[160,128]{1,0:T(8,128)S(1)} %get-tuple-element.28), channel_id=1, source_target_pairs={{0,16},{8,24},{16,0},{24,8},{1,17},{9,25},{17,1},{25,9},{2,18},{10... | collective-permute-start | bytes 245768 | tf_op jit(solution)/shard_map/ppermute | solution.py:410
  46.6 0.8 %collective-permute-start.7 = (f32[160,128]{1,0:T(8,128)S(1)}, f32[160,128]{1,0:T(8,128)S(1)}, u32[]{:S(2)}, u32[]{:S(2)}) collective-permute-start(f32[160,128]{1,0:T(8,128)S(1)} %get-tuple-element.29), channel_id=1, source_target_pairs={{0,24},{8,16},{16,8},{24,0},{1,25},{9,17},{17,9},{25,1},{2,26},{10... | collective-permute-start | bytes 245768 | tf_op jit(solution)/shard_map/ppermute | solution.py:410
  47.4 1.4 %collective-permute-done.5 = f32[160,128]{1,0:T(8,128)S(1)} collective-permute-done((f32[160,128]{1,0:T(8,128)S(1)}, f32[160,128]{1,0:T(8,128)S(1)}, u32[]{:S(2)}, u32[]{:S(2)}) %collective-permute-start.5) | collective-permute-done | bytes 81952 | tf_op jit(solution)/shard_map/ppermute | solution.py:410
  48.7 1.7 %collective-permute-done.6 = f32[160,128]{1,0:T(8,128)S(1)} collective-permute-done((f32[160,128]{1,0:T(8,128)S(1)}, f32[160,128]{1,0:T(8,128)S(1)}, u32[]{:S(2)}, u32[]{:S(2)}) %collective-permute-start.6) | collective-permute-done | bytes 81952 | tf_op jit(solution)/shard_map/ppermute | solution.py:410
  50.4 1.5 %collective-permute-done.7 = f32[160,128]{1,0:T(8,128)S(1)} collective-permute-done((f32[160,128]{1,0:T(8,128)S(1)}, f32[160,128]{1,0:T(8,128)S(1)}, u32[]{:S(2)}, u32[]{:S(2)}) %collective-permute-start.7) | collective-permute-done | bytes 81952 | tf_op jit(solution)/shard_map/ppermute | solution.py:410
  51.9 0.0 copy-start.3
  51.9 3.6 %collective-permute-start.10 = (f32[160,128]{1,0:T(8,128)S(1)}, f32[160,128]{1,0:T(8,128)S(1)}, u32[]{:S(2)}, u32[]{:S(2)}) collective-permute-start(f32[160,128]{1,0:T(8,128)S(1)} %add_add_fusion.1), channel_id=1, source_target_pairs={{0,6},{2,4},{4,2},{6,0},{1,7},{3,5},{5,3},{7,1},{8,14},{10,12},{12... | collective-permute-start | bytes 245768 | tf_op jit(solution)/shard_map/ppermute | solution.py:410
  55.5 0.8 %collective-permute-start.9 = (f32[160,128]{1,0:T(8,128)S(1)}, f32[160,128]{1,0:T(8,128)S(1)}, u32[]{:S(2)}, u32[]{:S(2)}) collective-permute-start(f32[160,128]{1,0:T(8,128)S(1)} %add_add_fusion.1), channel_id=1, source_target_pairs={{0,4},{2,6},{4,0},{6,2},{1,5},{3,7},{5,1},{7,3},{8,12},{10,14},{12... | collective-permute-start | bytes 245768 | tf_op jit(solution)/shard_map/ppermute | solution.py:410
  56.4 2.0 %collective-permute-done.10 = f32[160,128]{1,0:T(8,128)S(1)} collective-permute-done((f32[160,128]{1,0:T(8,128)S(1)}, f32[160,128]{1,0:T(8,128)S(1)}, u32[]{:S(2)}, u32[]{:S(2)}) %collective-permute-start.10) | collective-permute-done | bytes 81952 | tf_op jit(solution)/shard_map/ppermute | solution.py:410
  58.4 2.7 %collective-permute-done.8 = f32[160,128]{1,0:T(8,128)S(1)} collective-permute-done((f32[160,128]{1,0:T(8,128)S(1)}, f32[160,128]{1,0:T(8,128)S(1)}, u32[]{:S(2)}, u32[]{:S(2)}) %collective-permute-start.8) | collective-permute-done | bytes 81952 | tf_op jit(solution)/shard_map/ppermute | solution.py:410
  61.1 0.0 collective-permute-done.9
  61.1 1.1 %collective-permute-start.11 = (f32[160,128]{1,0:T(8,128)S(1)}, f32[160,128]{1,0:T(8,128)S(1)}, u32[]{:S(2)}, u32[]{:S(2)}) collective-permute-start(f32[160,128]{1,0:T(8,128)S(1)} %add_add_fusion.refs_0_), channel_id=1, source_target_pairs={{0,8},{8,0},{16,24},{24,16},{1,9},{9,1},{17,25},{25,17},{2,10},{10... | collective-permute-start | bytes 245768 | tf_op jit(solution)/shard_map/ppermute | solution.py:410
  62.2 0.9 %collective-permute-start.12 = (f32[160,128]{1,0:T(8,128)S(1)}, f32[160,128]{1,0:T(8,128)S(1)}, u32[]{:S(2)}, u32[]{:S(2)}) collective-permute-start(f32[160,128]{1,0:T(8,128)S(1)} %add_add_fusion.refs_0_), channel_id=1, source_target_pairs={{0,16},{8,24},{16,0},{24,8},{1,17},{9,25},{17,1},{25,9},{2,18},{10... | collective-permute-start | bytes 245768 | tf_op jit(solution)/shard_map/ppermute | solution.py:410
  63.1 1.6 %collective-permute-start.13 = (f32[160,128]{1,0:T(8,128)S(1)}, f32[160,128]{1,0:T(8,128)S(1)}, u32[]{:S(2)}, u32[]{:S(2)}) collective-permute-start(f32[160,128]{1,0:T(8,128)S(1)} %add_add_fusion.refs_0_), channel_id=1, source_target_pairs={{0,24},{8,16},{16,8},{24,0},{1,25},{9,17},{17,9},{25,1},{2,26},{10... | collective-permute-start | bytes 245768 | tf_op jit(solution)/shard_map/ppermute | solution.py:410
  64.7 1.2 %collective-permute-done.4.other = bf16[16,640]{1,0:T(8,128)(2,1)S(1)} collective-permute-done((bf16[16,640]{1,0:T(8,128)(2,1)S(1)}, bf16[16,640]{1,0:T(8,128)(2,1)S(1)}, u32[]{:S(2)}, u32[]{:S(2)}) %collective-permute-start.4) | collective-permute-done | bytes 20512 | tf_op jit(solution)/shard_map/ppermute | solution.py:406
  65.9 1.9 %ocean.1 = (f32[2,4,32,512]{3,2,1,0:T(8,128)}, f32[4,32,512]{2,1,0:T(8,128)}) custom-call(f32[2,4,32,512]{3,2,1,0:T(8,128)S(1)} %copy-done.1, f32[4,32,512]{2,1,0:T(8,128)S(1)} %copy-done.3, s32[32,512]{1,0:T(8,128)S(1)} %copy-done.4, bf16[16,640]{1,0:T(8,128)(2,1)S(1)} %get-tuple-element.23.mine, bf16[16,640]{1,0:T(8,128)(2,1)S(1)} %collective-permute-done.4.other, ...), custom_call_target="tpu_custom_call" | custom-call | flops 100000000 | bytes 4000000 | tf_op jit(solution)/shard_map/ocean/pallas_call | solution.py:476
  67.8 0.6 collective-permute-done.13.refs_3_
  68.4 1.1 %finish.1 = (f32[2,9,64,3]{3,2,1,0:T(8,128)S(1)}, f32[2,9,64,64]{3,2,1,0:T(8,128)}, f32[2,9,2,64]{3,2,1,0:T(2,128)}) custom-call(f32[160,128]{1,0:T(8,128)S(1)} %add_add_fusion.refs_0_, f32[160,128]{1,0:T(8,128)S(1)} %collective-permute-done.11.refs_1_, f32[160,128]{1,0:T(8,128)S(1)} %collective-permute-done.12.refs_2_, ...), custom_call_target="tpu_custom_call" | custom-call | tf_op jit(solution)/shard_map/finish/pallas_call | solution.py:487
  69.5 0.8 %copy.33 = f32[2,9,64,3]{2,0,3,1:T(2,128)} copy(f32[2,9,64,3]{3,2,1,0:T(8,128)S(1)} %get-tuple-element.45) | data formatting | bytes 27648
  (27 shorter events, 0.2 us)
Async XLA Ops:
  0.6 1.0 %copy-start = (f32[2,4,32,512]{3,2,1,0:T(8,128)S(1)}, f32[2,4,32,512]{3,2,1,0:T(8,128)}, u32[]{:S(2)}) copy-start(f32[2,4,32,512]{3,2,1,0:T(8,128)} %velo.5) | copy-start | bytes 1572868
  1.7 0.9 %copy-start.2 = (f32[4,32,512]{2,1,0:T(8,128)S(1)}, f32[4,32,512]{2,1,0:T(8,128)}, u32[]{:S(2)}) copy-start(f32[4,32,512]{2,1,0:T(8,128)} %temp.5) | copy-start | bytes 786436
  2.6 0.7 %copy-start.5 = (bf16[2,4,8,128]{3,2,1,0:T(8,128)(2,1)S(1)}, bf16[2,4,8,128]{3,2,1,0:T(8,128)(2,1)}, u32[]{:S(2)}) copy-start(bf16[2,4,8,128]{3,2,1,0:T(8,128)(2,1)} %target.1) | copy-start | bytes 49156
  3.8 5.2 %collective-permute-start = (f32[96,128]{1,0:T(8,128)S(1)}, f32[96,128]{1,0:T(8,128)S(1)}, u32[]{:S(2)}, u32[]{:S(2)}) collective-permute-start(f32[96,128]{1,0:T(8,128)S(1)} %get-tuple-element.20), channel_id=1, source_target_pairs={{0,2},{1,7},{2,0},{3,5},{4,6},{5,3},{6,4},{7,1},{8,10},{9,15},{10,... | collective-permute-start | bytes 147464 | tf_op jit(solution)/shard_map/ppermute | solution.py:401
  9.0 1.9 %collective-permute-start.1 = (f32[96,128]{1,0:T(8,128)S(1)}, f32[96,128]{1,0:T(8,128)S(1)}, u32[]{:S(2)}, u32[]{:S(2)}) collective-permute-start(f32[96,128]{1,0:T(8,128)S(1)} %collective-permute-done.got.got_lon), channel_id=1, source_target_pairs={{0,1},{1,0},{2,3},{3,2},{4,5},{5,4},{6,7},{7,6},{8,9},{9,8},{10,11... | collective-permute-start | bytes 147464 | tf_op jit(solution)/shard_map/ppermute | solution.py:406
  10.9 3.6 %copy-start.7 = (bf16[2,9,2,64]{3,2,1,0:T(2,128)(2,1)S(1)}, bf16[2,9,2,64]{3,2,1,0:T(2,128)(2,1)}, u32[]{:S(2)}) copy-start(bf16[2,9,2,64]{3,2,1,0:T(2,128)(2,1)} %param.13) | copy-start | bytes 13828
  10.9 3.6 %copy-start.6 = (bf16[2,9,64,64]{3,2,1,0:T(8,128)(2,1)S(1)}, bf16[2,9,64,64]{3,2,1,0:T(8,128)(2,1)}, u32[]{:S(2)}) copy-start(bf16[2,9,64,64]{3,2,1,0:T(8,128)(2,1)} %param.12) | copy-start | bytes 442372
  10.9 8.1 %collective-permute-start.2 = (f32[264,128]{1,0:T(8,128)S(1)}, f32[264,128]{1,0:T(8,128)S(1)}, u32[]{:S(2)}, u32[]{:S(2)}) collective-permute-start(f32[264,128]{1,0:T(8,128)S(1)} %get-tuple-element.22), channel_id=1, source_target_pairs={{0,8},{2,10},{4,12},{6,14},{8,0},{9,17},{10,2},{11,19},{12,4},{13,... | collective-permute-start | bytes 405512 | tf_op jit(solution)/shard_map/ppermute | solution.py:401
  19.1 3.2 %collective-permute-start.3 = (f32[264,128]{1,0:T(8,128)S(1)}, f32[264,128]{1,0:T(8,128)S(1)}, u32[]{:S(2)}, u32[]{:S(2)}) collective-permute-start(f32[264,128]{1,0:T(8,128)S(1)} %collective-permute-done.2.got.got_lat), channel_id=1, source_target_pairs={{0,1},{1,0},{2,3},{3,2},{4,5},{5,4},{6,7},{7,6},{8,9},{9,8},{10,11... | collective-permute-start | bytes 405512 | tf_op jit(solution)/shard_map/ppermute | solution.py:406
  21.2 0.7 %copy-start.8 = (bf16[2,9,64,3]{2,0,3,1:T(2,128)(2,1)S(1)}, bf16[2,9,64,3]{2,0,3,1:T(2,128)(2,1)}, u32[]{:S(2)}) copy-start(bf16[2,9,64,3]{2,0,3,1:T(2,128)(2,1)} %param.11) | copy-start | bytes 20740
  22.2 43.6 %copy-start.4 = (s32[32,512]{1,0:T(8,128)S(1)}, s32[32,512]{1,0:T(8,128)}, u32[]{:S(2)}) copy-start(s32[32,512]{1,0:T(8,128)} %land.1) | copy-start | bytes 196612
  43.8 22.1 %copy-start.1 = (f32[2,4,32,512]{3,2,1,0:T(8,128)S(1)}, f32[2,4,32,512]{3,2,1,0:T(8,128)}, u32[]{:S(2)}) copy-start(f32[2,4,32,512]{3,2,1,0:T(8,128)} %velo.5) | copy-start | bytes 1572868
  43.8 4.9 %collective-permute-start.5 = (f32[160,128]{1,0:T(8,128)S(1)}, f32[160,128]{1,0:T(8,128)S(1)}, u32[]{:S(2)}, u32[]{:S(2)}) collective-permute-start(f32[160,128]{1,0:T(8,128)S(1)} %get-tuple-element.27), channel_id=1, source_target_pairs={{0,8},{8,0},{16,24},{24,16},{1,9},{9,1},{17,25},{25,17},{2,10},{10... | collective-permute-start | bytes 245768 | tf_op jit(solution)/shard_map/ppermute | solution.py:410
  45.2 5.3 %collective-permute-start.6 = (f32[160,128]{1,0:T(8,128)S(1)}, f32[160,128]{1,0:T(8,128)S(1)}, u32[]{:S(2)}, u32[]{:S(2)}) collective-permute-start(f32[160,128]{1,0:T(8,128)S(1)} %get-tuple-element.28), channel_id=1, source_target_pairs={{0,16},{8,24},{16,0},{24,8},{1,17},{9,25},{17,1},{25,9},{2,18},{10... | collective-permute-start | bytes 245768 | tf_op jit(solution)/shard_map/ppermute | solution.py:410
  46.6 5.3 %collective-permute-start.7 = (f32[160,128]{1,0:T(8,128)S(1)}, f32[160,128]{1,0:T(8,128)S(1)}, u32[]{:S(2)}, u32[]{:S(2)}) collective-permute-start(f32[160,128]{1,0:T(8,128)S(1)} %get-tuple-element.29), channel_id=1, source_target_pairs={{0,24},{8,16},{16,8},{24,0},{1,25},{9,17},{17,9},{25,1},{2,26},{10... | collective-permute-start | bytes 245768 | tf_op jit(solution)/shard_map/ppermute | solution.py:410
  51.9 13.9 %copy-start.3 = (f32[4,32,512]{2,1,0:T(8,128)S(1)}, f32[4,32,512]{2,1,0:T(8,128)}, u32[]{:S(2)}) copy-start(f32[4,32,512]{2,1,0:T(8,128)} %temp.5) | copy-start | bytes 786436
  51.9 6.5 %collective-permute-start.10 = (f32[160,128]{1,0:T(8,128)S(1)}, f32[160,128]{1,0:T(8,128)S(1)}, u32[]{:S(2)}, u32[]{:S(2)}) collective-permute-start(f32[160,128]{1,0:T(8,128)S(1)} %add_add_fusion.1), channel_id=1, source_target_pairs={{0,6},{2,4},{4,2},{6,0},{1,7},{3,5},{5,3},{7,1},{8,14},{10,12},{12... | collective-permute-start | bytes 245768 | tf_op jit(solution)/shard_map/ppermute | solution.py:410
  55.5 5.5 %collective-permute-start.8 = (f32[160,128]{1,0:T(8,128)S(1)}, f32[160,128]{1,0:T(8,128)S(1)}, u32[]{:S(2)}, u32[]{:S(2)}) collective-permute-start(f32[160,128]{1,0:T(8,128)S(1)} %add_add_fusion.1), channel_id=1, source_target_pairs={{0,2},{2,0},{4,6},{6,4},{1,3},{3,1},{5,7},{7,5},{8,10},{10,8},{12,... | collective-permute-start | bytes 245768 | tf_op jit(solution)/shard_map/ppermute | solution.py:410
  55.5 5.5 %collective-permute-start.9 = (f32[160,128]{1,0:T(8,128)S(1)}, f32[160,128]{1,0:T(8,128)S(1)}, u32[]{:S(2)}, u32[]{:S(2)}) collective-permute-start(f32[160,128]{1,0:T(8,128)S(1)} %add_add_fusion.1), channel_id=1, source_target_pairs={{0,4},{2,6},{4,0},{6,2},{1,5},{3,7},{5,1},{7,3},{8,12},{10,14},{12... | collective-permute-start | bytes 245768 | tf_op jit(solution)/shard_map/ppermute | solution.py:410
  61.1 6.6 %collective-permute-start.11 = (f32[160,128]{1,0:T(8,128)S(1)}, f32[160,128]{1,0:T(8,128)S(1)}, u32[]{:S(2)}, u32[]{:S(2)}) collective-permute-start(f32[160,128]{1,0:T(8,128)S(1)} %add_add_fusion.refs_0_), channel_id=1, source_target_pairs={{0,8},{8,0},{16,24},{24,16},{1,9},{9,1},{17,25},{25,17},{2,10},{10... | collective-permute-start | bytes 245768 | tf_op jit(solution)/shard_map/ppermute | solution.py:410
  62.2 5.6 %collective-permute-start.12 = (f32[160,128]{1,0:T(8,128)S(1)}, f32[160,128]{1,0:T(8,128)S(1)}, u32[]{:S(2)}, u32[]{:S(2)}) collective-permute-start(f32[160,128]{1,0:T(8,128)S(1)} %add_add_fusion.refs_0_), channel_id=1, source_target_pairs={{0,16},{8,24},{16,0},{24,8},{1,17},{9,25},{17,1},{25,9},{2,18},{10... | collective-permute-start | bytes 245768 | tf_op jit(solution)/shard_map/ppermute | solution.py:410
  63.1 5.3 %collective-permute-start.13 = (f32[160,128]{1,0:T(8,128)S(1)}, f32[160,128]{1,0:T(8,128)S(1)}, u32[]{:S(2)}, u32[]{:S(2)}) collective-permute-start(f32[160,128]{1,0:T(8,128)S(1)} %add_add_fusion.refs_0_), channel_id=1, source_target_pairs={{0,24},{8,16},{16,8},{24,0},{1,25},{9,17},{17,9},{25,1},{2,26},{10... | collective-permute-start | bytes 245768 | tf_op jit(solution)/shard_map/ppermute | solution.py:410
  64.7 1.2 %collective-permute-start.4 = (bf16[16,640]{1,0:T(8,128)(2,1)S(1)}, bf16[16,640]{1,0:T(8,128)(2,1)S(1)}, u32[]{:S(2)}, u32[]{:S(2)}) collective-permute-start(bf16[16,640]{1,0:T(8,128)(2,1)S(1)} %get-tuple-element.23.mine), channel_id=1, source_target_pairs={{0,1},{1,0},{2,3},{3,2},{4,5},{5,4},{6,7},{7,6},{8,9},{9,8},{10,11... | collective-permute-start | bytes 61448 | tf_op jit(solution)/shard_map/ppermute | solution.py:406
where the time goes:
time: 70.7 us; the launch traced here: 70.3 us
  Pallas kernels  25.1 us (36%)
  starting transfers between devices  19.2 us (27%)
  waiting for transfers between devices  18 us (25%)
  local copies, waits for them, and re-layouts  7.13 us (10%)
  between operations  0.83 us (1%)
    pallas_call x1, Pallas kernels, per_device(): pl.pallas_call(functools.partial(closure_kernel, 2.0 / count, total_coars...  21.6 us
    ppermute x9, starting transfers between devices, partner(): lax.ppermute(value, axis, [(i, i ^ k) for i in range(lax.axis_size(axis))])  11.6 us
    ppermute x9, waiting for transfers between devices, partner(): lax.ppermute(value, axis, [(i, i ^ k) for i in range(lax.axis_size(axis))])  9.87 us
    ppermute x2, starting transfers between devices, swap(): got = lax.ppermute(value, ('lat', 'lon', 'mem'), swap_pairs(axis, wrap))  6.62 us
    ppermute x2, waiting for transfers between devices, swap(): got = lax.ppermute(value, ('lat', 'lon', 'mem'), swap_pairs(axis, wrap))  6.07 us
    unnamed x19, local copies, waits for them, and re-layouts  4.03 us
    ppermute x3, waiting for transfers between devices, swap_cores(): lax.ppermute(value, 'mem', [(i, i ^ 1) for i in range(lax.axis_size('mem'...  2.07 us
    pallas_call x1, Pallas kernels, per_device(): pl.pallas_call(functools.partial(ocean_kernel, rows * nlat, members), out...  1.88 us
  transfers between devices with their start and end apart: 14, of which 10 were waited for; matrix products, arithmetic and copies ran while one was open for 5% of the time, Pallas kernels for 3%

commit v1 on v0

v1 whole, which is shorter than its diff:
```python
import functools
import itertools
import math

import jax
import jax.numpy as jnp
from jax import lax
from jax.experimental import pallas as pl
from jax.experimental.pallas import tpu as pltpu
from jax.sharding import PartitionSpec as P

COARSE = 4
HALO = 5
GROUP = 16
LEVELS = 32000.0
H1_ROWS = 4
SIDE = 16
F32 = jnp.float32
BF16 = jnp.bfloat16
HIGH = lax.Precision.HIGHEST
VMEM_LIMIT = 48 * 1024 * 1024
COARSE_LIMIT = 64 * 1024 * 1024 - 512 * 1024


def dot(a, b, **kw):
    return jnp.dot(a, b, preferred_element_type=F32, **kw)


def dot_nt(a, b):
    return lax.dot_general(a, b, (((1,), (1,)), ((), ())), preferred_element_type=F32)


def lanes_of(shape):
    return lax.broadcasted_iota(jnp.int32, shape, len(shape) - 1)


def subs_of(shape):
    return lax.broadcasted_iota(jnp.int32, shape, len(shape) - 2)


def heads_up(axis):
    return (lax.axis_index(axis) + lax.axis_index("mem")) % 2 == 0


def halves(x):
    high = x.astype(BF16).astype(F32)
    return [high, x - high]


def encode(x):
    coded, exponents = [], []
    for at in range(0, x.shape[0], GROUP):
        part = x[at : at + GROUP]
        most = jnp.max(jnp.abs(part), axis=0, keepdims=True)
        exponent = jnp.ceil(jnp.log2(jnp.maximum(most, 1e-30)))
        coded.append(jnp.round(part * (jnp.exp2(-exponent) * LEVELS)))
        exponents.append(exponent)
    exponents.append(jnp.zeros((GROUP - len(exponents), x.shape[1]), F32))
    return jnp.concatenate(coded + exponents, 0).astype(jnp.int32).astype(jnp.int16)


def decode(ref):
    value = ref[...].astype(jnp.int32).astype(F32)
    rows = value.shape[0] - GROUP
    scale = jnp.exp2(value[rows:]) * (1.0 / LEVELS)
    pieces = [value[at : at + GROUP] * scale[i : i + 1] for i, at in enumerate(range(0, rows, GROUP))]
    return jnp.concatenate(pieces, 0)


def coarse_kernel(
    velo_hbm, temp_hbm, target_hbm, own, to_lon, edges, velo, temp, target, fine, sems
):
    copies = [
        pltpu.make_async_copy(velo_hbm.at[0], velo.at[0], sems.at[0]),
        pltpu.make_async_copy(velo_hbm.at[1], velo.at[1], sems.at[1]),
        pltpu.make_async_copy(temp_hbm, temp, sems.at[2]),
        pltpu.make_async_copy(target_hbm, target, sems.at[3]),
    ]
    for copy in copies:
        copy.start()
    levels, rows, cols = temp.shape
    height, width = rows // COARSE, cols // COARSE
    vregs = levels + 1
    pool_r = subs_of((cols, width)) // COARSE
    pool = jnp.where(pool_r == lanes_of((cols, width)), F32(1.0 / COARSE**2), F32(0.0))

    def field(f):
        return temp if f == 2 else velo.at[f]

    means = []
    for f in range(3):
        copies[f].wait()
        ref = field(f)
        pieces = []
        for j in range(cols // 128):
            fine[j] = ref[:, :, 128 * j : 128 * (j + 1)].reshape(levels * rows, 128)
            part = None
            for s in range(COARSE):
                piece = fine[j, pl.ds(s, levels * height, stride=COARSE), :]
                part = piece if part is None else part + piece
            pieces.append(part)
        means.append(jnp.concatenate(pieces, 1))
    mean = dot(jnp.concatenate(means, 0), pool, precision=HIGH)
    mean = mean.astype(BF16).astype(F32)

    copies[3].wait()
    lane = lanes_of((height, 128))

    def place(tiles):
        pieces = []
        for j in range(vregs):
            value = jnp.zeros((height, 128), F32)
            if j < levels:
                moved = pltpu.roll(tiles[j], 32 * j + SIDE, 1)
                value = jnp.where(lane >= 32 * j + SIDE, moved, value)
            if j > 0:
                moved = pltpu.roll(tiles[j - 1], 32 * (j - 1) + SIDE, 1)
                value = jnp.where(lane < 32 * (j - 1) + SIDE, moved, value)
            pieces.append(value)
        return pieces

    for ch in range(8):
        if ch < 4:
            tiles = [target[ch % 2, l].astype(F32) for l in range(levels)]
        elif ch < 7:
            base = (ch - 4) * levels * height
            tiles = [mean[base + l * height : base + (l + 1) * height] for l in range(levels)]
        if ch < 7:
            pieces = place(tiles)
        else:
            pieces = [jnp.zeros((height, 128), F32)] * vregs
        for j in range(vregs):
            own[j, pl.ds(ch, height, stride=8), :] = pieces[j]
    lane = lanes_of((8 * height, 128))
    to_west = jnp.zeros((8 * height, 128), F32)
    to_east = jnp.zeros((8 * height, 128), F32)
    for l in range(levels):
        here = (lane >= 32 * l) & (lane < 32 * (l + 1))
        to_west = jnp.where(here, own[l], to_west)
        to_east = jnp.where(here, own[l + 1], to_east)
    lane = lanes_of((rows, 128))
    first = jnp.zeros((rows, 128), F32)
    last = jnp.zeros((rows, 128), F32)
    for f in range(3):
        ref = field(f)
        for l in range(levels):
            n = f * levels + l
            first = jnp.where(lane == n, pltpu.roll(ref[l, :, 0:128], n, 1), first)
            last = jnp.where(lane == n, pltpu.roll(ref[l, :, cols - 128 :], n + 1, 1), last)
    tall = 8 * height
    east, north = heads_up("lon"), heads_up("lat")
    cells = jnp.where(east, to_east, to_west)
    to_lon[...] = jnp.concatenate([cells] + halves(jnp.where(east, last, first)), 0).astype(BF16)
    line = [jnp.where(north, field(f)[:, rows - 1, :], field(f)[:, 0, :]) for f in range(3)]
    line = [part[:, 128 * j : 128 * (j + 1)] for j in range(cols // 128) for part in line]
    edges[...] = jnp.concatenate(line, 0)


def merge_kernel(own, got, other, edges, full, message):
    vregs, tall = own.shape[:2]
    levels, deep = vregs - 1, 8 * HALO
    ahead, north = heads_up("lon"), heads_up("lat")
    near, far = (ref[...].astype(F32)[0:tall] for ref in (got, other))
    right, left = jnp.where(ahead, near, far), jnp.where(ahead, far, near)
    lane = lanes_of((tall, 128))
    pieces = []
    for j in range(vregs):
        value = own[j]
        if j < levels:
            at = 32 * j + SIDE
            value = jnp.where((lane >= at - HALO) & (lane < at), left, value)
        if j > 0:
            at = 32 * (j - 1) + SIDE
            value = jnp.where((lane >= at) & (lane < at + HALO), right, value)
        full[j] = value
        pieces.append(jnp.where(north, value[tall - deep :], value[:deep]))
    pieces.append(jnp.zeros((-deep * vregs % 16, 128), F32))
    message[...] = jnp.concatenate(pieces + halves(edges[...]), 0).astype(BF16)


def closure_kernel(
    scale, total_rows,
    full, got, other, wf, wm, wb, wl, wlt,
    force, *rest,
):
    nlat = lax.axis_size("lat")
    sends, (mine, xf, xb, h1, h2, yl, gb, d2, pf, packed) = rest[: nlat - 1], rest[nlat - 1 :]
    vregs = full.shape[0]
    height = full.shape[1] // 8
    wide = 128 * vregs
    span = height + 2 * HALO
    first_row = lax.axis_index("lat") * height

    def inside(row):
        at = first_row + row
        return jnp.where((at >= 0) & (at < total_rows), F32(1.0), F32(0.0))

    deep = 8 * HALO
    north = heads_up("lat")
    got, other = got[...].astype(F32), other[...].astype(F32)
    for j in range(vregs):
        near, far = got[deep * j : deep * (j + 1)], other[deep * j : deep * (j + 1)]
        above, below = jnp.where(north, near, far), jnp.where(north, far, near)
        xf[:, 128 * j : 128 * (j + 1)] = jnp.concatenate([below, full[j], above], 0)

    sub = subs_of((8, wide))
    lane = lanes_of((1, wide))
    within = lane % (128 + 2 * SIDE)
    tile = (within >= SIDE) & (within < SIDE + 128)
    tile_f = jnp.where(tile, F32(1.0), F32(0.0))
    tile_b = tile_f.astype(BF16)

    def window(ref, row, rows, step):
        return ref[step * row : step * (row + rows), :]

    def quad(get, row, left):
        return get(row) if left <= 2 else jnp.concatenate([get(row), get(row + 2)], 1)

    for r in range(span):
        x = window(xf, r, 1, 8)
        one = jnp.where(sub < 4, pltpu.roll(pltpu.roll(x, 1, 1), 4, 0), x)
        two = pltpu.roll(pltpu.roll(x, wide - 1, 1), 4, 0)
        xb[16 * r : 16 * (r + 1), :] = jnp.concatenate([one, two], 0).astype(BF16)

    step = wf.shape[0] // 128
    for q in range(0, height + 8, step):
        pre = dot(wf[...], window(xb, q, step + 2, 16))
        for i in range(step):
            h = (jnp.tanh(pre[128 * i : 128 * (i + 1)]) * inside(q + i - 4)).astype(BF16)
            for m in range(2):
                h1[m, 64 * (q + i) : 64 * (q + i + 1), :] = h[64 * m : 64 * (m + 1)]

    def columns(y, rr, t, sign):
        part = [y[192 * rr + 64 * b : 192 * rr + 64 * (b + 1), wide * t : wide * (t + 1)] for b in range(3)]
        return pltpu.roll(part[0], sign % wide, 1) + part[1] + pltpu.roll(part[2], -sign % wide, 1)

    rows = height + 6
    for p in range(0, rows, 4):
        for m in range(2):
            y = dot(wm[m], quad(lambda r: h1[m, 64 * r : 64 * (r + 4), :], p, rows - p))
            for i in range(min(4, rows - p)):
                h = jnp.tanh(columns(y, i % 2, i // 2, 1)) * inside(p + i - 3)
                at = 128 * (p + i) + 64 * m
                h2[at : at + 64, :] = h.astype(BF16)
        for i in range(p, min(p + 4, rows), 2):
            yl[72 * i : 72 * (i + 2), :] = dot(wl[...], window(h2, i, 2, 128))

    for s in range(height + 4):
        z = sum(yl[72 * (s + a) + 24 * a : 72 * (s + a) + 24 * (a + 1), :] for a in range(3))
        pred = pltpu.roll(z[0:8], 1, 1) + z[8:16] + pltpu.roll(z[16:24], wide - 1, 1)
        goal = window(xf, s + 3, 1, 8)
        g = ((pred - goal) * scale * inside(s - 2)).astype(BF16).astype(F32)
        one = jnp.where(sub < 4, pltpu.roll(g, wide - 1, 1), pltpu.roll(g, 4, 0))
        two = pltpu.roll(g, 1, 1)
        gb[16 * s : 16 * (s + 1), :] = jnp.concatenate([one, two], 0).astype(BF16)
        if 2 <= s < height + 2:
            both = pred + pltpu.roll(pred, 6, 0)
            pf[2 * (s - 2) : 2 * (s - 1), :] = both[0:2]
    force[...] = pf[...].astype(BF16)

    for u in range(height + 2):
        hidden = window(h2, u + 2, 1, 128).astype(F32)
        d = dot(wlt[...], window(gb, u, 3, 16)) * (1.0 - hidden * hidden) * inside(u - 1)
        for m in range(2):
            d2[m, 64 * u : 64 * (u + 1), :] = d[64 * m : 64 * (m + 1)].astype(BF16)

    sum_l = sum_f = None
    sum_m = [None, None]

    def add(total, term):
        return term if total is None else total + term

    for j in range(0, height, 4):
        left = height - j
        g = quad(lambda r: window(gb, r + 1, 4, 16) * tile_b, j, left)
        sum_l = add(sum_l, dot_nt(g, quad(lambda r: window(h2, r + 3, 2, 128), j, left)))
        d1 = [[None, None] for _ in range(4)]
        for m in range(2):
            y = dot(wb[m], quad(lambda r: d2[m, 64 * r : 64 * (r + 4), :], j, left))
            for i in range(4):
                hidden = h1[m, 64 * (j + i + 4) : 64 * (j + i + 5), :].astype(F32)
                d = columns(y, i % 2, i // 2, -1) * (1.0 - hidden * hidden) * tile_f
                d1[i][m] = d.astype(BF16)

            def moved(r):
                pieces = []
                for i in range(2):
                    d = d2[m, 64 * (r + i + 1) : 64 * (r + i + 2), :] * tile_b
                    pieces += [pltpu.roll(d, wide - 1, 1), d, pltpu.roll(d, 1, 1)]
                return jnp.concatenate(pieces, 0)

            rhs = quad(lambda r: h1[m, 64 * (r + 3) : 64 * (r + 7), :], j, left)
            sum_m[m] = add(sum_m[m], dot_nt(quad(moved, j, left), rhs))
        x = quad(lambda r: window(xb, r + 4, 4, 16), j, left)
        sum_f = add(sum_f, dot_nt(x, quad(lambda r: jnp.concatenate(d1[r - j] + d1[r - j + 1], 0), j, left)))
    gl = sum_l[0:48, 0:128] + sum_l[16:64, 128:256]
    gf = sum_f[0:48, 0:128] + sum_f[16:64, 128:256]
    gm = [t[0:192, 0:192] + t[192:384, 64:256] for t in sum_m]
    for m in range(2):
        packed[192 * m : 192 * (m + 1), :] = gm[m][:, 0:128]
    packed[384:576, :] = jnp.concatenate([gm[0][:, 128:192], gm[1][:, 128:192]], 1)
    pieces = [gf[16 * a : 16 * a + 12, :] for a in range(3)]
    last = jnp.where(lanes_of(gl.shape) < 64, gl, pltpu.roll(gl, 46, 0))
    pieces += [last[16 * s + 4 * b : 16 * s + 4 * b + 2] for s in range(3) for b in range(3)]
    pieces.append(jnp.zeros((packed.shape[0] - 576 - 54, 128), F32))
    packed[576:, :] = jnp.concatenate(pieces, 0)
    part = packed.shape[0] // nlat
    me = lax.axis_index("lat")
    for k, ref in enumerate((mine, *sends)):
        value = packed[pl.ds(pl.multiple_of((me ^ k) * part, 8), part), :]
        ref[...] = value if k == 0 else encode(value)


def tree_sum(values):
    while len(values) > 1:
        values = [sum(values[i : i + 2][1:], values[i]) for i in range(0, len(values), 2)]
    return values[0]


def sum_kernel(*refs):
    parts, out = refs[:-1], refs[-1]
    out[...] = encode(tree_sum([ref[...] if ref.dtype == F32 else decode(ref) for ref in parts]))


def finish_kernel(*refs):
    nlat = lax.axis_size("lat")
    parts, (first, middle, last, packed) = refs[:nlat], refs[nlat:]
    part = parts[0].shape[0] - GROUP
    me = lax.axis_index("lat")
    for k, ref in enumerate(parts):
        packed[pl.ds(pl.multiple_of((me ^ k) * part, 8), part), :] = decode(ref)
    for m in range(2):
        for b in range(3):
            two = packed[192 * m + 64 * b : 192 * m + 64 * (b + 1), :]
            third = packed[384 + 64 * b : 384 + 64 * (b + 1), :]
            middle[m, b] = two[:, 0:64]
            middle[m, 3 + b] = two[:, 64:128]
            middle[m, 6 + b] = third[:, 64 * m : 64 * (m + 1)]
    rows = packed[576:640, :]
    for m in range(2):
        for k in range(9):
            for c in range(3):
                first[k, c, m : m + 1] = rows[4 * k + c : 4 * k + c + 1, 64 * m : 64 * (m + 1)]
            at = 36 + 2 * (3 * (2 - k // 3) + k % 3)
            last[m, k] = rows[at : at + 2, 64 * m : 64 * (m + 1)]


def ocean_kernel(
    total_rows, members,
    velo, temp, land, mine, other, got_lon, other_lon, got_lat, other_lat,
    velo_next, temp_next,
):
    levels, rows, cols = temp.shape

    def whole(ref, at, size):
        value = ref[...].astype(F32)
        return value[at : at + size] + value[at + size : at + 2 * size]

    ahead = heads_up("lon")
    near, far = (whole(ref, ref.shape[0] - 2 * rows, rows) for ref in (got_lon, other_lon))
    ceast, cwest = jnp.where(ahead, near, far), jnp.where(ahead, far, near)
    ahead = heads_up("lat")
    lines = 3 * levels * (cols // 128)
    near, far = (whole(ref, ref.shape[0] - 2 * lines, lines) for ref in (got_lat, other_lat))
    near, far = (
        jnp.concatenate([x[3 * levels * j : 3 * levels * (j + 1)] for j in range(cols // 128)], 1) for x in (near, far)
    )
    rnorth, rsouth = jnp.where(ahead, near, far), jnp.where(ahead, far, near)
    height, width = rows // COARSE, cols // COARSE
    row = subs_of((rows, cols))
    lane = lanes_of((rows, cols))
    ids = (lax.axis_index("lat") * rows + subs_of((rows, 128))).astype(F32)
    coriolis = jnp.sin(F32(-math.pi / 2) + F32(math.pi) * (ids + 0.5) / F32(total_rows))
    coriolis = jnp.concatenate([coriolis] * (cols // 128), 1)
    wet = land[...].astype(F32) * 0.1
    up = [
        jnp.where(lanes_of((rows, 2 * height)) == subs_of((rows, 2 * height)) // COARSE * 2 + o, F32(1.0), F32(0.0)).astype(BF16)
        for o in range(2)
    ]
    tall = [[dot(u, ref[...]).astype(BF16) for ref in (mine, other)] for u in up]
    spread_k = subs_of((256, cols))
    spread_i = lanes_of((256, cols)) // COARSE

    def neighbours(q, n):
        east = jnp.where(lane == cols - 1, ceast[:, n : n + 1], pltpu.roll(q, cols - 1, 1))
        west = jnp.where(lane == 0, cwest[:, n : n + 1], pltpu.roll(q, 1, 1))
        north = jnp.where(row == rows - 1, rnorth[n : n + 1], pltpu.roll(q, rows - 1, 0))
        south = jnp.where(row == 0, rsouth[n : n + 1], pltpu.roll(q, 1, 0))
        return east, west, north, south

    cum_x = cum_y = None
    for l in range(levels):
        u, v, t = velo[0, l], velo[1, l], temp[l]
        ue, uw, un, us = neighbours(u, l)
        ve, vw, vn, vs = neighbours(v, levels + l)
        te, tw, tn, ts = neighbours(t, 2 * levels + l)
        dx, dy = te - tw, tn - ts
        cum_x = dx if cum_x is None else cum_x + dx
        cum_y = dy if cum_y is None else cum_y + dy
        spread = jnp.where(spread_k == spread_i + (32 * l + SIDE), F32(1.0), F32(0.0)).astype(BF16)
        f = []
        for o in range(2):
            total = None
            for part in tall[o]:
                term = dot(part[:, 128 * l : 128 * (l + 2)], spread)
                total = term if total is None else total + term
            f.append(total * (1.0 / members))
        lap_u = ue + uw + un + us - 4.0 * u
        lap_v = ve + vw + vn + vs - 4.0 * v
        lap_t = te + tw + tn + ts - 4.0 * t
        velo_next[0, l] = u + wet * (coriolis * v + 0.25 * cum_x + 0.5 * lap_u + f[0])
        velo_next[1, l] = v + wet * (0.25 * cum_y - coriolis * u + 0.5 * lap_v + f[1])
        temp_next[l] = t + wet * (0.3 * lap_t - 0.5 * (u * dx + v * dy))


def weights_kernel(first, middle, last, wf, wm, wb, wl, wlt):
    hid = middle.shape[-1]

    def slide(pieces, copies):
        zero = jnp.zeros_like(pieces[0])
        return [jnp.concatenate([zero] * r + pieces + [zero] * (copies - 1 - r), 1) for r in range(copies)]

    for m in range(2):
        for b in range(3):
            taps = [middle[m, 3 * a + b] for a in range(3)]
            turned = jnp.concatenate([t.astype(F32) for t in taps[::-1]], 0).T.astype(BF16)
            turned = [turned[:, hid * s : hid * (s + 1)] for s in range(3)]
            for ref, pieces in ((wm, taps), (wb, turned)):
                for r, block in enumerate(slide(pieces, 2)):
                    at = hid * (3 * r + b)
                    ref[m, at : at + hid, :] = block
    zero = jnp.zeros((1, 2 * hid), F32)
    rows = []
    for a in range(3):
        for b in range(4):
            for c in range(4):
                if b < 3 and c < 3:
                    w = first[3 * a + b, c].astype(F32)
                    rows.append(jnp.concatenate([w[0:1], w[1:2]], 1))
                else:
                    rows.append(zero)
    turned = jnp.concatenate(rows + [zero] * (2 * hid - 48), 0).T
    for r in range(H1_ROWS):
        wf[2 * hid * r : 2 * hid * (r + 1), :] = pltpu.roll(turned, 16 * r, 1).astype(BF16)[:, : wf.shape[1]]
    zero = jnp.zeros((2, hid), F32)
    block = []
    for k in range(9):
        w = [last[m, k].astype(F32) for m in range(2)]
        tops = [jnp.concatenate([w[0], zero], 1), jnp.concatenate([zero, w[1]], 1)]
        block.append(jnp.concatenate(tops + [jnp.zeros((4, 2 * hid), F32)], 0))
    for r, rows in enumerate(slide([jnp.concatenate(block, 0)], 2)):
        wl[72 * r : 72 * (r + 1), :] = rows.astype(BF16)
    rows = [block[3 * (2 - s) + b][0:4] if b < 3 else jnp.zeros((4, 2 * hid), F32) for s in range(3) for b in range(4)]
    wlt[...] = jnp.concatenate(rows, 0).T.astype(BF16)


def pairs_of(lat=None, lon=None):
    sizes = [lax.axis_size(name) for name in ("lat", "lon", "mem")]
    pairs = []
    for index in itertools.product(*(range(n) for n in sizes)):
        place = list(index)
        if lat is not None:
            place[0] += 1 if (index[0] + lat[index[2]]) % 2 == 0 else -1
        if lon is not None:
            place[1] += 1 if (index[1] + lon[index[2]]) % 2 == 0 else -1
            place[1] %= sizes[1]
        if 0 <= place[0] < sizes[0]:
            pairs.append(tuple((i[0] * sizes[1] + i[1]) * sizes[2] + i[2] for i in (index, place)))
    return pairs


def swap(value, pairs):
    got = lax.ppermute(value, ("lat", "lon", "mem"), pairs)
    return got, swap_cores(got)


def swap_cores(value):
    return lax.ppermute(value, "mem", [(i, i ^ 1) for i in range(lax.axis_size("mem"))])


def partner(value, axis, k):
    return lax.ppermute(value, axis, [(i, i ^ k) for i in range(lax.axis_size(axis))])


def per_device(velo, temp, land, target, w_first, w_middle, w_last):
    levels, rows, cols = temp.shape
    height, width = rows // COARSE, cols // COARSE
    wide = levels * (width + 2 * SIDE)
    vregs = wide // 128
    members = w_first.shape[0] * lax.axis_size("mem")
    nlat, nlon = lax.axis_size("lat"), lax.axis_size("lon")
    total_coarse = height * nlat
    count = 2.0 * levels * total_coarse * width * nlon
    params = pltpu.CompilerParams(vmem_limit_bytes=VMEM_LIMIT)
    vm = pltpu.VMEM

    def f32(*shape):
        return jax.ShapeDtypeStruct(shape, F32)

    def bf16(*shape):
        return jax.ShapeDtypeStruct(shape, BF16)

    hid = w_middle.shape[-1]
    hbm = pl.BlockSpec(memory_space=pltpu.HBM)
    deep, tall = 8 * HALO, 8 * height
    core = (0, 1)
    own, to_lon, edges = pl.pallas_call(
        coarse_kernel,
        in_specs=[hbm, hbm, hbm],
        out_shape=(
            vm((vregs, tall, 128), F32),
            vm((tall + 2 * rows, 128), BF16),
            vm((3 * levels * (cols // 128), 128), F32),
        ),
        scratch_shapes=[
            vm(velo.shape, F32),
            vm(temp.shape, F32),
            vm(target.shape, BF16),
            vm((cols // 128, levels * rows, 128), F32),
            pltpu.SemaphoreType.DMA((4,)),
        ],
        compiler_params=pltpu.CompilerParams(vmem_limit_bytes=COARSE_LIMIT),
        name="coarse",
    )(velo, temp, target)
    got_lon, other_lon = swap(to_lon, pairs_of(lon=core))
    full, to_lat = pl.pallas_call(
        merge_kernel,
        out_shape=(f32(vregs, tall, 128), bf16(-(-deep * vregs // 16) * 16 + 2 * edges.shape[0], 128)),
        compiler_params=params,
        name="merge",
    )(own, got_lon, other_lon, edges)
    got_lat, other_lat = swap(to_lat, pairs_of(lat=core))

    weights = pl.pallas_call(
        weights_kernel,
        out_shape=(
            bf16(H1_ROWS * 2 * hid, 16 * (H1_ROWS + 2)),
            bf16(2, 6 * hid, 4 * hid),
            bf16(2, 6 * hid, 4 * hid),
            bf16(144, 4 * hid),
            bf16(2 * hid, 48),
        ),
        cost_estimate=pl.CostEstimate(flops=10**7, bytes_accessed=4 * 10**6, transcendentals=0),
        compiler_params=params,
        name="weights",
    )(jnp.transpose(w_first, (1, 3, 0, 2)), w_middle, w_last)
    total = -(-630 // (GROUP * nlat)) * GROUP * nlat
    part = total // nlat
    force, *sends, mine = pl.pallas_call(
        functools.partial(closure_kernel, 2.0 / count, total_coarse),
        out_shape=(
            bf16(2 * height, wide),
            *[jax.ShapeDtypeStruct((part + GROUP, 128), jnp.int16)] * (nlat - 1),
            f32(part, 128),
        ),
        scratch_shapes=[
            vm((8 * (height + 2 * HALO), wide), F32),
            vm((16 * (height + 2 * HALO), wide), BF16),
            vm((2, 64 * (height + 8), wide), BF16),
            vm((128 * (height + 6), wide), BF16),
            vm((72 * (height + 6), wide), F32),
            vm((16 * (height + 4), wide), BF16),
            vm((2, 64 * (height + 2), wide), BF16),
            vm((2 * height, wide), F32),
            vm((total, 128), F32),
        ],
        compiler_params=params,
        name="closure",
    )(full, got_lat, other_lat, *weights)

    parts = [partner(value, "lat", k + 1) for k, value in enumerate(sends)]
    other = swap_cores(force)
    velo_next, temp_next = pl.pallas_call(
        functools.partial(ocean_kernel, rows * nlat, members),
        out_shape=(jax.ShapeDtypeStruct(velo.shape, F32), jax.ShapeDtypeStruct(temp.shape, F32)),
        cost_estimate=pl.CostEstimate(flops=10**8, bytes_accessed=4 * 10**6, transcendentals=0),
        compiler_params=params,
        name="ocean",
    )(velo, temp, land, force, other, got_lon, other_lon, got_lat, other_lat)

    def add_up(values, name):
        return pl.pallas_call(
            sum_kernel,
            out_shape=jax.ShapeDtypeStruct((part + GROUP, 128), jnp.int16),
            compiler_params=params,
            name=name,
        )(*values)

    summed = add_up([mine, *parts], "sum_lat")
    summed = add_up([summed] + [partner(summed, "lon", k) for k in range(1, nlon)], "sum_lon")
    parts = [summed] + [partner(summed, "lat", k) for k in range(1, nlat)]
    members_here, taps, _, inputs = w_first.shape
    first, middle, last = pl.pallas_call(
        finish_kernel,
        out_shape=(f32(taps, inputs, members_here, hid), f32(*w_middle.shape), f32(*w_last.shape)),
        scratch_shapes=[vm((total, 128), F32)],
        compiler_params=params,
        name="finish",
    )(*parts)
    return (velo_next, temp_next, jnp.transpose(first, (2, 0, 3, 1)), middle, last)


def solution(mesh):
    return jax.shard_map(
        per_device,
        mesh=mesh,
        in_specs=(
            P(None, None, "lat", "lon"),
            P(None, "lat", "lon"),
            P("lat", "lon"),
            P(None, None, "lat", "lon"),
            P("mem", None, None, None),
            P("mem", None, None, None),
            P("mem", None, None, None),
        ),
        out_specs=(
            P(None, None, "lat", "lon"),
            P(None, "lat", "lon"),
            P("mem", None, None, None),
            P("mem", None, None, None),
            P("mem", None, None, None),
        ),
        check_vma=False,
    )
```

time: 70.7 us -> 52.3 us (0.74)
  Pallas kernels: 25.1 us -> 14.2 us
  local copies, waits for them, and re-layouts: 7.13 us -> 0.98 us
  waiting for transfers between devices: 18 us -> 17 us
    pallas_call x1, Pallas kernels: 21.6 us -> 8.86 us  [per_device(): pl.pallas_call(functools.partial(closure_kernel, 2.0 / count, total_coars...]
    unnamed x19 -> x12, local copies, waits for them, and re-layouts: 4.03 us -> 0.98 us
    pallas_call x3 -> x6, Pallas kernels: 1.62 us -> 3.44 us  [the longest x1 1.67 us: per_device(): pl.pallas_call(coarse_kernel, in_specs=[hbm, hbm, hbm], out_shape=(vm((vr...]
    reshape x11 -> x0, local copies, waits for them, and re-layouts: 1.55 us -> none  [the longest x2 0.51 us: prepare(): mid = w_middle.reshape(m, 3, 3, hid, hid)]
    rev x3 -> x0, local copies, waits for them, and re-layouts: 1.49 us -> none  [the longest x1 1.47 us: prepare(): mid[:, ::-1]]
    ppermute x2, waiting for transfers between devices: 6.07 us -> 5.27 us  [swap(): got = lax.ppermute(value, ('lat', 'lon', 'mem'), pairs)]
  transfers between devices with their start and end apart: 14 -> 14, of which waited for: 10 -> 9; matrix products, arithmetic and copies ran while one was open for 5% -> 0% of each run, Pallas kernels for 3% -> 5%
where the time goes in v1:
time: 52.3 us; the launch traced here: 52 us
  starting transfers between devices  19 us (36%)
  waiting for transfers between devices  17 us (33%)
  Pallas kernels  14.2 us (27%)
  local copies, waits for them, and re-layouts  0.98 us (2%)
  between operations  0.74 us (1%)
    ppermute x9, starting transfers between devices, partner(): lax.ppermute(value, axis, [(i, i ^ k) for i in range(lax.axis_size(axis))])  11.6 us
    ppermute x9, waiting for transfers between devices, partner(): lax.ppermute(value, axis, [(i, i ^ k) for i in range(lax.axis_size(axis))])  9.7 us
    pallas_call x1, Pallas kernels, per_device(): pl.pallas_call(functools.partial(closure_kernel, 2.0 / count, total_coars...  8.86 us
    ppermute x2, starting transfers between devices, swap(): got = lax.ppermute(value, ('lat', 'lon', 'mem'), pairs)  6.49 us
    ppermute x2, waiting for transfers between devices, swap(): got = lax.ppermute(value, ('lat', 'lon', 'mem'), pairs)  5.27 us
    ppermute x3, waiting for transfers between devices, swap_cores(): lax.ppermute(value, 'mem', [(i, i ^ 1) for i in range(lax.axis_size('mem'...  2.05 us
    pallas_call x1, Pallas kernels, per_device(): pl.pallas_call(functools.partial(ocean_kernel, rows * nlat, members), out...  1.94 us
    pallas_call x1, Pallas kernels, per_device(): pl.pallas_call(coarse_kernel, in_specs=[hbm, hbm, hbm], out_shape=(vm((vr...  1.67 us
  transfers between devices with their start and end apart: 14, of which 9 were waited for; matrix products, arithmetic and copies ran while one was open for 0% of the time, Pallas kernels for 5%

profile of v1, /device:TPU:0, one launch (start us, length us, event | category | flops | bytes accessed | tf_op | source)
XLA Modules:
  0.0 52.0 jit_solution(22369518865395395)
XLA Ops:
  0.6 1.7 %coarse.1 = (f32[5,64,128]{2,1,0:T(8,128)S(1)}, bf16[128,128]{1,0:T(8,128)(2,1)S(1)}, f32[48,128]{1,0:T(8,128)S(1)}) custom-call(f32[2,4,32,512]{3,2,1,0:T(8,128)} %velo.1, f32[4,32,512]{2,1,0:T(8,128)} %temp.1, bf16[2,4,8,128]{3,2,1,0:T(8,128)(2,1)} %target_hbm.1), custom_call_target="tpu_custom_call" | custom-call | tf_op jit(solution)/shard_map/coarse/pallas_call | solution.py:507
  2.3 3.1 %collective-permute-start = (bf16[128,128]{1,0:T(8,128)(2,1)S(1)}, bf16[128,128]{1,0:T(8,128)(2,1)S(1)}, u32[]{:S(2)}, u32[]{:S(2)}) collective-permute-start(bf16[128,128]{1,0:T(8,128)(2,1)S(1)} %get-tuple-element.26), channel_id=1, source_target_pairs={{0,2},{1,7},{2,0},{3,5},{4,6},{5,3},{6,4},{7,1},{8,10},{9,15},{10,... | collective-permute-start | bytes 98312 | tf_op jit(solution)/shard_map/ppermute | solution.py:473
  5.4 1.9 %collective-permute-done.got.got_lon = bf16[128,128]{1,0:T(8,128)(2,1)S(1)} collective-permute-done((bf16[128,128]{1,0:T(8,128)(2,1)S(1)}, bf16[128,128]{1,0:T(8,128)(2,1)S(1)}, u32[]{:S(2)}, u32[]{:S(2)}) %collective-permute-start) | collective-permute-done | bytes 32800 | tf_op jit(solution)/shard_map/ppermute | solution.py:473
  7.3 1.0 %collective-permute-start.1 = (bf16[128,128]{1,0:T(8,128)(2,1)S(1)}, bf16[128,128]{1,0:T(8,128)(2,1)S(1)}, u32[]{:S(2)}, u32[]{:S(2)}) collective-permute-start(bf16[128,128]{1,0:T(8,128)(2,1)S(1)} %collective-permute-done.got.got_lon), channel_id=1, source_target_pairs={{0,1},{1,0},{2,3},{3,2},{4,5},{5,4},{6,7},{7,6},{8,9},{9,8},{10,11... | collective-permute-start | bytes 98312 | tf_op jit(solution)/shard_map/ppermute | solution.py:478
  8.3 0.9 %collective-permute-done.1.other.other_lon = bf16[128,128]{1,0:T(8,128)(2,1)S(1)} collective-permute-done((bf16[128,128]{1,0:T(8,128)(2,1)S(1)}, bf16[128,128]{1,0:T(8,128)(2,1)S(1)}, u32[]{:S(2)}, u32[]{:S(2)}) %collective-permute-start.1) | collective-permute-done | bytes 32800 | tf_op jit(solution)/shard_map/ppermute | solution.py:478
  9.1 0.0 copy-start.4
  9.1 0.0 copy-start.5
  9.2 3.4 %collective-permute-start.2 = (bf16[304,128]{1,0:T(8,128)(2,1)S(1)}, bf16[304,128]{1,0:T(8,128)(2,1)S(1)}, u32[]{:S(2)}, u32[]{:S(2)}) collective-permute-start(bf16[304,128]{1,0:T(8,128)(2,1)S(1)} %get-tuple-element.29), channel_id=1, source_target_pairs={{0,8},{2,10},{4,12},{6,14},{8,0},{9,17},{10,2},{11,19},{12,4},{13,... | collective-permute-start | bytes 233480 | tf_op jit(solution)/shard_map/ppermute | solution.py:473
  12.6 3.4 %collective-permute-done.2.got.got_lat = bf16[304,128]{1,0:T(8,128)(2,1)S(1)} collective-permute-done((bf16[304,128]{1,0:T(8,128)(2,1)S(1)}, bf16[304,128]{1,0:T(8,128)(2,1)S(1)}, u32[]{:S(2)}, u32[]{:S(2)}) %collective-permute-start.2) | collective-permute-done | bytes 77856 | tf_op jit(solution)/shard_map/ppermute | solution.py:473
  16.0 0.0 collective-permute-start.3
  16.0 0.0 copy-done.4
  16.0 0.0 copy-done.5
  16.0 0.0 copy-start.2
  16.0 1.0 %copy-done.2 = bf16[2,9,64,64]{3,2,1,0:T(8,128)(2,1)S(1)} copy-done((bf16[2,9,64,64]{3,2,1,0:T(8,128)(2,1)S(1)}, bf16[2,9,64,64]{3,2,1,0:T(8,128)(2,1)}, u32[]{:S(2)}) %copy-start.2) | copy-done | bytes 147480
  17.0 0.5 %weights.1 = (bf16[512,96]{1,0:T(8,128)(2,1)S(1)}, bf16[2,384,256]{2,1,0:T(8,128)(2,1)S(1)}, bf16[2,384,256]{2,1,0:T(8,128)(2,1)S(1)}, bf16[144,256]{1,0:T(8,128)(2,1)S(1)}, bf16[128,48]{1,0:T(8,128)(2,1)S(1)}) custom-call(bf16[9,3,2,64]{3,2,1,0:T(2,128)(2,1)S(1)} %bitcast.2, bf16[2,9,64,64]{3,2,1,0:T(8,128)(2,1)S(1)} %copy-done.2, ...), custom_call_target="tpu_custom_call" | custom-call | flops 10000000 | bytes 4000000 | tf_op jit(solution)/shard_map/weights/pallas_call | solution.py:534
  17.5 0.0 collective-permute-done.3.other.other_lat
  17.5 0.0 copy-start
  17.5 8.9 %closure.1 = (bf16[16,640]{1,0:T(8,128)(2,1)S(1)}, s16[176,128]{1,0:T(8,128)(2,1)S(1)}, s16[176,128]{1,0:T(8,128)(2,1)S(1)}, s16[176,128]{1,0:T(8,128)(2,1)S(1)}, f32[160,128]{1,0:T(8,128)S(1)}) custom-call(f32[5,64,128]{2,1,0:T(8,128)S(1)} %get-tuple-element.28.full, bf16[304,128]{1,0:T(8,128)(2,1)S(1)} %collective-permute-done.2.got.got_lat, ...), custom_call_target="tpu_custom_call" | custom-call | tf_op jit(solution)/shard_map/closure/pallas_call | solution.py:549
  26.4 0.0 copy-start.1
  26.4 1.3 %collective-permute-start.5 = (s16[176,128]{1,0:T(8,128)(2,1)S(1)}, s16[176,128]{1,0:T(8,128)(2,1)S(1)}, u32[]{:S(2)}, u32[]{:S(2)}) collective-permute-start(s16[176,128]{1,0:T(8,128)(2,1)S(1)} %get-tuple-element.39), channel_id=1, source_target_pairs={{0,8},{8,0},{16,24},{24,16},{1,9},{9,1},{17,25},{25,17},{2,10},{10... | collective-permute-start | bytes 135176 | tf_op jit(solution)/shard_map/ppermute | solution.py:482
  27.7 1.4 %collective-permute-start.6 = (s16[176,128]{1,0:T(8,128)(2,1)S(1)}, s16[176,128]{1,0:T(8,128)(2,1)S(1)}, u32[]{:S(2)}, u32[]{:S(2)}) collective-permute-start(s16[176,128]{1,0:T(8,128)(2,1)S(1)} %get-tuple-element.40), channel_id=1, source_target_pairs={{0,16},{8,24},{16,0},{24,8},{1,17},{9,25},{17,1},{25,9},{2,18},{10... | collective-permute-start | bytes 135176 | tf_op jit(solution)/shard_map/ppermute | solution.py:482
  29.1 0.8 %collective-permute-start.7 = (s16[176,128]{1,0:T(8,128)(2,1)S(1)}, s16[176,128]{1,0:T(8,128)(2,1)S(1)}, u32[]{:S(2)}, u32[]{:S(2)}) collective-permute-start(s16[176,128]{1,0:T(8,128)(2,1)S(1)} %get-tuple-element.41), channel_id=1, source_target_pairs={{0,24},{8,16},{16,8},{24,0},{1,25},{9,17},{17,9},{25,1},{2,26},{10... | collective-permute-start | bytes 135176 | tf_op jit(solution)/shard_map/ppermute | solution.py:482
  30.0 0.6 %collective-permute-done.5.refs_1_ = s16[176,128]{1,0:T(8,128)(2,1)S(1)} collective-permute-done((s16[176,128]{1,0:T(8,128)(2,1)S(1)}, s16[176,128]{1,0:T(8,128)(2,1)S(1)}, u32[]{:S(2)}, u32[]{:S(2)}) %collective-permute-start.5) | collective-permute-done | bytes 45088 | tf_op jit(solution)/shard_map/ppermute | solution.py:482
  30.5 1.3 %collective-permute-done.6.refs_2_ = s16[176,128]{1,0:T(8,128)(2,1)S(1)} collective-permute-done((s16[176,128]{1,0:T(8,128)(2,1)S(1)}, s16[176,128]{1,0:T(8,128)(2,1)S(1)}, u32[]{:S(2)}, u32[]{:S(2)}) %collective-permute-start.6) | collective-permute-done | bytes 45088 | tf_op jit(solution)/shard_map/ppermute | solution.py:482
  31.8 2.3 %collective-permute-done.7.refs_3_ = s16[176,128]{1,0:T(8,128)(2,1)S(1)} collective-permute-done((s16[176,128]{1,0:T(8,128)(2,1)S(1)}, s16[176,128]{1,0:T(8,128)(2,1)S(1)}, u32[]{:S(2)}, u32[]{:S(2)}) %collective-permute-start.7) | collective-permute-done | bytes 45088 | tf_op jit(solution)/shard_map/ppermute | solution.py:482
  34.1 0.1 sum_lat.1.refs_0_
  34.2 0.0 copy-start.3
  34.2 1.3 %collective-permute-start.8 = (s16[176,128]{1,0:T(8,128)(2,1)S(1)}, s16[176,128]{1,0:T(8,128)(2,1)S(1)}, u32[]{:S(2)}, u32[]{:S(2)}) collective-permute-start(s16[176,128]{1,0:T(8,128)(2,1)S(1)} %sum_lat.1.refs_0_), channel_id=1, source_target_pairs={{0,2},{2,0},{4,6},{6,4},{1,3},{3,1},{5,7},{7,5},{8,10},{10,8},{12,... | collective-permute-start | bytes 135176 | tf_op jit(solution)/shard_map/ppermute | solution.py:482
  35.5 2.9 %collective-permute-start.9 = (s16[176,128]{1,0:T(8,128)(2,1)S(1)}, s16[176,128]{1,0:T(8,128)(2,1)S(1)}, u32[]{:S(2)}, u32[]{:S(2)}) collective-permute-start(s16[176,128]{1,0:T(8,128)(2,1)S(1)} %sum_lat.1.refs_0_), channel_id=1, source_target_pairs={{0,4},{2,6},{4,0},{6,2},{1,5},{3,7},{5,1},{7,3},{8,12},{10,14},{12... | collective-permute-start | bytes 135176 | tf_op jit(solution)/shard_map/ppermute | solution.py:482
  38.4 0.3 collective-permute-start.10
  38.7 0.0 collective-permute-done.8.refs_1_
  38.7 2.3 %collective-permute-done.9.refs_2_ = s16[176,128]{1,0:T(8,128)(2,1)S(1)} collective-permute-done((s16[176,128]{1,0:T(8,128)(2,1)S(1)}, s16[176,128]{1,0:T(8,128)(2,1)S(1)}, u32[]{:S(2)}, u32[]{:S(2)}) %collective-permute-start.9) | collective-permute-done | bytes 45088 | tf_op jit(solution)/shard_map/ppermute | solution.py:482
  40.9 3.3 %collective-permute-done.10.refs_3_ = s16[176,128]{1,0:T(8,128)(2,1)S(1)} collective-permute-done((s16[176,128]{1,0:T(8,128)(2,1)S(1)}, s16[176,128]{1,0:T(8,128)(2,1)S(1)}, u32[]{:S(2)}, u32[]{:S(2)}) %collective-permute-start.10) | collective-permute-done | bytes 45088 | tf_op jit(solution)/shard_map/ppermute | solution.py:482
  44.2 0.1 sum_lon.1.refs_0_
  44.3 1.0 %collective-permute-start.11 = (s16[176,128]{1,0:T(8,128)(2,1)S(1)}, s16[176,128]{1,0:T(8,128)(2,1)S(1)}, u32[]{:S(2)}, u32[]{:S(2)}) collective-permute-start(s16[176,128]{1,0:T(8,128)(2,1)S(1)} %sum_lon.1.refs_0_), channel_id=1, source_target_pairs={{0,8},{8,0},{16,24},{24,16},{1,9},{9,1},{17,25},{25,17},{2,10},{10... | collective-permute-start | bytes 135176 | tf_op jit(solution)/shard_map/ppermute | solution.py:482
  45.3 0.4 collective-permute-start.12
  45.7 2.1 %collective-permute-start.13 = (s16[176,128]{1,0:T(8,128)(2,1)S(1)}, s16[176,128]{1,0:T(8,128)(2,1)S(1)}, u32[]{:S(2)}, u32[]{:S(2)}) collective-permute-start(s16[176,128]{1,0:T(8,128)(2,1)S(1)} %sum_lon.1.refs_0_), channel_id=1, source_target_pairs={{0,24},{8,16},{16,8},{24,0},{1,25},{9,17},{17,9},{25,1},{2,26},{10... | collective-permute-start | bytes 135176 | tf_op jit(solution)/shard_map/ppermute | solution.py:482
  47.9 0.0 collective-permute-start.4
  47.9 1.2 %collective-permute-done.4.other = bf16[16,640]{1,0:T(8,128)(2,1)S(1)} collective-permute-done((bf16[16,640]{1,0:T(8,128)(2,1)S(1)}, bf16[16,640]{1,0:T(8,128)(2,1)S(1)}, u32[]{:S(2)}, u32[]{:S(2)}) %collective-permute-start.4) | collective-permute-done | bytes 20512 | tf_op jit(solution)/shard_map/ppermute | solution.py:478
  49.1 0.0 copy-done
  49.1 0.0 copy-done.1
  49.1 0.0 copy-done.3
  49.1 1.9 %ocean.1 = (f32[2,4,32,512]{3,2,1,0:T(8,128)}, f32[4,32,512]{2,1,0:T(8,128)}) custom-call(f32[2,4,32,512]{3,2,1,0:T(8,128)S(1)} %copy-done, f32[4,32,512]{2,1,0:T(8,128)S(1)} %copy-done.1, s32[32,512]{1,0:T(8,128)S(1)} %copy-done.3, bf16[16,640]{1,0:T(8,128)(2,1)S(1)} %get-tuple-element.35.mine, bf16[16,640]{1,0:T(8,128)(2,1)S(1)} %collective-permute-done.4.other, ...), custom_call_target="tpu_custom_call" | custom-call | flops 100000000 | bytes 4000000 | tf_op jit(solution)/shard_map/ocean/pallas_call | solution.py:573
  51.0 0.0 collective-permute-done.11.refs_1_
  51.0 0.0 collective-permute-done.12.refs_2_
  51.0 0.0 collective-permute-done.13.refs_3_
  51.0 1.0 %finish.1 = (f32[9,3,2,64]{3,2,1,0:T(2,128)}, f32[2,9,64,64]{3,2,1,0:T(8,128)}, f32[2,9,2,64]{3,2,1,0:T(2,128)}) custom-call(s16[176,128]{1,0:T(8,128)(2,1)S(1)} %sum_lon.1.refs_0_, s16[176,128]{1,0:T(8,128)(2,1)S(1)} %collective-permute-done.11.refs_1_, s16[176,128]{1,0:T(8,128)(2,1)S(1)} %collective-permute-done.12.refs_2_, ...), custom_call_target="tpu_custom_call" | custom-call | tf_op jit(solution)/shard_map/finish/pallas_call | solution.py:593
  (1 shorter events, 0.0 us)
Async XLA Ops:
  2.3 5.0 %collective-permute-start = (bf16[128,128]{1,0:T(8,128)(2,1)S(1)}, bf16[128,128]{1,0:T(8,128)(2,1)S(1)}, u32[]{:S(2)}, u32[]{:S(2)}) collective-permute-start(bf16[128,128]{1,0:T(8,128)(2,1)S(1)} %get-tuple-element.26), channel_id=1, source_target_pairs={{0,2},{1,7},{2,0},{3,5},{4,6},{5,3},{6,4},{7,1},{8,10},{9,15},{10,... | collective-permute-start | bytes 98312 | tf_op jit(solution)/shard_map/ppermute | solution.py:473
  7.3 1.9 %collective-permute-start.1 = (bf16[128,128]{1,0:T(8,128)(2,1)S(1)}, bf16[128,128]{1,0:T(8,128)(2,1)S(1)}, u32[]{:S(2)}, u32[]{:S(2)}) collective-permute-start(bf16[128,128]{1,0:T(8,128)(2,1)S(1)} %collective-permute-done.got.got_lon), channel_id=1, source_target_pairs={{0,1},{1,0},{2,3},{3,2},{4,5},{5,4},{6,7},{7,6},{8,9},{9,8},{10,11... | collective-permute-start | bytes 98312 | tf_op jit(solution)/shard_map/ppermute | solution.py:478
  9.1 6.8 %copy-start.4 = (bf16[2,9,64,3]{2,0,3,1:T(2,128)(2,1)S(1)}, bf16[2,9,64,3]{2,0,3,1:T(2,128)(2,1)}, u32[]{:S(2)}) copy-start(bf16[2,9,64,3]{2,0,3,1:T(2,128)(2,1)} %param.11) | copy-start | bytes 20740
  9.1 6.8 %copy-start.5 = (bf16[2,9,2,64]{3,2,1,0:T(2,128)(2,1)S(1)}, bf16[2,9,2,64]{3,2,1,0:T(2,128)(2,1)}, u32[]{:S(2)}) copy-start(bf16[2,9,2,64]{3,2,1,0:T(2,128)(2,1)} %last.1) | copy-start | bytes 13828
  9.2 6.8 %collective-permute-start.2 = (bf16[304,128]{1,0:T(8,128)(2,1)S(1)}, bf16[304,128]{1,0:T(8,128)(2,1)S(1)}, u32[]{:S(2)}, u32[]{:S(2)}) collective-permute-start(bf16[304,128]{1,0:T(8,128)(2,1)S(1)} %get-tuple-element.29), channel_id=1, source_target_pairs={{0,8},{2,10},{4,12},{6,14},{8,0},{9,17},{10,2},{11,19},{12,4},{13,... | collective-permute-start | bytes 233480 | tf_op jit(solution)/shard_map/ppermute | solution.py:473
  16.0 1.5 %collective-permute-start.3 = (bf16[304,128]{1,0:T(8,128)(2,1)S(1)}, bf16[304,128]{1,0:T(8,128)(2,1)S(1)}, u32[]{:S(2)}, u32[]{:S(2)}) collective-permute-start(bf16[304,128]{1,0:T(8,128)(2,1)S(1)} %collective-permute-done.2.got.got_lat), channel_id=1, source_target_pairs={{0,1},{1,0},{2,3},{3,2},{4,5},{5,4},{6,7},{7,6},{8,9},{9,8},{10,11... | collective-permute-start | bytes 233480 | tf_op jit(solution)/shard_map/ppermute | solution.py:478
  16.0 1.0 %copy-start.2 = (bf16[2,9,64,64]{3,2,1,0:T(8,128)(2,1)S(1)}, bf16[2,9,64,64]{3,2,1,0:T(8,128)(2,1)}, u32[]{:S(2)}) copy-start(bf16[2,9,64,64]{3,2,1,0:T(8,128)(2,1)} %middle.1) | copy-start | bytes 442372
  17.5 31.5 %copy-start = (f32[2,4,32,512]{3,2,1,0:T(8,128)S(1)}, f32[2,4,32,512]{3,2,1,0:T(8,128)}, u32[]{:S(2)}) copy-start(f32[2,4,32,512]{3,2,1,0:T(8,128)} %velo.1) | copy-start | bytes 1572868
  26.4 22.7 %copy-start.1 = (f32[4,32,512]{2,1,0:T(8,128)S(1)}, f32[4,32,512]{2,1,0:T(8,128)}, u32[]{:S(2)}) copy-start(f32[4,32,512]{2,1,0:T(8,128)} %temp.1) | copy-start | bytes 786436
  26.4 4.1 %collective-permute-start.5 = (s16[176,128]{1,0:T(8,128)(2,1)S(1)}, s16[176,128]{1,0:T(8,128)(2,1)S(1)}, u32[]{:S(2)}, u32[]{:S(2)}) collective-permute-start(s16[176,128]{1,0:T(8,128)(2,1)S(1)} %get-tuple-element.39), channel_id=1, source_target_pairs={{0,8},{8,0},{16,24},{24,16},{1,9},{9,1},{17,25},{25,17},{2,10},{10... | collective-permute-start | bytes 135176 | tf_op jit(solution)/shard_map/ppermute | solution.py:482
  27.7 4.0 %collective-permute-start.6 = (s16[176,128]{1,0:T(8,128)(2,1)S(1)}, s16[176,128]{1,0:T(8,128)(2,1)S(1)}, u32[]{:S(2)}, u32[]{:S(2)}) collective-permute-start(s16[176,128]{1,0:T(8,128)(2,1)S(1)} %get-tuple-element.40), channel_id=1, source_target_pairs={{0,16},{8,24},{16,0},{24,8},{1,17},{9,25},{17,1},{25,9},{2,18},{10... | collective-permute-start | bytes 135176 | tf_op jit(solution)/shard_map/ppermute | solution.py:482
  29.1 4.9 %collective-permute-start.7 = (s16[176,128]{1,0:T(8,128)(2,1)S(1)}, s16[176,128]{1,0:T(8,128)(2,1)S(1)}, u32[]{:S(2)}, u32[]{:S(2)}) collective-permute-start(s16[176,128]{1,0:T(8,128)(2,1)S(1)} %get-tuple-element.41), channel_id=1, source_target_pairs={{0,24},{8,16},{16,8},{24,0},{1,25},{9,17},{17,9},{25,1},{2,26},{10... | collective-permute-start | bytes 135176 | tf_op jit(solution)/shard_map/ppermute | solution.py:482
  34.2 14.9 %copy-start.3 = (s32[32,512]{1,0:T(8,128)S(1)}, s32[32,512]{1,0:T(8,128)}, u32[]{:S(2)}) copy-start(s32[32,512]{1,0:T(8,128)} %land.1) | copy-start | bytes 196612
  34.2 4.5 %collective-permute-start.8 = (s16[176,128]{1,0:T(8,128)(2,1)S(1)}, s16[176,128]{1,0:T(8,128)(2,1)S(1)}, u32[]{:S(2)}, u32[]{:S(2)}) collective-permute-start(s16[176,128]{1,0:T(8,128)(2,1)S(1)} %sum_lat.1.refs_0_), channel_id=1, source_target_pairs={{0,2},{2,0},{4,6},{6,4},{1,3},{3,1},{5,7},{7,5},{8,10},{10,8},{12,... | collective-permute-start | bytes 135176 | tf_op jit(solution)/shard_map/ppermute | solution.py:482
  35.5 5.4 %collective-permute-start.9 = (s16[176,128]{1,0:T(8,128)(2,1)S(1)}, s16[176,128]{1,0:T(8,128)(2,1)S(1)}, u32[]{:S(2)}, u32[]{:S(2)}) collective-permute-start(s16[176,128]{1,0:T(8,128)(2,1)S(1)} %sum_lat.1.refs_0_), channel_id=1, source_target_pairs={{0,4},{2,6},{4,0},{6,2},{1,5},{3,7},{5,1},{7,3},{8,12},{10,14},{12... | collective-permute-start | bytes 135176 | tf_op jit(solution)/shard_map/ppermute | solution.py:482
  38.4 5.8 %collective-permute-start.10 = (s16[176,128]{1,0:T(8,128)(2,1)S(1)}, s16[176,128]{1,0:T(8,128)(2,1)S(1)}, u32[]{:S(2)}, u32[]{:S(2)}) collective-permute-start(s16[176,128]{1,0:T(8,128)(2,1)S(1)} %sum_lat.1.refs_0_), channel_id=1, source_target_pairs={{0,6},{2,4},{4,2},{6,0},{1,7},{3,5},{5,3},{7,1},{8,14},{10,12},{12... | collective-permute-start | bytes 135176 | tf_op jit(solution)/shard_map/ppermute | solution.py:482
  44.3 6.7 %collective-permute-start.11 = (s16[176,128]{1,0:T(8,128)(2,1)S(1)}, s16[176,128]{1,0:T(8,128)(2,1)S(1)}, u32[]{:S(2)}, u32[]{:S(2)}) collective-permute-start(s16[176,128]{1,0:T(8,128)(2,1)S(1)} %sum_lon.1.refs_0_), channel_id=1, source_target_pairs={{0,8},{8,0},{16,24},{24,16},{1,9},{9,1},{17,25},{25,17},{2,10},{10... | collective-permute-start | bytes 135176 | tf_op jit(solution)/shard_map/ppermute | solution.py:482
  45.3 5.7 %collective-permute-start.12 = (s16[176,128]{1,0:T(8,128)(2,1)S(1)}, s16[176,128]{1,0:T(8,128)(2,1)S(1)}, u32[]{:S(2)}, u32[]{:S(2)}) collective-permute-start(s16[176,128]{1,0:T(8,128)(2,1)S(1)} %sum_lon.1.refs_0_), channel_id=1, source_target_pairs={{0,16},{8,24},{16,0},{24,8},{1,17},{9,25},{17,1},{25,9},{2,18},{10... | collective-permute-start | bytes 135176 | tf_op jit(solution)/shard_map/ppermute | solution.py:482
  45.7 5.3 %collective-permute-start.13 = (s16[176,128]{1,0:T(8,128)(2,1)S(1)}, s16[176,128]{1,0:T(8,128)(2,1)S(1)}, u32[]{:S(2)}, u32[]{:S(2)}) collective-permute-start(s16[176,128]{1,0:T(8,128)(2,1)S(1)} %sum_lon.1.refs_0_), channel_id=1, source_target_pairs={{0,24},{8,16},{16,8},{24,0},{1,25},{9,17},{17,9},{25,1},{2,26},{10... | collective-permute-start | bytes 135176 | tf_op jit(solution)/shard_map/ppermute | solution.py:482
  47.9 1.2 %collective-permute-start.4 = (bf16[16,640]{1,0:T(8,128)(2,1)S(1)}, bf16[16,640]{1,0:T(8,128)(2,1)S(1)}, u32[]{:S(2)}, u32[]{:S(2)}) collective-permute-start(bf16[16,640]{1,0:T(8,128)(2,1)S(1)} %get-tuple-element.35.mine), channel_id=1, source_target_pairs={{0,1},{1,0},{2,3},{3,2},{4,5},{5,4},{6,7},{7,6},{8,9},{9,8},{10,11... | collective-permute-start | bytes 61448 | tf_op jit(solution)/shard_map/ppermute | solution.py:478

commit v2 on v1

--- a/solution.py
+++ b/solution.py
@@ -18,7 +18,7 @@
 F32 = jnp.float32
 BF16 = jnp.bfloat16
 HIGH = lax.Precision.HIGHEST
-VMEM_LIMIT = 48 * 1024 * 1024
+VMEM_LIMIT = 32 * 1024 * 1024
 COARSE_LIMIT = 64 * 1024 * 1024 - 512 * 1024
 
 
@@ -40,6 +40,12 @@
 
 def heads_up(axis):
     return (lax.axis_index(axis) + lax.axis_index("mem")) % 2 == 0
+
+
+def north_and_south(got, other):
+    ahead, place = heads_up("lat"), lax.axis_index("lat")
+    north, south = jnp.where(ahead, got, other), jnp.where(ahead, other, got)
+    return jnp.where(place < lax.axis_size("lat") - 1, north, 0.0), jnp.where(place > 0, south, 0.0)
 
 
 def halves(x):
@@ -148,22 +154,22 @@
             first = jnp.where(lane == n, pltpu.roll(ref[l, :, 0:128], n, 1), first)
             last = jnp.where(lane == n, pltpu.roll(ref[l, :, cols - 128 :], n + 1, 1), last)
     tall = 8 * height
-    east, north = heads_up("lon"), heads_up("lat")
+    east = heads_up("lon")
     cells = jnp.where(east, to_east, to_west)
     to_lon[...] = jnp.concatenate([cells] + halves(jnp.where(east, last, first)), 0).astype(BF16)
-    line = [jnp.where(north, field(f)[:, rows - 1, :], field(f)[:, 0, :]) for f in range(3)]
-    line = [part[:, 128 * j : 128 * (j + 1)] for j in range(cols // 128) for part in line]
-    edges[...] = jnp.concatenate(line, 0)
+    for i, row in enumerate((rows - 1, 0)):
+        line = [field(f)[:, row, 128 * j : 128 * (j + 1)] for j in range(cols // 128) for f in range(3)]
+        edges[i] = jnp.concatenate(line, 0)
 
 
 def merge_kernel(own, got, other, edges, full, message):
     vregs, tall = own.shape[:2]
     levels, deep = vregs - 1, 8 * HALO
-    ahead, north = heads_up("lon"), heads_up("lat")
+    ahead = heads_up("lon")
     near, far = (ref[...].astype(F32)[0:tall] for ref in (got, other))
     right, left = jnp.where(ahead, near, far), jnp.where(ahead, far, near)
     lane = lanes_of((tall, 128))
-    pieces = []
+    upper, lower = [], []
     for j in range(vregs):
         value = own[j]
         if j < levels:
@@ -173,18 +179,41 @@
             at = 32 * (j - 1) + SIDE
             value = jnp.where((lane >= at) & (lane < at + HALO), right, value)
         full[j] = value
-        pieces.append(jnp.where(north, value[tall - deep :], value[:deep]))
-    pieces.append(jnp.zeros((-deep * vregs % 16, 128), F32))
-    message[...] = jnp.concatenate(pieces + halves(edges[...]), 0).astype(BF16)
+        upper.append(value[tall - deep :])
+        lower.append(value[:deep])
+    pad = [jnp.zeros((-deep * vregs % 16, 128), F32)]
+    upper, lower = (jnp.concatenate(x + pad + halves(edges[i]), 0) for i, x in enumerate((upper, lower)))
+    message[...] = jnp.where(heads_up("lat"), upper, lower).astype(BF16)
+
+
+def add(sums, name, term):
+    sums[name] = sums[name] + term if name in sums else term
+
+
+def window(ref, row, rows, step):
+    return ref[step * row : step * (row + rows), :]
+
+
+def quad(get, row, left):
+    return get(row) if left <= 2 else jnp.concatenate([get(row), get(row + 2)], 1)
+
+
+def taps(ref, m, row):
+    return jnp.concatenate([ref[b, m, 64 * row : 64 * (row + 4), :] for b in range(3)], 0)
+
+
+def inner_lanes(wide):
+    within = lanes_of((1, wide)) % (128 + 2 * SIDE)
+    return jnp.where((within >= SIDE) & (within < SIDE + 128), F32(1.0), F32(0.0))
 
 
 def closure_kernel(
     scale, total_rows,
-    full, got, other, wf, wm, wb, wl, wlt,
+    full, got, other, wf, wm, wl, wlt,
     force, *rest,
 ):
     nlat = lax.axis_size("lat")
-    sends, (mine, xf, xb, h1, h2, yl, gb, d2, pf, packed) = rest[: nlat - 1], rest[nlat - 1 :]
+    sends, (mine, xb, inner, d2, xf, h1, h2, yl, gb, pf, packed) = rest[: nlat - 1], rest[nlat - 1 :]
     vregs = full.shape[0]
     height = full.shape[1] // 8
     wide = 128 * vregs
@@ -196,25 +225,13 @@
         return jnp.where((at >= 0) & (at < total_rows), F32(1.0), F32(0.0))
 
     deep = 8 * HALO
-    north = heads_up("lat")
     got, other = got[...].astype(F32), other[...].astype(F32)
     for j in range(vregs):
-        near, far = got[deep * j : deep * (j + 1)], other[deep * j : deep * (j + 1)]
-        above, below = jnp.where(north, near, far), jnp.where(north, far, near)
+        above, below = north_and_south(got[deep * j : deep * (j + 1)], other[deep * j : deep * (j + 1)])
         xf[:, 128 * j : 128 * (j + 1)] = jnp.concatenate([below, full[j], above], 0)
 
     sub = subs_of((8, wide))
-    lane = lanes_of((1, wide))
-    within = lane % (128 + 2 * SIDE)
-    tile = (within >= SIDE) & (within < SIDE + 128)
-    tile_f = jnp.where(tile, F32(1.0), F32(0.0))
-    tile_b = tile_f.astype(BF16)
-
-    def window(ref, row, rows, step):
-        return ref[step * row : step * (row + rows), :]
-
-    def quad(get, row, left):
-        return get(row) if left <= 2 else jnp.concatenate([get(row), get(row + 2)], 1)
+    tile_b = inner_lanes(wide).astype(BF16)
 
     for r in range(span):
         x = window(xf, r, 1, 8)
@@ -222,30 +239,37 @@
         two = pltpu.roll(pltpu.roll(x, wide - 1, 1), 4, 0)
         xb[16 * r : 16 * (r + 1), :] = jnp.concatenate([one, two], 0).astype(BF16)
 
+    def shifts(x, m, at, ref):
+        for b in range(3):
+            moved = x if b == 1 else pltpu.roll(x, (1 - b) % wide, 1)
+            ref[b, m, 64 * at : 64 * (at + 1), :] = moved
+
     step = wf.shape[0] // 128
-    for q in range(0, height + 8, step):
+
+    def make_h1(q):
         pre = dot(wf[...], window(xb, q, step + 2, 16))
         for i in range(step):
             h = (jnp.tanh(pre[128 * i : 128 * (i + 1)]) * inside(q + i - 4)).astype(BF16)
             for m in range(2):
-                h1[m, 64 * (q + i) : 64 * (q + i + 1), :] = h[64 * m : 64 * (m + 1)]
-
-    def columns(y, rr, t, sign):
-        part = [y[192 * rr + 64 * b : 192 * rr + 64 * (b + 1), wide * t : wide * (t + 1)] for b in range(3)]
-        return pltpu.roll(part[0], sign % wide, 1) + part[1] + pltpu.roll(part[2], -sign % wide, 1)
+                part = h[64 * m : 64 * (m + 1)]
+                shifts(part, m, q + i, h1)
+                if 4 <= q + i < height + 4:
+                    inner[m, 64 * (q + i - 4) : 64 * (q + i - 3), :] = part
 
     rows = height + 6
-    for p in range(0, rows, 4):
+
+    def make_h2(p):
         for m in range(2):
-            y = dot(wm[m], quad(lambda r: h1[m, 64 * r : 64 * (r + 4), :], p, rows - p))
+            y = dot(wm[m], quad(lambda r: taps(h1, m, r), p, rows - p))
             for i in range(min(4, rows - p)):
-                h = jnp.tanh(columns(y, i % 2, i // 2, 1)) * inside(p + i - 3)
+                pre = y[64 * (i % 2) : 64 * (i % 2 + 1), wide * (i // 2) : wide * (i // 2 + 1)]
+                h = jnp.tanh(pre) * inside(p + i - 3)
                 at = 128 * (p + i) + 64 * m
                 h2[at : at + 64, :] = h.astype(BF16)
         for i in range(p, min(p + 4, rows), 2):
             yl[72 * i : 72 * (i + 2), :] = dot(wl[...], window(h2, i, 2, 128))
 
-    for s in range(height + 4):
+    def make_g3(s):
         z = sum(yl[72 * (s + a) + 24 * a : 72 * (s + a) + 24 * (a + 1), :] for a in range(3))
         pred = pltpu.roll(z[0:8], 1, 1) + z[8:16] + pltpu.roll(z[16:24], wide - 1, 1)
         goal = window(xf, s + 3, 1, 8)
@@ -256,53 +280,56 @@
         if 2 <= s < height + 2:
             both = pred + pltpu.roll(pred, 6, 0)
             pf[2 * (s - 2) : 2 * (s - 1), :] = both[0:2]
-    force[...] = pf[...].astype(BF16)
-
-    for u in range(height + 2):
+
+    def make_d2(u):
         hidden = window(h2, u + 2, 1, 128).astype(F32)
         d = dot(wlt[...], window(gb, u, 3, 16)) * (1.0 - hidden * hidden) * inside(u - 1)
         for m in range(2):
-            d2[m, 64 * u : 64 * (u + 1), :] = d[64 * m : 64 * (m + 1)].astype(BF16)
-
-    sum_l = sum_f = None
-    sum_m = [None, None]
-
-    def add(total, term):
-        return term if total is None else total + term
-
-    for j in range(0, height, 4):
+            shifts(d[64 * m : 64 * (m + 1)].astype(BF16), m, u, d2)
+
+    sums = {}
+
+    def make_grads(j):
         left = height - j
         g = quad(lambda r: window(gb, r + 1, 4, 16) * tile_b, j, left)
-        sum_l = add(sum_l, dot_nt(g, quad(lambda r: window(h2, r + 3, 2, 128), j, left)))
-        d1 = [[None, None] for _ in range(4)]
+        add(sums, "l", dot_nt(g, quad(lambda r: window(h2, r + 3, 2, 128), j, left)))
         for m in range(2):
-            y = dot(wb[m], quad(lambda r: d2[m, 64 * r : 64 * (r + 4), :], j, left))
-            for i in range(4):
-                hidden = h1[m, 64 * (j + i + 4) : 64 * (j + i + 5), :].astype(F32)
-                d = columns(y, i % 2, i // 2, -1) * (1.0 - hidden * hidden) * tile_f
-                d1[i][m] = d.astype(BF16)
 
             def moved(r):
-                pieces = []
-                for i in range(2):
-                    d = d2[m, 64 * (r + i + 1) : 64 * (r + i + 2), :] * tile_b
-                    pieces += [pltpu.roll(d, wide - 1, 1), d, pltpu.roll(d, 1, 1)]
-                return jnp.concatenate(pieces, 0)
-
-            rhs = quad(lambda r: h1[m, 64 * (r + 3) : 64 * (r + 7), :], j, left)
-            sum_m[m] = add(sum_m[m], dot_nt(quad(moved, j, left), rhs))
-        x = quad(lambda r: window(xb, r + 4, 4, 16), j, left)
-        sum_f = add(sum_f, dot_nt(x, quad(lambda r: jnp.concatenate(d1[r - j] + d1[r - j + 1], 0), j, left)))
-    gl = sum_l[0:48, 0:128] + sum_l[16:64, 128:256]
-    gf = sum_f[0:48, 0:128] + sum_f[16:64, 128:256]
-    gm = [t[0:192, 0:192] + t[192:384, 64:256] for t in sum_m]
+                return jnp.concatenate([d2[b, m, 64 * (r + 1) : 64 * (r + 3), :] for b in (2, 1, 0)], 0)
+
+            rhs = quad(lambda r: h1[1, m, 64 * (r + 3) : 64 * (r + 7), :] * tile_b, j, left)
+            add(sums, m, dot_nt(quad(moved, j, left), rhs))
+
+    done = dict.fromkeys(("h1", "h2", "g3", "d2", "d1"), 0)
+    while done["d1"] < height:
+        if done["d1"] + 6 <= done["d2"]:
+            make_grads(done["d1"])
+            done["d1"] += 4
+        elif done["d2"] < height + 2 and done["d2"] + 3 <= done["g3"]:
+            make_d2(done["d2"])
+            done["d2"] += 1
+        elif done["g3"] < height + 4 and done["g3"] + 3 <= done["h2"]:
+            make_g3(done["g3"])
+            done["g3"] += 1
+        elif done["h2"] < rows and min(done["h2"] + 6, height + 8) <= done["h1"]:
+            make_h2(done["h2"])
+            done["h2"] = min(done["h2"] + 4, rows)
+        else:
+            make_h1(done["h1"])
+            done["h1"] += step
+    force[...] = pf[...].astype(BF16)
+    gl = sums["l"][0:48, 0:128] + sums["l"][16:64, 128:256]
+    gm = []
+    for m in range(2):
+        parts = [sums[m][64 * i : 64 * (i + 1)] for i in range(6)]
+        gm.append(jnp.concatenate([parts[2 * b][:, 0:192] + parts[2 * b + 1][:, 64:256] for b in range(3)], 0))
     for m in range(2):
         packed[192 * m : 192 * (m + 1), :] = gm[m][:, 0:128]
     packed[384:576, :] = jnp.concatenate([gm[0][:, 128:192], gm[1][:, 128:192]], 1)
-    pieces = [gf[16 * a : 16 * a + 12, :] for a in range(3)]
     last = jnp.where(lanes_of(gl.shape) < 64, gl, pltpu.roll(gl, 46, 0))
-    pieces += [last[16 * s + 4 * b : 16 * s + 4 * b + 2] for s in range(3) for b in range(3)]
-    pieces.append(jnp.zeros((packed.shape[0] - 576 - 54, 128), F32))
+    pieces = [last[16 * s + 4 * b : 16 * s + 4 * b + 2] for s in range(3) for b in range(3)]
+    pieces.append(jnp.zeros((packed.shape[0] - 576 - 18, 128), F32))
     packed[576:, :] = jnp.concatenate(pieces, 0)
     part = packed.shape[0] // nlat
     me = lax.axis_index("lat")
@@ -311,24 +338,51 @@
         ref[...] = value if k == 0 else encode(value)
 
 
+def first_grad_kernel(xb, inner, d2, wb, out):
+    wide = xb.shape[1]
+    height = xb.shape[0] // 16 - 2 * HALO
+    mask = inner_lanes(wide)
+    sums = {}
+    for j in range(0, height, 4):
+        left = height - j
+        d1 = [[None, None] for _ in range(4)]
+        for m in range(2):
+            y = dot(wb[m], quad(lambda r: taps(d2, m, r), j, left))
+            for i in range(4):
+                hidden = inner[m, 64 * (j + i) : 64 * (j + i + 1), :].astype(F32)
+                pre = y[64 * (i % 2) : 64 * (i % 2 + 1), wide * (i // 2) : wide * (i // 2 + 1)]
+                d1[i][m] = (pre * (1.0 - hidden * hidden) * mask).astype(BF16)
+        x = quad(lambda r: window(xb, r + 4, 4, 16), j, left)
+        add(sums, "f", dot_nt(x, quad(lambda r: jnp.concatenate(d1[r - j] + d1[r - j + 1], 0), j, left)))
+    out[...] = sums["f"][0:48, 0:128] + sums["f"][16:64, 128:256]
+
+
 def tree_sum(values):
     while len(values) > 1:
         values = [sum(values[i : i + 2][1:], values[i]) for i in range(0, len(values), 2)]
     return values[0]
 
 
-def sum_kernel(*refs):
+def sum_lat_kernel(mine, first, *refs):
     parts, out = refs[:-1], refs[-1]
-    out[...] = encode(tree_sum([ref[...] if ref.dtype == F32 else decode(ref) for ref in parts]))
+    total = tree_sum([mine[...]] + [decode(ref) for ref in parts])
+    out[...] = encode(jnp.concatenate([total, first[...]], 0))
+
+
+def sum_lon_kernel(*refs):
+    parts, out = refs[:-1], refs[-1]
+    out[...] = encode(tree_sum([decode(ref) for ref in parts]))
 
 
 def finish_kernel(*refs):
     nlat = lax.axis_size("lat")
     parts, (first, middle, last, packed) = refs[:nlat], refs[nlat:]
-    part = parts[0].shape[0] - GROUP
+    part = packed.shape[0] // nlat
     me = lax.axis_index("lat")
-    for k, ref in enumerate(parts):
-        packed[pl.ds(pl.multiple_of((me ^ k) * part, 8), part), :] = decode(ref)
+    values = [decode(ref) for ref in parts]
+    for k, value in enumerate(values):
+        packed[pl.ds(pl.multiple_of((me ^ k) * part, 8), part), :] = value[:part]
+    inputs = tree_sum([value[part:] for value in values])
     for m in range(2):
         for b in range(3):
             two = packed[192 * m + 64 * b : 192 * m + 64 * (b + 1), :]
@@ -336,12 +390,13 @@
             middle[m, b] = two[:, 0:64]
             middle[m, 3 + b] = two[:, 64:128]
             middle[m, 6 + b] = third[:, 64 * m : 64 * (m + 1)]
-    rows = packed[576:640, :]
+    rows = packed[576:608, :]
     for m in range(2):
         for k in range(9):
             for c in range(3):
-                first[k, c, m : m + 1] = rows[4 * k + c : 4 * k + c + 1, 64 * m : 64 * (m + 1)]
-            at = 36 + 2 * (3 * (2 - k // 3) + k % 3)
+                at = 16 * (k // 3) + 4 * (k % 3) + c
+                first[k, c, m : m + 1] = inputs[at : at + 1, 64 * m : 64 * (m + 1)]
+            at = 2 * (3 * (2 - k // 3) + k % 3)
             last[m, k] = rows[at : at + 2, 64 * m : 64 * (m + 1)]
 
 
@@ -359,13 +414,12 @@
     ahead = heads_up("lon")
     near, far = (whole(ref, ref.shape[0] - 2 * rows, rows) for ref in (got_lon, other_lon))
     ceast, cwest = jnp.where(ahead, near, far), jnp.where(ahead, far, near)
-    ahead = heads_up("lat")
     lines = 3 * levels * (cols // 128)
     near, far = (whole(ref, ref.shape[0] - 2 * lines, lines) for ref in (got_lat, other_lat))
     near, far = (
         jnp.concatenate([x[3 * levels * j : 3 * levels * (j + 1)] for j in range(cols // 128)], 1) for x in (near, far)
     )
-    rnorth, rsouth = jnp.where(ahead, near, far), jnp.where(ahead, far, near)
+    rnorth, rsouth = north_and_south(near, far)
     height, width = rows // COARSE, cols // COARSE
     row = subs_of((rows, cols))
     lane = lanes_of((rows, cols))
@@ -413,8 +467,14 @@
         temp_next[l] = t + wet * (0.3 * lap_t - 0.5 * (u * dx + v * dy))
 
 
-def weights_kernel(first, middle, last, wf, wm, wb, wl, wlt):
+def weights_kernel(first_hbm, middle_hbm, last_hbm, wf, wm, wb, wl, wlt, first, middle, last, sems):
     hid = middle.shape[-1]
+    pairs = ((first_hbm, first), (middle_hbm, middle), (last_hbm, last))
+    copies = [pltpu.make_async_copy(*pair, sems.at[i]) for i, pair in enumerate(pairs)]
+    for copy in copies:
+        copy.start()
+    for copy in copies:
+        copy.wait()
 
     def slide(pieces, copies):
         zero = jnp.zeros_like(pieces[0])
@@ -425,10 +485,9 @@
             taps = [middle[m, 3 * a + b] for a in range(3)]
             turned = jnp.concatenate([t.astype(F32) for t in taps[::-1]], 0).T.astype(BF16)
             turned = [turned[:, hid * s : hid * (s + 1)] for s in range(3)]
-            for ref, pieces in ((wm, taps), (wb, turned)):
+            for ref, pieces, at in ((wm, taps, b), (wb, turned, 2 - b)):
                 for r, block in enumerate(slide(pieces, 2)):
-                    at = hid * (3 * r + b)
-                    ref[m, at : at + hid, :] = block
+                    ref[m, hid * r : hid * (r + 1), 4 * hid * at : 4 * hid * (at + 1)] = block
     zero = jnp.zeros((1, 2 * hid), F32)
     rows = []
     for a in range(3):
@@ -461,17 +520,12 @@
         place = list(index)
         if lat is not None:
             place[0] += 1 if (index[0] + lat[index[2]]) % 2 == 0 else -1
+            place[0] %= sizes[0]
         if lon is not None:
             place[1] += 1 if (index[1] + lon[index[2]]) % 2 == 0 else -1
             place[1] %= sizes[1]
-        if 0 <= place[0] < sizes[0]:
-            pairs.append(tuple((i[0] * sizes[1] + i[1]) * sizes[2] + i[2] for i in (index, place)))
+        pairs.append(tuple((i[0] * sizes[1] + i[1]) * sizes[2] + i[2] for i in (index, place)))
     return pairs
-
-
-def swap(value, pairs):
-    got = lax.ppermute(value, ("lat", "lon", "mem"), pairs)
-    return got, swap_cores(got)
 
 
 def swap_cores(value):
@@ -510,7 +564,7 @@
         out_shape=(
             vm((vregs, tall, 128), F32),
             vm((tall + 2 * rows, 128), BF16),
-            vm((3 * levels * (cols // 128), 128), F32),
+            vm((2, 3 * levels * (cols // 128), 128), F32),
         ),
         scratch_shapes=[
             vm(velo.shape, F32),
@@ -522,54 +576,88 @@
         compiler_params=pltpu.CompilerParams(vmem_limit_bytes=COARSE_LIMIT),
         name="coarse",
     )(velo, temp, target)
-    got_lon, other_lon = swap(to_lon, pairs_of(lon=core))
+    everywhere = ("lat", "lon", "mem")
+    got_lon = lax.ppermute(to_lon, everywhere, pairs_of(lon=core))
+    kept_in_hbm = (pltpu.with_memory_space_constraint(w, pltpu.HBM) for w in (jnp.transpose(w_first, (1, 3, 0, 2)), w_middle, w_last))
+    weights = pl.pallas_call(
+        weights_kernel,
+        in_specs=[hbm, hbm, hbm],
+        out_shape=(
+            bf16(H1_ROWS * 2 * hid, 16 * (H1_ROWS + 2)),
+            bf16(2, 2 * hid, 12 * hid),
+            bf16(2, 2 * hid, 12 * hid),
+            bf16(144, 4 * hid),
+            bf16(2 * hid, 48),
+        ),
+        scratch_shapes=[
+            vm((w_first.shape[1], w_first.shape[3], w_first.shape[0], hid), BF16),
+            vm(w_middle.shape, BF16),
+            vm(w_last.shape, BF16),
+            pltpu.SemaphoreType.DMA((3,)),
+        ],
+        cost_estimate=pl.CostEstimate(flops=10**8, bytes_accessed=4 * 10**6, transcendentals=0),
+        compiler_params=params,
+        name="weights",
+    )(*kept_in_hbm)
+    other_lon = swap_cores(got_lon)
+    message = bf16(-(-deep * vregs // 16) * 16 + 2 * edges.shape[1], 128)
     full, to_lat = pl.pallas_call(
         merge_kernel,
-        out_shape=(f32(vregs, tall, 128), bf16(-(-deep * vregs // 16) * 16 + 2 * edges.shape[0], 128)),
+        out_shape=(f32(vregs, tall, 128), message),
         compiler_params=params,
         name="merge",
     )(own, got_lon, other_lon, edges)
-    got_lat, other_lat = swap(to_lat, pairs_of(lat=core))
-
-    weights = pl.pallas_call(
-        weights_kernel,
-        out_shape=(
-            bf16(H1_ROWS * 2 * hid, 16 * (H1_ROWS + 2)),
-            bf16(2, 6 * hid, 4 * hid),
-            bf16(2, 6 * hid, 4 * hid),
-            bf16(144, 4 * hid),
-            bf16(2 * hid, 48),
-        ),
-        cost_estimate=pl.CostEstimate(flops=10**7, bytes_accessed=4 * 10**6, transcendentals=0),
-        compiler_params=params,
-        name="weights",
-    )(jnp.transpose(w_first, (1, 3, 0, 2)), w_middle, w_last)
-    total = -(-630 // (GROUP * nlat)) * GROUP * nlat
+    got_lat = lax.ppermute(to_lat, everywhere, pairs_of(lat=core))
+    got_lat, weights = lax.optimization_barrier((got_lat, weights))
+    other_lat = swap_cores(got_lat)
+
+    total = -(-594 // (GROUP * nlat)) * GROUP * nlat
     part = total // nlat
-    force, *sends, mine = pl.pallas_call(
+    coded = jax.ShapeDtypeStruct((part + GROUP, 128), jnp.int16)
+    wf, wm, wb, wl, wlt = weights
+    force, *rest = pl.pallas_call(
         functools.partial(closure_kernel, 2.0 / count, total_coarse),
         out_shape=(
             bf16(2 * height, wide),
-            *[jax.ShapeDtypeStruct((part + GROUP, 128), jnp.int16)] * (nlat - 1),
+            *[coded] * (nlat - 1),
             f32(part, 128),
+            vm((16 * (height + 2 * HALO), wide), BF16),
+            vm((2, 64 * height, wide), BF16),
+            vm((3, 2, 64 * (height + 2), wide), BF16),
         ),
         scratch_shapes=[
             vm((8 * (height + 2 * HALO), wide), F32),
-            vm((16 * (height + 2 * HALO), wide), BF16),
-            vm((2, 64 * (height + 8), wide), BF16),
+            vm((3, 2, 64 * (height + 8), wide), BF16),
             vm((128 * (height + 6), wide), BF16),
             vm((72 * (height + 6), wide), F32),
             vm((16 * (height + 4), wide), BF16),
-            vm((2, 64 * (height + 2), wide), BF16),
             vm((2 * height, wide), F32),
             vm((total, 128), F32),
         ],
         compiler_params=params,
         name="closure",
-    )(full, got_lat, other_lat, *weights)
-
+    )(full, got_lat, other_lat, wf, wm, wl, wlt)
+    sends, (mine, *kept) = rest[: nlat - 1], rest[nlat - 1 :]
+
+    other = swap_cores(force)
     parts = [partner(value, "lat", k + 1) for k, value in enumerate(sends)]
-    other = swap_cores(force)
+    first = pl.pallas_call(
+        first_grad_kernel,
+        out_shape=f32(48, 128),
+        cost_estimate=pl.CostEstimate(flops=2 * 10**9, bytes_accessed=4 * 10**6, transcendentals=0),
+        compiler_params=params,
+        name="first_grad",
+    )(*kept, wb)
+    def add_up(kernel, values, name):
+        return pl.pallas_call(
+            kernel,
+            out_shape=jax.ShapeDtypeStruct((part + 48 + GROUP, 128), jnp.int16),
+            compiler_params=params,
+            name=name,
+        )(*values)
+
+    parts, other = lax.optimization_barrier((parts, other))
+    summed = add_up(sum_lat_kernel, [mine, first, *parts], "sum_lat")
     velo_next, temp_next = pl.pallas_call(
         functools.partial(ocean_kernel, rows * nlat, members),
         out_shape=(jax.ShapeDtypeStruct(velo.shape, F32), jax.ShapeDtypeStruct(temp.shape, F32)),
@@ -577,17 +665,9 @@
         compiler_params=params,
         name="ocean",
     )(velo, temp, land, force, other, got_lon, other_lon, got_lat, other_lat)
-
-    def add_up(values, name):
-        return pl.pallas_call(
-            sum_kernel,
-            out_shape=jax.ShapeDtypeStruct((part + GROUP, 128), jnp.int16),
-            compiler_params=params,
-            name=name,
-        )(*values)
-
-    summed = add_up([mine, *parts], "sum_lat")
-    summed = add_up([summed] + [partner(summed, "lon", k) for k in range(1, nlon)], "sum_lon")
+    parts = [summed] + [partner(summed, "lon", k) for k in range(1, nlon)]
+    parts, velo_next, temp_next = lax.optimization_barrier((parts, velo_next, temp_next))
+    summed = add_up(sum_lon_kernel, parts, "sum_lon")
     parts = [summed] + [partner(summed, "lat", k) for k in range(1, nlat)]
     members_here, taps, _, inputs = w_first.shape
     first, middle, last = pl.pallas_call(

time: 52.3 us -> 47.6 us (0.910)
  waiting for transfers between devices: 17 us -> 13.7 us
  starting transfers between devices: 19 us -> 17.4 us
  Pallas kernels: 14.2 us -> 15.6 us
  local copies, waits for them, and re-layouts: 0.98 us -> 0.02 us
    pallas_call x4 -> x5, Pallas kernels: 0.76 us -> 3.37 us  [the longest x1 1.58 us: per_device(): pl.pallas_call(first_grad_kernel, out_shape=f32(48, 128), cost_estimate=p...]
    ppermute x9, waiting for transfers between devices: 9.7 us -> 7.83 us  [partner(): lax.ppermute(value, axis, [(i, i ^ k) for i in range(lax.axis_size(axis))])]
    ppermute x2, starting transfers between devices: 6.49 us -> 4.64 us  [the longest x1 3.09 us: per_device(): got_lon = lax.ppermute(to_lon, everywhere, pairs_of(lon=core))]
    ppermute x2, waiting for transfers between devices: 5.27 us -> 3.74 us  [the longest x1 1.89 us: per_device(): got_lon = lax.ppermute(to_lon, everywhere, pairs_of(lon=core))]
    pallas_call x1, Pallas kernels: 8.86 us -> 7.63 us  [per_device(): pl.pallas_call(functools.partial(closure_kernel, 2.0 / count, total_coars...]
    unnamed x12 -> x6, local copies, waits for them, and re-layouts: 0.98 us -> 0.02 us
  transfers between devices with their start and end apart: 14 -> 14, of which waited for: 9 -> 10; matrix products, arithmetic and copies ran while one was open for 0% -> 0% of each run, Pallas kernels for 5% -> 11%
where the time goes in v2:
time: 47.6 us; the launch traced here: 47.4 us
  starting transfers between devices  17.4 us (37%)
  Pallas kernels  15.6 us (33%)
  waiting for transfers between devices  13.7 us (29%)
  between operations  0.73 us (2%)
    ppermute x9, starting transfers between devices, partner(): lax.ppermute(value, axis, [(i, i ^ k) for i in range(lax.axis_size(axis))])  11.5 us
    ppermute x9, waiting for transfers between devices, partner(): lax.ppermute(value, axis, [(i, i ^ k) for i in range(lax.axis_size(axis))])  7.83 us
    pallas_call x1, Pallas kernels, per_device(): pl.pallas_call(functools.partial(closure_kernel, 2.0 / count, total_coars...  7.63 us
    ppermute x1, starting transfers between devices, per_device(): got_lon = lax.ppermute(to_lon, everywhere, pairs_of(lon=core))  3.09 us
    ppermute x3, waiting for transfers between devices, swap_cores(): lax.ppermute(value, 'mem', [(i, i ^ 1) for i in range(lax.axis_size('mem'...  2.13 us
    ppermute x1, waiting for transfers between devices, per_device(): got_lon = lax.ppermute(to_lon, everywhere, pairs_of(lon=core))  1.89 us
    pallas_call x1, Pallas kernels, per_device(): pl.pallas_call(functools.partial(ocean_kernel, rows * nlat, members), out...  1.88 us
    ppermute x1, waiting for transfers between devices, per_device(): got_lat = lax.ppermute(to_lat, everywhere, pairs_of(lat=core))  1.85 us
  transfers between devices with their start and end apart: 14, of which 10 were waited for; matrix products, arithmetic and copies ran while one was open for 0% of the time, Pallas kernels for 11%

profile of v2, /device:TPU:0, one launch (start us, length us, event | category | flops | bytes accessed | tf_op | source)
XLA Modules:
  0.0 47.4 jit_solution(9462806538246574629)
XLA Ops:
  0.6 0.0 copy-start.2
  0.6 1.7 %coarse.1 = (f32[5,64,128]{2,1,0:T(8,128)S(1)}, bf16[128,128]{1,0:T(8,128)(2,1)S(1)}, f32[2,48,128]{2,1,0:T(8,128)S(1)}) custom-call(f32[2,4,32,512]{3,2,1,0:T(8,128)} %velo.1, f32[4,32,512]{2,1,0:T(8,128)} %temp.1, bf16[2,4,8,128]{3,2,1,0:T(8,128)(2,1)} %target_hbm.1), custom_call_target="tpu_custom_call" | custom-call | tf_op jit(solution)/shard_map/coarse/pallas_call | solution.py:561
  2.4 0.0 copy-start
  2.4 0.0 copy-start.1
  2.4 3.1 %collective-permute-start = (bf16[128,128]{1,0:T(8,128)(2,1)S(1)}, bf16[128,128]{1,0:T(8,128)(2,1)S(1)}, u32[]{:S(2)}, u32[]{:S(2)}) collective-permute-start(bf16[128,128]{1,0:T(8,128)(2,1)S(1)} %get-tuple-element.45), channel_id=1, source_target_pairs={{0,2},{1,7},{2,0},{3,5},{4,6},{5,3},{6,4},{7,1},{8,10},{9,15},{10,... | collective-permute-start | bytes 98312 | tf_op jit(solution)/shard_map/ppermute | solution.py:580
  5.5 1.9 %collective-permute-done.got.got_lon = bf16[128,128]{1,0:T(8,128)(2,1)S(1)} collective-permute-done((bf16[128,128]{1,0:T(8,128)(2,1)S(1)}, bf16[128,128]{1,0:T(8,128)(2,1)S(1)}, u32[]{:S(2)}, u32[]{:S(2)}) %collective-permute-start) | collective-permute-done | bytes 32800 | tf_op jit(solution)/shard_map/ppermute | solution.py:580
  7.4 1.0 %collective-permute-start.1 = (bf16[128,128]{1,0:T(8,128)(2,1)S(1)}, bf16[128,128]{1,0:T(8,128)(2,1)S(1)}, u32[]{:S(2)}, u32[]{:S(2)}) collective-permute-start(bf16[128,128]{1,0:T(8,128)(2,1)S(1)} %collective-permute-done.got.got_lon), channel_id=1, source_target_pairs={{0,1},{1,0},{2,3},{3,2},{4,5},{5,4},{6,7},{7,6},{8,9},{9,8},{10,11... | collective-permute-start | bytes 98312 | tf_op jit(solution)/shard_map/ppermute | solution.py:532
  8.4 0.9 %collective-permute-done.1.other.other_lon = bf16[128,128]{1,0:T(8,128)(2,1)S(1)} collective-permute-done((bf16[128,128]{1,0:T(8,128)(2,1)S(1)}, bf16[128,128]{1,0:T(8,128)(2,1)S(1)}, u32[]{:S(2)}, u32[]{:S(2)}) %collective-permute-start.1) | collective-permute-done | bytes 32800 | tf_op jit(solution)/shard_map/ppermute | solution.py:532
  9.3 1.6 %collective-permute-start.2 = (bf16[304,128]{1,0:T(8,128)(2,1)S(1)}, bf16[304,128]{1,0:T(8,128)(2,1)S(1)}, u32[]{:S(2)}, u32[]{:S(2)}) collective-permute-start(bf16[304,128]{1,0:T(8,128)(2,1)S(1)} %get-tuple-element.48), channel_id=1, source_target_pairs={{0,8},{1,25},{2,10},{3,27},{4,12},{5,29},{6,14},{7,31},{8,0},{9,17... | collective-permute-start | bytes 233480 | tf_op jit(solution)/shard_map/ppermute | solution.py:610
  10.8 1.6 %weights.1 = (bf16[512,96]{1,0:T(8,128)(2,1)S(1)}, bf16[2,128,768]{2,1,0:T(8,128)(2,1)S(1)}, bf16[2,128,768]{2,1,0:T(8,128)(2,1)S(1)}, bf16[144,256]{1,0:T(8,128)(2,1)S(1)}, bf16[128,48]{1,0:T(8,128)(2,1)S(1)}) custom-call(bf16[9,3,2,64]{3,2,1,0:T(2,128)(2,1)} %bitcast.3, bf16[2,9,64,64]{3,2,1,0:T(8,128)(2,1)} %middle_hbm.1, bf16[2,9,2,64]{3,2,1,0:T(2,128)(2,1)} %last_hbm.1), custom_call_target="tpu_custom_call" | custom-call | flops 100000000 | bytes 4000000 | tf_op jit(solution)/shard_map/weights/pallas_call | solution.py:582
  12.4 1.8 %collective-permute-done.2.got.got_lat = bf16[304,128]{1,0:T(8,128)(2,1)S(1)} collective-permute-done((bf16[304,128]{1,0:T(8,128)(2,1)S(1)}, bf16[304,128]{1,0:T(8,128)(2,1)S(1)}, u32[]{:S(2)}, u32[]{:S(2)}) %collective-permute-start.2) | collective-permute-done | bytes 77856 | tf_op jit(solution)/shard_map/ppermute | solution.py:610
  14.2 0.0 collective-permute-start.3
  14.2 1.3 %collective-permute-done.3.other.other_lat = bf16[304,128]{1,0:T(8,128)(2,1)S(1)} collective-permute-done((bf16[304,128]{1,0:T(8,128)(2,1)S(1)}, bf16[304,128]{1,0:T(8,128)(2,1)S(1)}, u32[]{:S(2)}, u32[]{:S(2)}) %collective-permute-start.3) | collective-permute-done | bytes 77856 | tf_op jit(solution)/shard_map/ppermute | solution.py:532
  15.5 7.6 %closure.1 = (bf16[16,640]{1,0:T(8,128)(2,1)S(1)}, s16[176,128]{1,0:T(8,128)(2,1)S(1)}, s16[176,128]{1,0:T(8,128)(2,1)S(1)}, s16[176,128]{1,0:T(8,128)(2,1)S(1)}...) custom-call(f32[5,64,128]{2,1,0:T(8,128)S(1)} %get-tuple-element.47., ...), custom_call_target="tpu_custom_call" | custom-call | tf_op jit(solution)/shard_map/closure/pallas_call | solution.py:618
  23.1 0.2 collective-permute-start.7
  23.4 1.5 %collective-permute-start.4 = (s16[176,128]{1,0:T(8,128)(2,1)S(1)}, s16[176,128]{1,0:T(8,128)(2,1)S(1)}, u32[]{:S(2)}, u32[]{:S(2)}) collective-permute-start(s16[176,128]{1,0:T(8,128)(2,1)S(1)} %get-tuple-element.64), channel_id=1, source_target_pairs={{0,8},{8,0},{16,24},{24,16},{1,9},{9,1},{17,25},{25,17},{2,10},{10... | collective-permute-start | bytes 135176 | tf_op jit(solution)/shard_map/ppermute | solution.py:536
  24.8 1.5 %collective-permute-start.5 = (s16[176,128]{1,0:T(8,128)(2,1)S(1)}, s16[176,128]{1,0:T(8,128)(2,1)S(1)}, u32[]{:S(2)}, u32[]{:S(2)}) collective-permute-start(s16[176,128]{1,0:T(8,128)(2,1)S(1)} %get-tuple-element.65), channel_id=1, source_target_pairs={{0,16},{8,24},{16,0},{24,8},{1,17},{9,25},{17,1},{25,9},{2,18},{10... | collective-permute-start | bytes 135176 | tf_op jit(solution)/shard_map/ppermute | solution.py:536
  26.3 0.5 %collective-permute-start.6 = (s16[176,128]{1,0:T(8,128)(2,1)S(1)}, s16[176,128]{1,0:T(8,128)(2,1)S(1)}, u32[]{:S(2)}, u32[]{:S(2)}) collective-permute-start(s16[176,128]{1,0:T(8,128)(2,1)S(1)} %get-tuple-element.66), channel_id=1, source_target_pairs={{0,24},{8,16},{16,8},{24,0},{1,25},{9,17},{17,9},{25,1},{2,26},{10... | collective-permute-start | bytes 135176 | tf_op jit(solution)/shard_map/ppermute | solution.py:536
  26.9 1.6 %first_grad.1.first = f32[48,128]{1,0:T(8,128)S(1)} custom-call(bf16[288,640]{1,0:T(8,128)(2,1)S(1)} %get-tuple-element.60.xb, bf16[2,512,640]{2,1,0:T(8,128)(2,1)S(1)} %get-tuple-element.61.inner, bf16[3,2,640,640]{3,2,1,0:T(8,128)(2,1)S(1)} %get-tuple-element.62.d2, bf16[2,128,768]{2,1,0:T(8,128)(2,1)S(1)} %get-tuple-element.63.wb), custom_call_target="tpu_custom_call" | custom-call | flops 2000000000 | bytes 4000000 | tf_op jit(solution)/shard_map/first_grad/pallas_call | solution.py:644
  28.4 0.0 collective-permute-done.7.other
  28.5 0.0 collective-permute-done.4.refs_0_
  28.5 0.4 collective-permute-done.5.refs_1_
  28.9 2.4 %collective-permute-done.6.refs_2_ = s16[176,128]{1,0:T(8,128)(2,1)S(1)} collective-permute-done((s16[176,128]{1,0:T(8,128)(2,1)S(1)}, s16[176,128]{1,0:T(8,128)(2,1)S(1)}, u32[]{:S(2)}, u32[]{:S(2)}) %collective-permute-start.6) | collective-permute-done | bytes 45088 | tf_op jit(solution)/shard_map/ppermute | solution.py:536
  31.3 0.1 sum_lat.1.refs_0_
  31.4 3.6 %collective-permute-start.10 = (s16[224,128]{1,0:T(8,128)(2,1)S(1)}, s16[224,128]{1,0:T(8,128)(2,1)S(1)}, u32[]{:S(2)}, u32[]{:S(2)}) collective-permute-start(s16[224,128]{1,0:T(8,128)(2,1)S(1)} %sum_lat.1.refs_0_), channel_id=1, source_target_pairs={{0,6},{2,4},{4,2},{6,0},{1,7},{3,5},{5,3},{7,1},{8,14},{10,12},{12... | collective-permute-start | bytes 172040 | tf_op jit(solution)/shard_map/ppermute | solution.py:536
  35.0 0.0 collective-permute-start.9
  35.0 0.8 %collective-permute-start.8 = (s16[224,128]{1,0:T(8,128)(2,1)S(1)}, s16[224,128]{1,0:T(8,128)(2,1)S(1)}, u32[]{:S(2)}, u32[]{:S(2)}) collective-permute-start(s16[224,128]{1,0:T(8,128)(2,1)S(1)} %sum_lat.1.refs_0_), channel_id=1, source_target_pairs={{0,2},{2,0},{4,6},{6,4},{1,3},{3,1},{5,7},{7,5},{8,10},{10,8},{12,... | collective-permute-start | bytes 172040 | tf_op jit(solution)/shard_map/ppermute | solution.py:536
  35.8 0.0 copy-done.2
  35.8 0.0 copy-done
  35.8 0.0 copy-done.1
  35.8 1.9 %ocean.1 = (f32[2,4,32,512]{3,2,1,0:T(8,128)}, f32[4,32,512]{2,1,0:T(8,128)}) custom-call(f32[2,4,32,512]{3,2,1,0:T(8,128)S(1)} %copy-done, f32[4,32,512]{2,1,0:T(8,128)S(1)} %copy-done.1, s32[32,512]{1,0:T(8,128)S(1)} %copy-done.2, bf16[16,640]{1,0:T(8,128)(2,1)S(1)} %get-tuple-element.67.mine, bf16[16,640]{1,0:T(8,128)(2,1)S(1)} %collective-permute-done.7.other, ...), custom_call_target="tpu_custom_call" | custom-call | flops 100000000 | bytes 4000000 | tf_op jit(solution)/shard_map/ocean/pallas_call | solution.py:661
  37.7 0.0 collective-permute-done.10.refs_3_
  37.7 2.3 %collective-permute-done.9.refs_2_ = s16[224,128]{1,0:T(8,128)(2,1)S(1)} collective-permute-done((s16[224,128]{1,0:T(8,128)(2,1)S(1)}, s16[224,128]{1,0:T(8,128)(2,1)S(1)}, u32[]{:S(2)}, u32[]{:S(2)}) %collective-permute-start.9) | collective-permute-done | bytes 57376 | tf_op jit(solution)/shard_map/ppermute | solution.py:536
  40.0 0.0 collective-permute-done.8.refs_1_
  40.1 0.1 sum_lon.1.refs_0_
  40.2 0.6 %collective-permute-start.13 = (s16[224,128]{1,0:T(8,128)(2,1)S(1)}, s16[224,128]{1,0:T(8,128)(2,1)S(1)}, u32[]{:S(2)}, u32[]{:S(2)}) collective-permute-start(s16[224,128]{1,0:T(8,128)(2,1)S(1)} %sum_lon.1.refs_0_), channel_id=1, source_target_pairs={{0,24},{8,16},{16,8},{24,0},{1,25},{9,17},{17,9},{25,1},{2,26},{10... | collective-permute-start | bytes 172040 | tf_op jit(solution)/shard_map/ppermute | solution.py:536
  40.8 1.5 %collective-permute-start.12 = (s16[224,128]{1,0:T(8,128)(2,1)S(1)}, s16[224,128]{1,0:T(8,128)(2,1)S(1)}, u32[]{:S(2)}, u32[]{:S(2)}) collective-permute-start(s16[224,128]{1,0:T(8,128)(2,1)S(1)} %sum_lon.1.refs_0_), channel_id=1, source_target_pairs={{0,16},{8,24},{16,0},{24,8},{1,17},{9,25},{17,1},{25,9},{2,18},{10... | collective-permute-start | bytes 172040 | tf_op jit(solution)/shard_map/ppermute | solution.py:536
  42.2 1.5 %collective-permute-start.11 = (s16[224,128]{1,0:T(8,128)(2,1)S(1)}, s16[224,128]{1,0:T(8,128)(2,1)S(1)}, u32[]{:S(2)}, u32[]{:S(2)}) collective-permute-start(s16[224,128]{1,0:T(8,128)(2,1)S(1)} %sum_lon.1.refs_0_), channel_id=1, source_target_pairs={{0,8},{8,0},{16,24},{24,16},{1,9},{9,1},{17,25},{25,17},{2,10},{10... | collective-permute-start | bytes 172040 | tf_op jit(solution)/shard_map/ppermute | solution.py:536
  43.7 1.7 %collective-permute-done.13.refs_3_ = s16[224,128]{1,0:T(8,128)(2,1)S(1)} collective-permute-done((s16[224,128]{1,0:T(8,128)(2,1)S(1)}, s16[224,128]{1,0:T(8,128)(2,1)S(1)}, u32[]{:S(2)}, u32[]{:S(2)}) %collective-permute-start.13) | collective-permute-done | bytes 57376 | tf_op jit(solution)/shard_map/ppermute | solution.py:536
  45.4 0.1 collective-permute-done.12.refs_2_
  45.6 0.8 %collective-permute-done.11.refs_1_ = s16[224,128]{1,0:T(8,128)(2,1)S(1)} collective-permute-done((s16[224,128]{1,0:T(8,128)(2,1)S(1)}, s16[224,128]{1,0:T(8,128)(2,1)S(1)}, u32[]{:S(2)}, u32[]{:S(2)}) %collective-permute-start.11) | collective-permute-done | bytes 57376 | tf_op jit(solution)/shard_map/ppermute | solution.py:536
  46.4 1.0 %finish.1 = (f32[9,3,2,64]{3,2,1,0:T(2,128)}, f32[2,9,64,64]{3,2,1,0:T(8,128)}, f32[2,9,2,64]{3,2,1,0:T(2,128)}) custom-call(s16[224,128]{1,0:T(8,128)(2,1)S(1)} %sum_lon.1.refs_0_, s16[224,128]{1,0:T(8,128)(2,1)S(1)} %collective-permute-done.11.refs_1_, s16[224,128]{1,0:T(8,128)(2,1)S(1)} %collective-permute-done.12.refs_2_, ...), custom_call_target="tpu_custom_call" | custom-call | tf_op jit(solution)/shard_map/finish/pallas_call | solution.py:673
  (1 shorter events, 0.0 us)
Async XLA Ops:
  0.6 35.2 %copy-start.2 = (s32[32,512]{1,0:T(8,128)S(1)}, s32[32,512]{1,0:T(8,128)}, u32[]{:S(2)}) copy-start(s32[32,512]{1,0:T(8,128)} %land.1) | copy-start | bytes 196612
  2.4 33.5 %copy-start = (f32[2,4,32,512]{3,2,1,0:T(8,128)S(1)}, f32[2,4,32,512]{3,2,1,0:T(8,128)}, u32[]{:S(2)}) copy-start(f32[2,4,32,512]{3,2,1,0:T(8,128)} %velo.1) | copy-start | bytes 1572868
  2.4 33.5 %copy-start.1 = (f32[4,32,512]{2,1,0:T(8,128)S(1)}, f32[4,32,512]{2,1,0:T(8,128)}, u32[]{:S(2)}) copy-start(f32[4,32,512]{2,1,0:T(8,128)} %temp.1) | copy-start | bytes 786436
  2.4 5.0 %collective-permute-start = (bf16[128,128]{1,0:T(8,128)(2,1)S(1)}, bf16[128,128]{1,0:T(8,128)(2,1)S(1)}, u32[]{:S(2)}, u32[]{:S(2)}) collective-permute-start(bf16[128,128]{1,0:T(8,128)(2,1)S(1)} %get-tuple-element.45), channel_id=1, source_target_pairs={{0,2},{1,7},{2,0},{3,5},{4,6},{5,3},{6,4},{7,1},{8,10},{9,15},{10,... | collective-permute-start | bytes 98312 | tf_op jit(solution)/shard_map/ppermute | solution.py:580
  7.4 1.9 %collective-permute-start.1 = (bf16[128,128]{1,0:T(8,128)(2,1)S(1)}, bf16[128,128]{1,0:T(8,128)(2,1)S(1)}, u32[]{:S(2)}, u32[]{:S(2)}) collective-permute-start(bf16[128,128]{1,0:T(8,128)(2,1)S(1)} %collective-permute-done.got.got_lon), channel_id=1, source_target_pairs={{0,1},{1,0},{2,3},{3,2},{4,5},{5,4},{6,7},{7,6},{8,9},{9,8},{10,11... | collective-permute-start | bytes 98312 | tf_op jit(solution)/shard_map/ppermute | solution.py:532
  9.3 5.0 %collective-permute-start.2 = (bf16[304,128]{1,0:T(8,128)(2,1)S(1)}, bf16[304,128]{1,0:T(8,128)(2,1)S(1)}, u32[]{:S(2)}, u32[]{:S(2)}) collective-permute-start(bf16[304,128]{1,0:T(8,128)(2,1)S(1)} %get-tuple-element.48), channel_id=1, source_target_pairs={{0,8},{1,25},{2,10},{3,27},{4,12},{5,29},{6,14},{7,31},{8,0},{9,17... | collective-permute-start | bytes 233480 | tf_op jit(solution)/shard_map/ppermute | solution.py:610
  14.2 1.3 %collective-permute-start.3 = (bf16[304,128]{1,0:T(8,128)(2,1)S(1)}, bf16[304,128]{1,0:T(8,128)(2,1)S(1)}, u32[]{:S(2)}, u32[]{:S(2)}) collective-permute-start(bf16[304,128]{1,0:T(8,128)(2,1)S(1)} %collective-permute-done.2.got.got_lat), channel_id=1, source_target_pairs={{0,1},{1,0},{2,3},{3,2},{4,5},{5,4},{6,7},{7,6},{8,9},{9,8},{10,11... | collective-permute-start | bytes 233480 | tf_op jit(solution)/shard_map/ppermute | solution.py:532
  23.1 5.3 %collective-permute-start.7 = (bf16[16,640]{1,0:T(8,128)(2,1)S(1)}, bf16[16,640]{1,0:T(8,128)(2,1)S(1)}, u32[]{:S(2)}, u32[]{:S(2)}) collective-permute-start(bf16[16,640]{1,0:T(8,128)(2,1)S(1)} %get-tuple-element.67.mine), channel_id=1, source_target_pairs={{0,1},{1,0},{2,3},{3,2},{4,5},{5,4},{6,7},{7,6},{8,9},{9,8},{10,11... | collective-permute-start | bytes 61448 | tf_op jit(solution)/shard_map/ppermute | solution.py:532
  23.4 5.1 %collective-permute-start.4 = (s16[176,128]{1,0:T(8,128)(2,1)S(1)}, s16[176,128]{1,0:T(8,128)(2,1)S(1)}, u32[]{:S(2)}, u32[]{:S(2)}) collective-permute-start(s16[176,128]{1,0:T(8,128)(2,1)S(1)} %get-tuple-element.64), channel_id=1, source_target_pairs={{0,8},{8,0},{16,24},{24,16},{1,9},{9,1},{17,25},{25,17},{2,10},{10... | collective-permute-start | bytes 135176 | tf_op jit(solution)/shard_map/ppermute | solution.py:536
  24.8 4.0 %collective-permute-start.5 = (s16[176,128]{1,0:T(8,128)(2,1)S(1)}, s16[176,128]{1,0:T(8,128)(2,1)S(1)}, u32[]{:S(2)}, u32[]{:S(2)}) collective-permute-start(s16[176,128]{1,0:T(8,128)(2,1)S(1)} %get-tuple-element.65), channel_id=1, source_target_pairs={{0,16},{8,24},{16,0},{24,8},{1,17},{9,25},{17,1},{25,9},{2,18},{10... | collective-permute-start | bytes 135176 | tf_op jit(solution)/shard_map/ppermute | solution.py:536
  26.3 4.9 %collective-permute-start.6 = (s16[176,128]{1,0:T(8,128)(2,1)S(1)}, s16[176,128]{1,0:T(8,128)(2,1)S(1)}, u32[]{:S(2)}, u32[]{:S(2)}) collective-permute-start(s16[176,128]{1,0:T(8,128)(2,1)S(1)} %get-tuple-element.66), channel_id=1, source_target_pairs={{0,24},{8,16},{16,8},{24,0},{1,25},{9,17},{17,9},{25,1},{2,26},{10... | collective-permute-start | bytes 135176 | tf_op jit(solution)/shard_map/ppermute | solution.py:536
  31.4 6.3 %collective-permute-start.10 = (s16[224,128]{1,0:T(8,128)(2,1)S(1)}, s16[224,128]{1,0:T(8,128)(2,1)S(1)}, u32[]{:S(2)}, u32[]{:S(2)}) collective-permute-start(s16[224,128]{1,0:T(8,128)(2,1)S(1)} %sum_lat.1.refs_0_), channel_id=1, source_target_pairs={{0,6},{2,4},{4,2},{6,0},{1,7},{3,5},{5,3},{7,1},{8,14},{10,12},{12... | collective-permute-start | bytes 172040 | tf_op jit(solution)/shard_map/ppermute | solution.py:536
  35.0 5.1 %collective-permute-start.9 = (s16[224,128]{1,0:T(8,128)(2,1)S(1)}, s16[224,128]{1,0:T(8,128)(2,1)S(1)}, u32[]{:S(2)}, u32[]{:S(2)}) collective-permute-start(s16[224,128]{1,0:T(8,128)(2,1)S(1)} %sum_lat.1.refs_0_), channel_id=1, source_target_pairs={{0,4},{2,6},{4,0},{6,2},{1,5},{3,7},{5,1},{7,3},{8,12},{10,14},{12... | collective-permute-start | bytes 172040 | tf_op jit(solution)/shard_map/ppermute | solution.py:536
  35.0 5.1 %collective-permute-start.8 = (s16[224,128]{1,0:T(8,128)(2,1)S(1)}, s16[224,128]{1,0:T(8,128)(2,1)S(1)}, u32[]{:S(2)}, u32[]{:S(2)}) collective-permute-start(s16[224,128]{1,0:T(8,128)(2,1)S(1)} %sum_lat.1.refs_0_), channel_id=1, source_target_pairs={{0,2},{2,0},{4,6},{6,4},{1,3},{3,1},{5,7},{7,5},{8,10},{10,8},{12,... | collective-permute-start | bytes 172040 | tf_op jit(solution)/shard_map/ppermute | solution.py:536
  40.2 5.2 %collective-permute-start.13 = (s16[224,128]{1,0:T(8,128)(2,1)S(1)}, s16[224,128]{1,0:T(8,128)(2,1)S(1)}, u32[]{:S(2)}, u32[]{:S(2)}) collective-permute-start(s16[224,128]{1,0:T(8,128)(2,1)S(1)} %sum_lon.1.refs_0_), channel_id=1, source_target_pairs={{0,24},{8,16},{16,8},{24,0},{1,25},{9,17},{17,9},{25,1},{2,26},{10... | collective-permute-start | bytes 172040 | tf_op jit(solution)/shard_map/ppermute | solution.py:536
  40.8 4.8 %collective-permute-start.12 = (s16[224,128]{1,0:T(8,128)(2,1)S(1)}, s16[224,128]{1,0:T(8,128)(2,1)S(1)}, u32[]{:S(2)}, u32[]{:S(2)}) collective-permute-start(s16[224,128]{1,0:T(8,128)(2,1)S(1)} %sum_lon.1.refs_0_), channel_id=1, source_target_pairs={{0,16},{8,24},{16,0},{24,8},{1,17},{9,25},{17,1},{25,9},{2,18},{10... | collective-permute-start | bytes 172040 | tf_op jit(solution)/shard_map/ppermute | solution.py:536
  42.2 4.2 %collective-permute-start.11 = (s16[224,128]{1,0:T(8,128)(2,1)S(1)}, s16[224,128]{1,0:T(8,128)(2,1)S(1)}, u32[]{:S(2)}, u32[]{:S(2)}) collective-permute-start(s16[224,128]{1,0:T(8,128)(2,1)S(1)} %sum_lon.1.refs_0_), channel_id=1, source_target_pairs={{0,8},{8,0},{16,24},{24,16},{1,9},{9,1},{17,25},{25,17},{2,10},{10... | collective-permute-start | bytes 172040 | tf_op jit(solution)/shard_map/ppermute | solution.py:536

commit v3 on v2

--- a/solution.py
+++ b/solution.py
@@ -11,6 +11,7 @@
 
 COARSE = 4
 HALO = 5
+PACKED = 3 * HALO + 4
 GROUP = 16
 LEVELS = 32000.0
 H1_ROWS = 4
@@ -19,7 +20,7 @@
 BF16 = jnp.bfloat16
 HIGH = lax.Precision.HIGHEST
 VMEM_LIMIT = 32 * 1024 * 1024
-COARSE_LIMIT = 64 * 1024 * 1024 - 512 * 1024
+COARSE_LIMIT = 60 * 1024 * 1024
 
 
 def dot(a, b, **kw):
@@ -74,13 +75,15 @@
 
 
 def coarse_kernel(
-    velo_hbm, temp_hbm, target_hbm, own, to_lon, edges, velo, temp, target, fine, sems
+    velo_hbm, temp_hbm, target_hbm, *refs
 ):
+    from_hbm, (own, to_lon, edges, *weights), (velo, temp, target, fine, sems) = refs[:3], refs[3:9], refs[9:]
     copies = [
         pltpu.make_async_copy(velo_hbm.at[0], velo.at[0], sems.at[0]),
         pltpu.make_async_copy(velo_hbm.at[1], velo.at[1], sems.at[1]),
         pltpu.make_async_copy(temp_hbm, temp, sems.at[2]),
         pltpu.make_async_copy(target_hbm, target, sems.at[3]),
+        *(pltpu.make_async_copy(*pair, sems.at[4 + i]) for i, pair in enumerate(zip(from_hbm, weights))),
     ]
     for copy in copies:
         copy.start()
@@ -160,11 +163,13 @@
     for i, row in enumerate((rows - 1, 0)):
         line = [field(f)[:, row, 128 * j : 128 * (j + 1)] for j in range(cols // 128) for f in range(3)]
         edges[i] = jnp.concatenate(line, 0)
+    for copy in copies[4:]:
+        copy.wait()
 
 
 def merge_kernel(own, got, other, edges, full, message):
     vregs, tall = own.shape[:2]
-    levels, deep = vregs - 1, 8 * HALO
+    levels = vregs - 1
     ahead = heads_up("lon")
     near, far = (ref[...].astype(F32)[0:tall] for ref in (got, other))
     right, left = jnp.where(ahead, near, far), jnp.where(ahead, far, near)
@@ -179,13 +184,27 @@
             at = 32 * (j - 1) + SIDE
             value = jnp.where((lane >= at) & (lane < at + HALO), right, value)
         full[j] = value
-        upper.append(value[tall - deep :])
-        lower.append(value[:deep])
-    pad = [jnp.zeros((-deep * vregs % 16, 128), F32)]
+        last = tall // 8
+        for pieces, first, goals in ((upper, last - HALO, (last - 2, last - 1)), (lower, 0, (0, 1))):
+            pieces += [value[8 * r + 4 : 8 * r + 7] for r in range(first, first + HALO)]
+            pieces += [value[8 * r : 8 * r + 2] for r in goals]
+    pad = [jnp.zeros((-PACKED * vregs % 16, 128), F32)]
     upper, lower = (jnp.concatenate(x + pad + halves(edges[i]), 0) for i, x in enumerate((upper, lower)))
     message[...] = jnp.where(heads_up("lat"), upper, lower).astype(BF16)
 
 
+def unpack(message, j, goal_rows):
+    at = PACKED * j
+    rows = []
+    for i in range(HALO):
+        goal = jnp.zeros((2, 128), F32)
+        if i in goal_rows:
+            start = at + 3 * HALO + 2 * goal_rows.index(i)
+            goal = message[start : start + 2]
+        rows += [goal, goal, message[at + 3 * i : at + 3 * (i + 1)], jnp.zeros((1, 128), F32)]
+    return jnp.concatenate(rows, 0)
+
+
 def add(sums, name, term):
     sums[name] = sums[name] + term if name in sums else term
 
@@ -200,6 +219,41 @@
 
 def taps(ref, m, row):
     return jnp.concatenate([ref[b, m, 64 * row : 64 * (row + 4), :] for b in range(3)], 0)
+
+
+def columns_around(x):
+    wide = x.shape[1]
+    return [pltpu.roll(x, 1, 1), x, pltpu.roll(x, wide - 1, 1)]
+
+
+def spread_columns(x):
+    wide = x.shape[1]
+    one = jnp.where(subs_of(x.shape) < 4, pltpu.roll(pltpu.roll(x, 1, 1), 4, 0), x)
+    two = pltpu.roll(pltpu.roll(x, wide - 1, 1), 4, 0)
+    return jnp.concatenate([one, two], 0).astype(BF16)
+
+
+def inner_kernel(full, wf, wm, h1, h2, xb):
+    vregs, height = full.shape[0], full.shape[1] // 8
+    wide = 128 * vregs
+    for r in range(height):
+        x = jnp.concatenate([full[j, 8 * r : 8 * (r + 1), :] for j in range(vregs)], 1)
+        xb[16 * r : 16 * (r + 1), :] = spread_columns(x)
+    half = (height - 2) // 2
+    y = dot(wf[0 : 128 * half, 0 : 16 * (half + 2)], jnp.concatenate([window(xb, r, half + 2, 16) for r in (0, half)], 1))
+    for i in range(2 * half):
+        t = i // half
+        h = jnp.tanh(y[128 * (i - t * half) : 128 * (i - t * half + 1), wide * t : wide * (t + 1)]).astype(BF16)
+        for m in range(2):
+            for b, moved in enumerate(columns_around(h[64 * m : 64 * (m + 1)])):
+                h1[b, m, 64 * i : 64 * (i + 1), :] = moved
+    for p in range(0, height - 4, 4):
+        for m in range(2):
+            y = dot(wm[m], quad(lambda r: taps(h1, m, r), p, 4))
+            for i in range(4):
+                pre = y[64 * (i % 2) : 64 * (i % 2 + 1), wide * (i // 2) : wide * (i // 2 + 1)]
+                at = 128 * (p + i) + 64 * m
+                h2[at : at + 64, :] = jnp.tanh(pre).astype(BF16)
 
 
 def inner_lanes(wide):
@@ -209,11 +263,11 @@
 
 def closure_kernel(
     scale, total_rows,
-    full, got, other, wf, wm, wl, wlt,
+    full, got, other, h1_inner, h2_inner, wf, wm, wl, wlt,
     force, *rest,
 ):
     nlat = lax.axis_size("lat")
-    sends, (mine, xb, inner, d2, xf, h1, h2, yl, gb, pf, packed) = rest[: nlat - 1], rest[nlat - 1 :]
+    sends, (mine, xb, inner, h2, gb, d2, xf, h1, yl, pf, packed) = rest[: nlat - 1], rest[nlat - 1 :]
     vregs = full.shape[0]
     height = full.shape[1] // 8
     wide = 128 * vregs
@@ -224,54 +278,64 @@
         at = first_row + row
         return jnp.where((at >= 0) & (at < total_rows), F32(1.0), F32(0.0))
 
-    deep = 8 * HALO
-    got, other = got[...].astype(F32), other[...].astype(F32)
+    north, south = north_and_south(got[...].astype(F32), other[...].astype(F32))
     for j in range(vregs):
-        above, below = north_and_south(got[deep * j : deep * (j + 1)], other[deep * j : deep * (j + 1)])
+        above, below = unpack(north, j, (0, 1)), unpack(south, j, (HALO - 2, HALO - 1))
         xf[:, 128 * j : 128 * (j + 1)] = jnp.concatenate([below, full[j], above], 0)
 
     sub = subs_of((8, wide))
     tile_b = inner_lanes(wide).astype(BF16)
 
     for r in range(span):
-        x = window(xf, r, 1, 8)
-        one = jnp.where(sub < 4, pltpu.roll(pltpu.roll(x, 1, 1), 4, 0), x)
-        two = pltpu.roll(pltpu.roll(x, wide - 1, 1), 4, 0)
-        xb[16 * r : 16 * (r + 1), :] = jnp.concatenate([one, two], 0).astype(BF16)
-
-    def shifts(x, m, at, ref):
-        for b in range(3):
-            moved = x if b == 1 else pltpu.roll(x, (1 - b) % wide, 1)
-            ref[b, m, 64 * at : 64 * (at + 1), :] = moved
-
-    step = wf.shape[0] // 128
-
-    def make_h1(q):
-        pre = dot(wf[...], window(xb, q, step + 2, 16))
-        for i in range(step):
-            h = (jnp.tanh(pre[128 * i : 128 * (i + 1)]) * inside(q + i - 4)).astype(BF16)
-            for m in range(2):
-                part = h[64 * m : 64 * (m + 1)]
-                shifts(part, m, q + i, h1)
-                if 4 <= q + i < height + 4:
-                    inner[m, 64 * (q + i - 4) : 64 * (q + i - 3), :] = part
+        xb[16 * r : 16 * (r + 1), :] = spread_columns(window(xf, r, 1, 8))
+
+    known = range(5, height + 3)
+
+    def h1_row(b, m, i):
+        ref, at = (h1_inner, i - known[0]) if i in known else (h1, i)
+        return ref[b, m, 64 * at : 64 * (at + 1), :]
+
+    def make_h1(starts, count):
+        weights = wf[0 : 128 * count, 0 : 16 * (count + 2)]
+        y = dot(weights, jnp.concatenate([window(xb, r, count + 2, 16) for r in starts], 1))
+        for t, start in enumerate(starts):
+            for i in range(count):
+                pre = y[128 * i : 128 * (i + 1), wide * t : wide * (t + 1)]
+                h = (jnp.tanh(pre) * inside(start + i - 4)).astype(BF16)
+                for m in range(2):
+                    at = 64 * (start + i)
+                    for b, moved in enumerate(columns_around(h[64 * m : 64 * (m + 1)])):
+                        h1[b, m, at : at + 64, :] = moved
+
+    def h1_rows(b, m, row):
+        return jnp.concatenate([h1_row(b, m, row + i) for i in range(4)], 0)
 
     rows = height + 6
-
-    def make_h2(p):
+    h2[128 * 5 : 128 * (height + 1), :] = h2_inner[...]
+
+    def make_h2(starts, count):
         for m in range(2):
-            y = dot(wm[m], quad(lambda r: taps(h1, m, r), p, rows - p))
-            for i in range(min(4, rows - p)):
-                pre = y[64 * (i % 2) : 64 * (i % 2 + 1), wide * (i // 2) : wide * (i // 2 + 1)]
-                h = jnp.tanh(pre) * inside(p + i - 3)
-                at = 128 * (p + i) + 64 * m
-                h2[at : at + 64, :] = h.astype(BF16)
-        for i in range(p, min(p + 4, rows), 2):
-            yl[72 * i : 72 * (i + 2), :] = dot(wl[...], window(h2, i, 2, 128))
+            windows = [jnp.concatenate([h1_rows(b, m, r) for b in range(3)], 0) for r in starts]
+            y = dot(wm[m, 0 : 64 * count, :], jnp.concatenate(windows, 1))
+            for t, start in enumerate(starts):
+                for i in range(count):
+                    pre = y[64 * i : 64 * (i + 1), wide * t : wide * (t + 1)]
+                    h = jnp.tanh(pre) * inside(start + i - 3)
+                    at = 128 * (start + i) + 64 * m
+                    h2[at : at + 64, :] = h.astype(BF16)
+
+    def make_yl(p):
+        y = dot(wl[...], quad(lambda r: window(h2, r, 2, 128), p, rows - p))
+        for t in range(y.shape[1] // wide):
+            at = 32 * (p + 2 * t)
+            yl[at : at + 64, :] = y[:, wide * t : wide * (t + 1)]
 
     def make_g3(s):
-        z = sum(yl[72 * (s + a) + 24 * a : 72 * (s + a) + 24 * (a + 1), :] for a in range(3))
-        pred = pltpu.roll(z[0:8], 1, 1) + z[8:16] + pltpu.roll(z[16:24], wide - 1, 1)
+        z = 0.0
+        for pair in ((s, s + 2) if s % 2 == 0 else (s - 1, s + 1)):
+            at = 32 * pair + 16 * (s + 2 - pair)
+            z = z + yl[at : at + 16, :]
+        pred = pltpu.roll(z[0:8], 1, 1) + pltpu.roll(z[0:8], 4, 0) + pltpu.roll(z[8:16], wide - 1, 1)
         goal = window(xf, s + 3, 1, 8)
         g = ((pred - goal) * scale * inside(s - 2)).astype(BF16).astype(F32)
         one = jnp.where(sub < 4, pltpu.roll(g, wide - 1, 1), pltpu.roll(g, 4, 0))
@@ -282,44 +346,45 @@
             pf[2 * (s - 2) : 2 * (s - 1), :] = both[0:2]
 
     def make_d2(u):
-        hidden = window(h2, u + 2, 1, 128).astype(F32)
-        d = dot(wlt[...], window(gb, u, 3, 16)) * (1.0 - hidden * hidden) * inside(u - 1)
-        for m in range(2):
-            shifts(d[64 * m : 64 * (m + 1)].astype(BF16), m, u, d2)
+        y = dot(wlt[...], jnp.concatenate([window(gb, r, 3, 16) for r in (u, u + 1)], 1))
+        for t in range(2):
+            hidden = window(h2, u + t + 2, 1, 128).astype(F32)
+            d = y[:, wide * t : wide * (t + 1)] * (1.0 - hidden * hidden) * inside(u + t - 1)
+            for m in range(2):
+                for b, moved in enumerate(columns_around(d[64 * m : 64 * (m + 1)].astype(BF16))):
+                    d2[b, m, 64 * (u + t) : 64 * (u + t + 1), :] = moved
 
     sums = {}
 
     def make_grads(j):
         left = height - j
-        g = quad(lambda r: window(gb, r + 1, 4, 16) * tile_b, j, left)
-        add(sums, "l", dot_nt(g, quad(lambda r: window(h2, r + 3, 2, 128), j, left)))
         for m in range(2):
 
             def moved(r):
                 return jnp.concatenate([d2[b, m, 64 * (r + 1) : 64 * (r + 3), :] for b in (2, 1, 0)], 0)
 
-            rhs = quad(lambda r: h1[1, m, 64 * (r + 3) : 64 * (r + 7), :] * tile_b, j, left)
+            rhs = quad(lambda r: h1_rows(1, m, r + 3) * tile_b, j, left)
             add(sums, m, dot_nt(quad(moved, j, left), rhs))
 
-    done = dict.fromkeys(("h1", "h2", "g3", "d2", "d1"), 0)
-    while done["d1"] < height:
-        if done["d1"] + 6 <= done["d2"]:
-            make_grads(done["d1"])
-            done["d1"] += 4
-        elif done["d2"] < height + 2 and done["d2"] + 3 <= done["g3"]:
-            make_d2(done["d2"])
-            done["d2"] += 1
-        elif done["g3"] < height + 4 and done["g3"] + 3 <= done["h2"]:
-            make_g3(done["g3"])
-            done["g3"] += 1
-        elif done["h2"] < rows and min(done["h2"] + 6, height + 8) <= done["h1"]:
-            make_h2(done["h2"])
-            done["h2"] = min(done["h2"] + 4, rows)
-        else:
-            make_h1(done["h1"])
-            done["h1"] += step
+    make_h1((0, height + 4), 4)
+    make_h1((4, height + 3), 1)
+    make_h2((0, 2), 2)
+    make_h2((4, height + 1), 1)
+    for p in range(0, height, 4):
+        make_yl(p)
+    make_h2((height + 2, height + 4), 2)
+    for p in range(height, rows, 4):
+        make_yl(p)
+    for m in range(2):
+        for r in range(height):
+            inner[m, 64 * r : 64 * (r + 1), :] = h1_row(1, m, r + 4)
+    for r in range(height + 4):
+        make_g3(r)
+    for u in range(0, height + 2, 2):
+        make_d2(u)
+    for j in range(0, height, 4):
+        make_grads(j)
     force[...] = pf[...].astype(BF16)
-    gl = sums["l"][0:48, 0:128] + sums["l"][16:64, 128:256]
     gm = []
     for m in range(2):
         parts = [sums[m][64 * i : 64 * (i + 1)] for i in range(6)]
@@ -327,10 +392,8 @@
     for m in range(2):
         packed[192 * m : 192 * (m + 1), :] = gm[m][:, 0:128]
     packed[384:576, :] = jnp.concatenate([gm[0][:, 128:192], gm[1][:, 128:192]], 1)
-    last = jnp.where(lanes_of(gl.shape) < 64, gl, pltpu.roll(gl, 46, 0))
-    pieces = [last[16 * s + 4 * b : 16 * s + 4 * b + 2] for s in range(3) for b in range(3)]
-    pieces.append(jnp.zeros((packed.shape[0] - 576 - 18, 128), F32))
-    packed[576:, :] = jnp.concatenate(pieces, 0)
+    if packed.shape[0] > 576:
+        packed[576:, :] = jnp.zeros((packed.shape[0] - 576, 128), F32)
     part = packed.shape[0] // nlat
     me = lax.axis_index("lat")
     for k, ref in enumerate((mine, *sends)):
@@ -338,13 +401,15 @@
         ref[...] = value if k == 0 else encode(value)
 
 
-def first_grad_kernel(xb, inner, d2, wb, out):
+def outer_grads_kernel(xb, inner, h2, gb, d2, wb, out):
     wide = xb.shape[1]
     height = xb.shape[0] // 16 - 2 * HALO
     mask = inner_lanes(wide)
     sums = {}
     for j in range(0, height, 4):
         left = height - j
+        g = quad(lambda r: window(gb, r + 1, 4, 16) * mask.astype(BF16), j, left)
+        add(sums, "l", dot_nt(g, quad(lambda r: window(h2, r + 3, 2, 128), j, left)))
         d1 = [[None, None] for _ in range(4)]
         for m in range(2):
             y = dot(wb[m], quad(lambda r: taps(d2, m, r), j, left))
@@ -354,7 +419,12 @@
                 d1[i][m] = (pre * (1.0 - hidden * hidden) * mask).astype(BF16)
         x = quad(lambda r: window(xb, r + 4, 4, 16), j, left)
         add(sums, "f", dot_nt(x, quad(lambda r: jnp.concatenate(d1[r - j] + d1[r - j + 1], 0), j, left)))
-    out[...] = sums["f"][0:48, 0:128] + sums["f"][16:64, 128:256]
+    first, last = (sums[name][0:48, 0:128] + sums[name][16:64, 128:256] for name in "fl")
+    last = jnp.where(lanes_of(last.shape) < 64, last, pltpu.roll(last, 46, 0))
+    places = [(a, b) for a in range(3) for b in range(3)]
+    pieces = [first[16 * a + 4 * b : 16 * a + 4 * b + 3] for a, b in places]
+    pieces += [last[16 * a + 4 * b : 16 * a + 4 * b + 2] for a, b in places]
+    out[...] = jnp.concatenate(pieces + [jnp.zeros((3, 128), F32)], 0)
 
 
 def tree_sum(values):
@@ -363,10 +433,10 @@
     return values[0]
 
 
-def sum_lat_kernel(mine, first, *refs):
+def sum_lat_kernel(mine, outer, *refs):
     parts, out = refs[:-1], refs[-1]
     total = tree_sum([mine[...]] + [decode(ref) for ref in parts])
-    out[...] = encode(jnp.concatenate([total, first[...]], 0))
+    out[...] = encode(jnp.concatenate([total, outer[...]], 0))
 
 
 def sum_lon_kernel(*refs):
@@ -382,7 +452,7 @@
     values = [decode(ref) for ref in parts]
     for k, value in enumerate(values):
         packed[pl.ds(pl.multiple_of((me ^ k) * part, 8), part), :] = value[:part]
-    inputs = tree_sum([value[part:] for value in values])
+    outer = tree_sum([value[part:] for value in values])
     for m in range(2):
         for b in range(3):
             two = packed[192 * m + 64 * b : 192 * m + 64 * (b + 1), :]
@@ -390,14 +460,13 @@
             middle[m, b] = two[:, 0:64]
             middle[m, 3 + b] = two[:, 64:128]
             middle[m, 6 + b] = third[:, 64 * m : 64 * (m + 1)]
-    rows = packed[576:608, :]
     for m in range(2):
         for k in range(9):
             for c in range(3):
-                at = 16 * (k // 3) + 4 * (k % 3) + c
-                first[k, c, m : m + 1] = inputs[at : at + 1, 64 * m : 64 * (m + 1)]
-            at = 2 * (3 * (2 - k // 3) + k % 3)
-            last[m, k] = rows[at : at + 2, 64 * m : 64 * (m + 1)]
+                at = 3 * k + c
+                first[k, c, m : m + 1] = outer[at : at + 1, 64 * m : 64 * (m + 1)]
+            at = 27 + 2 * (3 * (2 - k // 3) + k % 3)
+            last[m, k] = outer[at : at + 2, 64 * m : 64 * (m + 1)]
 
 
 def ocean_kernel(
@@ -467,14 +536,8 @@
         temp_next[l] = t + wet * (0.3 * lap_t - 0.5 * (u * dx + v * dy))
 
 
-def weights_kernel(first_hbm, middle_hbm, last_hbm, wf, wm, wb, wl, wlt, first, middle, last, sems):
+def weights_kernel(first, middle, last, wf, wm, wb, wl, wlt):
     hid = middle.shape[-1]
-    pairs = ((first_hbm, first), (middle_hbm, middle), (last_hbm, last))
-    copies = [pltpu.make_async_copy(*pair, sems.at[i]) for i, pair in enumerate(pairs)]
-    for copy in copies:
-        copy.start()
-    for copy in copies:
-        copy.wait()
 
     def slide(pieces, copies):
         zero = jnp.zeros_like(pieces[0])
@@ -502,15 +565,18 @@
     for r in range(H1_ROWS):
         wf[2 * hid * r : 2 * hid * (r + 1), :] = pltpu.roll(turned, 16 * r, 1).astype(BF16)[:, : wf.shape[1]]
     zero = jnp.zeros((2, hid), F32)
-    block = []
-    for k in range(9):
-        w = [last[m, k].astype(F32) for m in range(2)]
-        tops = [jnp.concatenate([w[0], zero], 1), jnp.concatenate([zero, w[1]], 1)]
-        block.append(jnp.concatenate(tops + [jnp.zeros((4, 2 * hid), F32)], 0))
-    for r, rows in enumerate(slide([jnp.concatenate(block, 0)], 2)):
-        wl[72 * r : 72 * (r + 1), :] = rows.astype(BF16)
-    rows = [block[3 * (2 - s) + b][0:4] if b < 3 else jnp.zeros((4, 2 * hid), F32) for s in range(3) for b in range(4)]
-    wlt[...] = jnp.concatenate(rows, 0).T.astype(BF16)
+    by_row = []
+    for a in range(3):
+        rows = []
+        for b in range(3):
+            w = [last[m, 3 * a + b].astype(F32) for m in range(2)]
+            rows += [jnp.concatenate([w[0], zero], 1), jnp.concatenate([zero, w[1]], 1)]
+        by_row.append(jnp.concatenate(rows + [jnp.zeros((4, 2 * hid), F32)], 0))
+    none = jnp.zeros((16, 2 * hid), F32)
+    for e in range(-1, 3):
+        taps = [by_row[r - e + 1] if abs(r - e) <= 1 else none for r in range(2)]
+        wl[16 * (e + 1) : 16 * (e + 2), :] = jnp.concatenate(taps, 1).astype(BF16)
+    wlt[...] = jnp.concatenate(by_row[::-1], 0).T.astype(BF16)
 
 
 def pairs_of(lat=None, lon=None):
@@ -556,51 +622,45 @@
 
     hid = w_middle.shape[-1]
     hbm = pl.BlockSpec(memory_space=pltpu.HBM)
-    deep, tall = 8 * HALO, 8 * height
+    tall = 8 * height
     core = (0, 1)
-    own, to_lon, edges = pl.pallas_call(
+    raw = (jnp.transpose(w_first, (1, 3, 0, 2)), w_middle, w_last)
+    own, to_lon, edges, *raw = pl.pallas_call(
         coarse_kernel,
-        in_specs=[hbm, hbm, hbm],
+        in_specs=[hbm] * 6,
         out_shape=(
             vm((vregs, tall, 128), F32),
             vm((tall + 2 * rows, 128), BF16),
             vm((2, 3 * levels * (cols // 128), 128), F32),
+            *(vm(w.shape, BF16) for w in raw),
         ),
         scratch_shapes=[
             vm(velo.shape, F32),
             vm(temp.shape, F32),
             vm(target.shape, BF16),
             vm((cols // 128, levels * rows, 128), F32),
-            pltpu.SemaphoreType.DMA((4,)),
+            pltpu.SemaphoreType.DMA((7,)),
         ],
         compiler_params=pltpu.CompilerParams(vmem_limit_bytes=COARSE_LIMIT),
         name="coarse",
-    )(velo, temp, target)
+    )(velo, temp, target, *raw)
     everywhere = ("lat", "lon", "mem")
     got_lon = lax.ppermute(to_lon, everywhere, pairs_of(lon=core))
-    kept_in_hbm = (pltpu.with_memory_space_constraint(w, pltpu.HBM) for w in (jnp.transpose(w_first, (1, 3, 0, 2)), w_middle, w_last))
     weights = pl.pallas_call(
         weights_kernel,
-        in_specs=[hbm, hbm, hbm],
         out_shape=(
             bf16(H1_ROWS * 2 * hid, 16 * (H1_ROWS + 2)),
             bf16(2, 2 * hid, 12 * hid),
             bf16(2, 2 * hid, 12 * hid),
-            bf16(144, 4 * hid),
+            bf16(64, 4 * hid),
             bf16(2 * hid, 48),
         ),
-        scratch_shapes=[
-            vm((w_first.shape[1], w_first.shape[3], w_first.shape[0], hid), BF16),
-            vm(w_middle.shape, BF16),
-            vm(w_last.shape, BF16),
-            pltpu.SemaphoreType.DMA((3,)),
-        ],
         cost_estimate=pl.CostEstimate(flops=10**8, bytes_accessed=4 * 10**6, transcendentals=0),
         compiler_params=params,
         name="weights",
-    )(*kept_in_hbm)
+    )(*raw)
     other_lon = swap_cores(got_lon)
-    message = bf16(-(-deep * vregs // 16) * 16 + 2 * edges.shape[1], 128)
+    message = bf16(-(-PACKED * vregs // 16) * 16 + 2 * edges.shape[1], 128)
     full, to_lat = pl.pallas_call(
         merge_kernel,
         out_shape=(f32(vregs, tall, 128), message),
@@ -608,10 +668,19 @@
         name="merge",
     )(own, got_lon, other_lon, edges)
     got_lat = lax.ppermute(to_lat, everywhere, pairs_of(lat=core))
-    got_lat, weights = lax.optimization_barrier((got_lat, weights))
+    wf, wm, wb, wl, wlt = weights
+    tops = pl.pallas_call(
+        inner_kernel,
+        out_shape=(vm((3, 2, 64 * (height - 2), wide), BF16), vm((128 * (height - 4), wide), BF16)),
+        scratch_shapes=[vm((16 * height, wide), BF16)],
+        cost_estimate=pl.CostEstimate(flops=10**9, bytes_accessed=4 * 10**6, transcendentals=0),
+        compiler_params=params,
+        name="inner",
+    )(full, wf, wm)
+    got_lat, tops, weights = lax.optimization_barrier((got_lat, tops, (wf, wm, wb, wl, wlt)))
     other_lat = swap_cores(got_lat)
 
-    total = -(-594 // (GROUP * nlat)) * GROUP * nlat
+    total = -(-576 // (GROUP * nlat)) * GROUP * nlat
     part = total // nlat
     coded = jax.ShapeDtypeStruct((part + GROUP, 128), jnp.int16)
     wf, wm, wb, wl, wlt = weights
@@ -623,30 +692,30 @@
             f32(part, 128),
             vm((16 * (height + 2 * HALO), wide), BF16),
             vm((2, 64 * height, wide), BF16),
+            vm((128 * (height + 6), wide), BF16),
+            vm((16 * (height + 4), wide), BF16),
             vm((3, 2, 64 * (height + 2), wide), BF16),
         ),
         scratch_shapes=[
             vm((8 * (height + 2 * HALO), wide), F32),
             vm((3, 2, 64 * (height + 8), wide), BF16),
-            vm((128 * (height + 6), wide), BF16),
-            vm((72 * (height + 6), wide), F32),
-            vm((16 * (height + 4), wide), BF16),
+            vm((32 * (height + 6), wide), F32),
             vm((2 * height, wide), F32),
             vm((total, 128), F32),
         ],
         compiler_params=params,
         name="closure",
-    )(full, got_lat, other_lat, wf, wm, wl, wlt)
+    )(full, got_lat, other_lat, *tops, wf, wm, wl, wlt)
     sends, (mine, *kept) = rest[: nlat - 1], rest[nlat - 1 :]
 
     other = swap_cores(force)
-    parts = [partner(value, "lat", k + 1) for k, value in enumerate(sends)]
-    first = pl.pallas_call(
-        first_grad_kernel,
+    parts = [partner(sends[k - 1], "lat", k) for k in reversed(range(1, nlat))][::-1]
+    outer = pl.pallas_call(
+        outer_grads_kernel,
         out_shape=f32(48, 128),
         cost_estimate=pl.CostEstimate(flops=2 * 10**9, bytes_accessed=4 * 10**6, transcendentals=0),
         compiler_params=params,
-        name="first_grad",
+        name="outer_grads",
     )(*kept, wb)
     def add_up(kernel, values, name):
         return pl.pallas_call(
@@ -657,7 +726,7 @@
         )(*values)
 
     parts, other = lax.optimization_barrier((parts, other))
-    summed = add_up(sum_lat_kernel, [mine, first, *parts], "sum_lat")
+    summed = add_up(sum_lat_kernel, [mine, outer, *parts], "sum_lat")
     velo_next, temp_next = pl.pallas_call(
         functools.partial(ocean_kernel, rows * nlat, members),
         out_shape=(jax.ShapeDtypeStruct(velo.shape, F32), jax.ShapeDtypeStruct(temp.shape, F32)),

time: 47.6 us -> 44.4 us (0.933)
  waiting for transfers between devices: 13.7 us -> 11.9 us
  Pallas kernels: 15.6 us -> 14.2 us
    pallas_call x1, Pallas kernels: 7.63 us -> 5.26 us  [per_device(): pl.pallas_call(functools.partial(closure_kernel, 2.0 / count, total_coars...]
    pallas_call x3 -> x4, Pallas kernels: 4.85 us -> 5.75 us  [the longest x1 2.27 us: per_device(): pl.pallas_call(outer_grads_kernel, out_shape=f32(48, 128), cost_estimate=...]
    ppermute x9, waiting for transfers between devices: 7.83 us -> 6.93 us  [partner(): lax.ppermute(value, axis, [(i, i ^ k) for i in range(lax.axis_size(axis))])]
    ppermute x3, waiting for transfers between devices: 2.13 us -> 1.54 us  [swap_cores(): lax.ppermute(value, 'mem', [(i, i ^ 1) for i in range(lax.axis_size('mem'...]
  transfers between devices with their start and end apart: 14 -> 14, of which waited for: 10 -> 9; matrix products, arithmetic and copies ran while one was open for 0% -> 0% of each run, Pallas kernels for 11% -> 14%
where the time goes in v3:
time: 44.4 us; the launch traced here: 44.2 us
  starting transfers between devices  17.4 us (39%)
  Pallas kernels  14.2 us (32%)
  waiting for transfers between devices  11.9 us (27%)
  between operations  0.72 us (2%)
    ppermute x9, starting transfers between devices, partner(): lax.ppermute(value, axis, [(i, i ^ k) for i in range(lax.axis_size(axis))])  11.5 us
    ppermute x9, waiting for transfers between devices, partner(): lax.ppermute(value, axis, [(i, i ^ k) for i in range(lax.axis_size(axis))])  6.93 us
    pallas_call x1, Pallas kernels, per_device(): pl.pallas_call(functools.partial(closure_kernel, 2.0 / count, total_coars...  5.26 us
    ppermute x1, starting transfers between devices, per_device(): got_lon = lax.ppermute(to_lon, everywhere, pairs_of(lon=core))  3.09 us
    pallas_call x1, Pallas kernels, per_device(): pl.pallas_call(outer_grads_kernel, out_shape=f32(48, 128), cost_estimate=...  2.27 us
    pallas_call x1, Pallas kernels, per_device(): pl.pallas_call(functools.partial(ocean_kernel, rows * nlat, members), out...  1.94 us
    ppermute x1, waiting for transfers between devices, per_device(): got_lon = lax.ppermute(to_lon, everywhere, pairs_of(lon=core))  1.89 us
    pallas_call x1, Pallas kernels, per_device(): pl.pallas_call(coarse_kernel, in_specs=[hbm] * 6, out_shape=(vm((vregs, t...  1.71 us
  transfers between devices with their start and end apart: 14, of which 9 were waited for; matrix products, arithmetic and copies ran while one was open for 0% of the time, Pallas kernels for 14%

profile of v3, /device:TPU:0, one launch (start us, length us, event | category | flops | bytes accessed | tf_op | source)
XLA Modules:
  0.0 44.2 jit_solution(15069624108032705381)
XLA Ops:
  0.6 1.7 %coarse.1 = (f32[5,64,128]{2,1,0:T(8,128)S(1)}, bf16[128,128]{1,0:T(8,128)(2,1)S(1)}, f32[2,48,128]{2,1,0:T(8,128)S(1)}, bf16[9,3,2,64]{3,2,1,0:T(2,128)(2,1)S(1...) custom-call(f32[2,4,32,512]{3,2,1,0:T(8,128)} %velo.1, f32[4,32,512]{2,1,0:T(8,128)} %temp.1, ...), custom_call_target="tpu_custom_call" | custom-call | tf_op jit(solution)/shard_map/coarse/pallas_call | solution.py:628
  2.4 3.1 %collective-permute-start = (bf16[128,128]{1,0:T(8,128)(2,1)S(1)}, bf16[128,128]{1,0:T(8,128)(2,1)S(1)}, u32[]{:S(2)}, u32[]{:S(2)}) collective-permute-start(bf16[128,128]{1,0:T(8,128)(2,1)S(1)} %get-tuple-element.54), channel_id=1, source_target_pairs={{0,2},{1,7},{2,0},{3,5},{4,6},{5,3},{6,4},{7,1},{8,10},{9,15},{10,... | collective-permute-start | bytes 98312 | tf_op jit(solution)/shard_map/ppermute | solution.py:648
  5.4 1.9 %collective-permute-done.got.got_lon = bf16[128,128]{1,0:T(8,128)(2,1)S(1)} collective-permute-done((bf16[128,128]{1,0:T(8,128)(2,1)S(1)}, bf16[128,128]{1,0:T(8,128)(2,1)S(1)}, u32[]{:S(2)}, u32[]{:S(2)}) %collective-permute-start) | collective-permute-done | bytes 32800 | tf_op jit(solution)/shard_map/ppermute | solution.py:648
  7.3 1.0 %collective-permute-start.1 = (bf16[128,128]{1,0:T(8,128)(2,1)S(1)}, bf16[128,128]{1,0:T(8,128)(2,1)S(1)}, u32[]{:S(2)}, u32[]{:S(2)}) collective-permute-start(bf16[128,128]{1,0:T(8,128)(2,1)S(1)} %collective-permute-done.got.got_lon), channel_id=1, source_target_pairs={{0,1},{1,0},{2,3},{3,2},{4,5},{5,4},{6,7},{7,6},{8,9},{9,8},{10,11... | collective-permute-start | bytes 98312 | tf_op jit(solution)/shard_map/ppermute | solution.py:598
  8.3 0.5 %weights.1 = (bf16[512,96]{1,0:T(8,128)(2,1)S(1)}, bf16[2,128,768]{2,1,0:T(8,128)(2,1)S(1)}, bf16[2,128,768]{2,1,0:T(8,128)(2,1)S(1)}, bf16[64,256]{1,0:T(8,128)(2,1)S(1)}, bf16[128,48]{1,0:T(8,128)(2,1)S(1)}) custom-call(bf16[9,3,2,64]{3,2,1,0:T(2,128)(2,1)S(1)} %get-tuple-element.58.first, bf16[2,9,64,64]{3,2,1,0:T(8,128)(2,1)S(1)} %get-tuple-element.59.middle, ...), custom_call_target="tpu_custom_call" | custom-call | flops 100000000 | bytes 4000000 | tf_op jit(solution)/shard_map/weights/pallas_call | solution.py:649
  8.9 0.3 collective-permute-done.1.other.other_lon
  9.2 0.1 merge.1
  9.3 1.6 %collective-permute-start.2 = (bf16[192,128]{1,0:T(8,128)(2,1)S(1)}, bf16[192,128]{1,0:T(8,128)(2,1)S(1)}, u32[]{:S(2)}, u32[]{:S(2)}) collective-permute-start(bf16[192,128]{1,0:T(8,128)(2,1)S(1)} %get-tuple-element.57), channel_id=1, source_target_pairs={{0,8},{1,25},{2,10},{3,27},{4,12},{5,29},{6,14},{7,31},{8,0},{9,17... | collective-permute-start | bytes 147464 | tf_op jit(solution)/shard_map/ppermute | solution.py:670
  10.8 1.2 %inner.1 = (bf16[3,2,384,640]{3,2,1,0:T(8,128)(2,1)S(1)}, bf16[512,640]{1,0:T(8,128)(2,1)S(1)}) custom-call(f32[5,64,128]{2,1,0:T(8,128)S(1)} %get-tuple-element.56.full, bf16[512,96]{1,0:T(8,128)(2,1)S(1)} %get-tuple-element.71.wf, bf16[2,128,768]{2,1,0:T(8,128)(2,1)S(1)} %get-tuple-element.72.wm), custom_call_target="tpu_custom_call" | custom-call | flops 1000000000 | bytes 4000000 | tf_op jit(solution)/shard_map/inner/pallas_call | solution.py:672
  12.0 1.6 %collective-permute-done.2.got.got_lat = bf16[192,128]{1,0:T(8,128)(2,1)S(1)} collective-permute-done((bf16[192,128]{1,0:T(8,128)(2,1)S(1)}, bf16[192,128]{1,0:T(8,128)(2,1)S(1)}, u32[]{:S(2)}, u32[]{:S(2)}) %collective-permute-start.2) | collective-permute-done | bytes 49184 | tf_op jit(solution)/shard_map/ppermute | solution.py:670
  13.6 0.0 collective-permute-start.3
  13.6 1.2 %collective-permute-done.3.other.other_lat = bf16[192,128]{1,0:T(8,128)(2,1)S(1)} collective-permute-done((bf16[192,128]{1,0:T(8,128)(2,1)S(1)}, bf16[192,128]{1,0:T(8,128)(2,1)S(1)}, u32[]{:S(2)}, u32[]{:S(2)}) %collective-permute-start.3) | collective-permute-done | bytes 49184 | tf_op jit(solution)/shard_map/ppermute | solution.py:598
  14.8 5.3 %closure.1 = (bf16[16,640]{1,0:T(8,128)(2,1)S(1)}, s16[160,128]{1,0:T(8,128)(2,1)S(1)}, s16[160,128]{1,0:T(8,128)(2,1)S(1)}, s16[160,128]{1,0:T(8,128)(2,1)S(1)}...) custom-call(f32[5,64,128]{2,1,0:T(8,128)S(1)} %get-tuple-element.56., ...), custom_call_target="tpu_custom_call" | custom-call | tf_op jit(solution)/shard_map/closure/pallas_call | solution.py:687
  20.1 0.2 collective-permute-start.7
  20.3 1.5 %collective-permute-start.4 = (s16[160,128]{1,0:T(8,128)(2,1)S(1)}, s16[160,128]{1,0:T(8,128)(2,1)S(1)}, u32[]{:S(2)}, u32[]{:S(2)}) collective-permute-start(s16[160,128]{1,0:T(8,128)(2,1)S(1)} %get-tuple-element.82), channel_id=1, source_target_pairs={{0,8},{8,0},{16,24},{24,16},{1,9},{9,1},{17,25},{25,17},{2,10},{10... | collective-permute-start | bytes 122888 | tf_op jit(solution)/shard_map/ppermute | solution.py:602
  21.8 1.4 %collective-permute-start.5 = (s16[160,128]{1,0:T(8,128)(2,1)S(1)}, s16[160,128]{1,0:T(8,128)(2,1)S(1)}, u32[]{:S(2)}, u32[]{:S(2)}) collective-permute-start(s16[160,128]{1,0:T(8,128)(2,1)S(1)} %get-tuple-element.83), channel_id=1, source_target_pairs={{0,16},{8,24},{16,0},{24,8},{1,17},{9,25},{17,1},{25,9},{2,18},{10... | collective-permute-start | bytes 122888 | tf_op jit(solution)/shard_map/ppermute | solution.py:602
  23.3 0.5 %collective-permute-start.6 = (s16[160,128]{1,0:T(8,128)(2,1)S(1)}, s16[160,128]{1,0:T(8,128)(2,1)S(1)}, u32[]{:S(2)}, u32[]{:S(2)}) collective-permute-start(s16[160,128]{1,0:T(8,128)(2,1)S(1)} %get-tuple-element.84), channel_id=1, source_target_pairs={{0,24},{8,16},{16,8},{24,0},{1,25},{9,17},{17,9},{25,1},{2,26},{10... | collective-permute-start | bytes 122888 | tf_op jit(solution)/shard_map/ppermute | solution.py:602
  23.8 0.0 copy-start
  23.8 0.0 copy-start.1
  23.8 0.0 copy-start.2
  23.8 2.3 %outer_grads.1.outer = f32[48,128]{1,0:T(8,128)S(1)} custom-call(bf16[288,640]{1,0:T(8,128)(2,1)S(1)} %get-tuple-element.76.xb, bf16[2,512,640]{2,1,0:T(8,128)(2,1)S(1)} %get-tuple-element.77.inner, bf16[1792,640]{1,0:T(8,128)(2,1)S(1)} %get-tuple-element.78.h2, bf16[192,640]{1,0:T(8,128)(2,1)S(1)} %get-tuple-element.79.gb, ...), custom_call_target="tpu_custom_call" | custom-call | flops 2000000000 | bytes 4000000 | tf_op jit(solution)/shard_map/outer_grads/pallas_call | solution.py:713
  26.1 0.0 collective-permute-done.7.other
  26.1 0.0 collective-permute-done.4.refs_0_
  26.1 0.0 collective-permute-done.5.refs_1_
  26.1 2.0 %collective-permute-done.6.refs_2_ = s16[160,128]{1,0:T(8,128)(2,1)S(1)} collective-permute-done((s16[160,128]{1,0:T(8,128)(2,1)S(1)}, s16[160,128]{1,0:T(8,128)(2,1)S(1)}, u32[]{:S(2)}, u32[]{:S(2)}) %collective-permute-start.6) | collective-permute-done | bytes 40992 | tf_op jit(solution)/shard_map/ppermute | solution.py:602
  28.2 0.1 sum_lat.1.refs_0_
  28.3 3.6 %collective-permute-start.10 = (s16[208,128]{1,0:T(8,128)(2,1)S(1)}, s16[208,128]{1,0:T(8,128)(2,1)S(1)}, u32[]{:S(2)}, u32[]{:S(2)}) collective-permute-start(s16[208,128]{1,0:T(8,128)(2,1)S(1)} %sum_lat.1.refs_0_), channel_id=1, source_target_pairs={{0,6},{2,4},{4,2},{6,0},{1,7},{3,5},{5,3},{7,1},{8,14},{10,12},{12... | collective-permute-start | bytes 159752 | tf_op jit(solution)/shard_map/ppermute | solution.py:602
  31.9 0.0 collective-permute-start.9
  31.9 0.8 %collective-permute-start.8 = (s16[208,128]{1,0:T(8,128)(2,1)S(1)}, s16[208,128]{1,0:T(8,128)(2,1)S(1)}, u32[]{:S(2)}, u32[]{:S(2)}) collective-permute-start(s16[208,128]{1,0:T(8,128)(2,1)S(1)} %sum_lat.1.refs_0_), channel_id=1, source_target_pairs={{0,2},{2,0},{4,6},{6,4},{1,3},{3,1},{5,7},{7,5},{8,10},{10,8},{12,... | collective-permute-start | bytes 159752 | tf_op jit(solution)/shard_map/ppermute | solution.py:602
  32.7 0.0 copy-done
  32.7 0.0 copy-done.1
  32.7 0.0 copy-done.2
  32.7 1.9 %ocean.1 = (f32[2,4,32,512]{3,2,1,0:T(8,128)}, f32[4,32,512]{2,1,0:T(8,128)}) custom-call(f32[2,4,32,512]{3,2,1,0:T(8,128)S(1)} %copy-done, f32[4,32,512]{2,1,0:T(8,128)S(1)} %copy-done.1, s32[32,512]{1,0:T(8,128)S(1)} %copy-done.2, bf16[16,640]{1,0:T(8,128)(2,1)S(1)} %get-tuple-element.85.mine, bf16[16,640]{1,0:T(8,128)(2,1)S(1)} %collective-permute-done.7.other, ...), custom_call_target="tpu_custom_call" | custom-call | flops 100000000 | bytes 4000000 | tf_op jit(solution)/shard_map/ocean/pallas_call | solution.py:730
  34.7 0.0 collective-permute-done.10.refs_3_
  34.7 2.2 %collective-permute-done.9.refs_2_ = s16[208,128]{1,0:T(8,128)(2,1)S(1)} collective-permute-done((s16[208,128]{1,0:T(8,128)(2,1)S(1)}, s16[208,128]{1,0:T(8,128)(2,1)S(1)}, u32[]{:S(2)}, u32[]{:S(2)}) %collective-permute-start.9) | collective-permute-done | bytes 53280 | tf_op jit(solution)/shard_map/ppermute | solution.py:602
  36.9 0.0 collective-permute-done.8.refs_1_
  36.9 0.1 sum_lon.1.refs_0_
  37.0 0.6 %collective-permute-start.13 = (s16[208,128]{1,0:T(8,128)(2,1)S(1)}, s16[208,128]{1,0:T(8,128)(2,1)S(1)}, u32[]{:S(2)}, u32[]{:S(2)}) collective-permute-start(s16[208,128]{1,0:T(8,128)(2,1)S(1)} %sum_lon.1.refs_0_), channel_id=1, source_target_pairs={{0,24},{8,16},{16,8},{24,0},{1,25},{9,17},{17,9},{25,1},{2,26},{10... | collective-permute-start | bytes 159752 | tf_op jit(solution)/shard_map/ppermute | solution.py:602
  37.7 1.4 %collective-permute-start.12 = (s16[208,128]{1,0:T(8,128)(2,1)S(1)}, s16[208,128]{1,0:T(8,128)(2,1)S(1)}, u32[]{:S(2)}, u32[]{:S(2)}) collective-permute-start(s16[208,128]{1,0:T(8,128)(2,1)S(1)} %sum_lon.1.refs_0_), channel_id=1, source_target_pairs={{0,16},{8,24},{16,0},{24,8},{1,17},{9,25},{17,1},{25,9},{2,18},{10... | collective-permute-start | bytes 159752 | tf_op jit(solution)/shard_map/ppermute | solution.py:602
  39.1 1.5 %collective-permute-start.11 = (s16[208,128]{1,0:T(8,128)(2,1)S(1)}, s16[208,128]{1,0:T(8,128)(2,1)S(1)}, u32[]{:S(2)}, u32[]{:S(2)}) collective-permute-start(s16[208,128]{1,0:T(8,128)(2,1)S(1)} %sum_lon.1.refs_0_), channel_id=1, source_target_pairs={{0,8},{8,0},{16,24},{24,16},{1,9},{9,1},{17,25},{25,17},{2,10},{10... | collective-permute-start | bytes 159752 | tf_op jit(solution)/shard_map/ppermute | solution.py:602
  40.6 1.7 %collective-permute-done.13.refs_3_ = s16[208,128]{1,0:T(8,128)(2,1)S(1)} collective-permute-done((s16[208,128]{1,0:T(8,128)(2,1)S(1)}, s16[208,128]{1,0:T(8,128)(2,1)S(1)}, u32[]{:S(2)}, u32[]{:S(2)}) %collective-permute-start.13) | collective-permute-done | bytes 53280 | tf_op jit(solution)/shard_map/ppermute | solution.py:602
  42.2 0.1 collective-permute-done.12.refs_2_
  42.4 0.9 %collective-permute-done.11.refs_1_ = s16[208,128]{1,0:T(8,128)(2,1)S(1)} collective-permute-done((s16[208,128]{1,0:T(8,128)(2,1)S(1)}, s16[208,128]{1,0:T(8,128)(2,1)S(1)}, u32[]{:S(2)}, u32[]{:S(2)}) %collective-permute-start.11) | collective-permute-done | bytes 53280 | tf_op jit(solution)/shard_map/ppermute | solution.py:602
  43.2 1.0 %finish.1 = (f32[9,3,2,64]{3,2,1,0:T(2,128)}, f32[2,9,64,64]{3,2,1,0:T(8,128)}, f32[2,9,2,64]{3,2,1,0:T(2,128)}) custom-call(s16[208,128]{1,0:T(8,128)(2,1)S(1)} %sum_lon.1.refs_0_, s16[208,128]{1,0:T(8,128)(2,1)S(1)} %collective-permute-done.11.refs_1_, s16[208,128]{1,0:T(8,128)(2,1)S(1)} %collective-permute-done.12.refs_2_, ...), custom_call_target="tpu_custom_call" | custom-call | tf_op jit(solution)/shard_map/finish/pallas_call | solution.py:742
Async XLA Ops:
  2.4 5.0 %collective-permute-start = (bf16[128,128]{1,0:T(8,128)(2,1)S(1)}, bf16[128,128]{1,0:T(8,128)(2,1)S(1)}, u32[]{:S(2)}, u32[]{:S(2)}) collective-permute-start(bf16[128,128]{1,0:T(8,128)(2,1)S(1)} %get-tuple-element.54), channel_id=1, source_target_pairs={{0,2},{1,7},{2,0},{3,5},{4,6},{5,3},{6,4},{7,1},{8,10},{9,15},{10,... | collective-permute-start | bytes 98312 | tf_op jit(solution)/shard_map/ppermute | solution.py:648
  7.3 1.9 %collective-permute-start.1 = (bf16[128,128]{1,0:T(8,128)(2,1)S(1)}, bf16[128,128]{1,0:T(8,128)(2,1)S(1)}, u32[]{:S(2)}, u32[]{:S(2)}) collective-permute-start(bf16[128,128]{1,0:T(8,128)(2,1)S(1)} %collective-permute-done.got.got_lon), channel_id=1, source_target_pairs={{0,1},{1,0},{2,3},{3,2},{4,5},{5,4},{6,7},{7,6},{8,9},{9,8},{10,11... | collective-permute-start | bytes 98312 | tf_op jit(solution)/shard_map/ppermute | solution.py:598
  9.3 4.3 %collective-permute-start.2 = (bf16[192,128]{1,0:T(8,128)(2,1)S(1)}, bf16[192,128]{1,0:T(8,128)(2,1)S(1)}, u32[]{:S(2)}, u32[]{:S(2)}) collective-permute-start(bf16[192,128]{1,0:T(8,128)(2,1)S(1)} %get-tuple-element.57), channel_id=1, source_target_pairs={{0,8},{1,25},{2,10},{3,27},{4,12},{5,29},{6,14},{7,31},{8,0},{9,17... | collective-permute-start | bytes 147464 | tf_op jit(solution)/shard_map/ppermute | solution.py:670
  13.6 1.2 %collective-permute-start.3 = (bf16[192,128]{1,0:T(8,128)(2,1)S(1)}, bf16[192,128]{1,0:T(8,128)(2,1)S(1)}, u32[]{:S(2)}, u32[]{:S(2)}) collective-permute-start(bf16[192,128]{1,0:T(8,128)(2,1)S(1)} %collective-permute-done.2.got.got_lat), channel_id=1, source_target_pairs={{0,1},{1,0},{2,3},{3,2},{4,5},{5,4},{6,7},{7,6},{8,9},{9,8},{10,11... | collective-permute-start | bytes 147464 | tf_op jit(solution)/shard_map/ppermute | solution.py:598
  20.1 6.0 %collective-permute-start.7 = (bf16[16,640]{1,0:T(8,128)(2,1)S(1)}, bf16[16,640]{1,0:T(8,128)(2,1)S(1)}, u32[]{:S(2)}, u32[]{:S(2)}) collective-permute-start(bf16[16,640]{1,0:T(8,128)(2,1)S(1)} %get-tuple-element.85.mine), channel_id=1, source_target_pairs={{0,1},{1,0},{2,3},{3,2},{4,5},{5,4},{6,7},{7,6},{8,9},{9,8},{10,11... | collective-permute-start | bytes 61448 | tf_op jit(solution)/shard_map/ppermute | solution.py:598
  20.3 5.8 %collective-permute-start.4 = (s16[160,128]{1,0:T(8,128)(2,1)S(1)}, s16[160,128]{1,0:T(8,128)(2,1)S(1)}, u32[]{:S(2)}, u32[]{:S(2)}) collective-permute-start(s16[160,128]{1,0:T(8,128)(2,1)S(1)} %get-tuple-element.82), channel_id=1, source_target_pairs={{0,8},{8,0},{16,24},{24,16},{1,9},{9,1},{17,25},{25,17},{2,10},{10... | collective-permute-start | bytes 122888 | tf_op jit(solution)/shard_map/ppermute | solution.py:602
  21.8 4.3 %collective-permute-start.5 = (s16[160,128]{1,0:T(8,128)(2,1)S(1)}, s16[160,128]{1,0:T(8,128)(2,1)S(1)}, u32[]{:S(2)}, u32[]{:S(2)}) collective-permute-start(s16[160,128]{1,0:T(8,128)(2,1)S(1)} %get-tuple-element.83), channel_id=1, source_target_pairs={{0,16},{8,24},{16,0},{24,8},{1,17},{9,25},{17,1},{25,9},{2,18},{10... | collective-permute-start | bytes 122888 | tf_op jit(solution)/shard_map/ppermute | solution.py:602
  23.3 4.9 %collective-permute-start.6 = (s16[160,128]{1,0:T(8,128)(2,1)S(1)}, s16[160,128]{1,0:T(8,128)(2,1)S(1)}, u32[]{:S(2)}, u32[]{:S(2)}) collective-permute-start(s16[160,128]{1,0:T(8,128)(2,1)S(1)} %get-tuple-element.84), channel_id=1, source_target_pairs={{0,24},{8,16},{16,8},{24,0},{1,25},{9,17},{17,9},{25,1},{2,26},{10... | collective-permute-start | bytes 122888 | tf_op jit(solution)/shard_map/ppermute | solution.py:602
  23.8 8.9 %copy-start = (f32[2,4,32,512]{3,2,1,0:T(8,128)S(1)}, f32[2,4,32,512]{3,2,1,0:T(8,128)}, u32[]{:S(2)}) copy-start(f32[2,4,32,512]{3,2,1,0:T(8,128)} %velo.1) | copy-start | bytes 1572868
  23.8 8.9 %copy-start.1 = (f32[4,32,512]{2,1,0:T(8,128)S(1)}, f32[4,32,512]{2,1,0:T(8,128)}, u32[]{:S(2)}) copy-start(f32[4,32,512]{2,1,0:T(8,128)} %temp.1) | copy-start | bytes 786436
  23.8 8.9 %copy-start.2 = (s32[32,512]{1,0:T(8,128)S(1)}, s32[32,512]{1,0:T(8,128)}, u32[]{:S(2)}) copy-start(s32[32,512]{1,0:T(8,128)} %land.1) | copy-start | bytes 196612
  28.3 6.4 %collective-permute-start.10 = (s16[208,128]{1,0:T(8,128)(2,1)S(1)}, s16[208,128]{1,0:T(8,128)(2,1)S(1)}, u32[]{:S(2)}, u32[]{:S(2)}) collective-permute-start(s16[208,128]{1,0:T(8,128)(2,1)S(1)} %sum_lat.1.refs_0_), channel_id=1, source_target_pairs={{0,6},{2,4},{4,2},{6,0},{1,7},{3,5},{5,3},{7,1},{8,14},{10,12},{12... | collective-permute-start | bytes 159752 | tf_op jit(solution)/shard_map/ppermute | solution.py:602
  31.9 5.0 %collective-permute-start.9 = (s16[208,128]{1,0:T(8,128)(2,1)S(1)}, s16[208,128]{1,0:T(8,128)(2,1)S(1)}, u32[]{:S(2)}, u32[]{:S(2)}) collective-permute-start(s16[208,128]{1,0:T(8,128)(2,1)S(1)} %sum_lat.1.refs_0_), channel_id=1, source_target_pairs={{0,4},{2,6},{4,0},{6,2},{1,5},{3,7},{5,1},{7,3},{8,12},{10,14},{12... | collective-permute-start | bytes 159752 | tf_op jit(solution)/shard_map/ppermute | solution.py:602
  31.9 5.0 %collective-permute-start.8 = (s16[208,128]{1,0:T(8,128)(2,1)S(1)}, s16[208,128]{1,0:T(8,128)(2,1)S(1)}, u32[]{:S(2)}, u32[]{:S(2)}) collective-permute-start(s16[208,128]{1,0:T(8,128)(2,1)S(1)} %sum_lat.1.refs_0_), channel_id=1, source_target_pairs={{0,2},{2,0},{4,6},{6,4},{1,3},{3,1},{5,7},{7,5},{8,10},{10,8},{12,... | collective-permute-start | bytes 159752 | tf_op jit(solution)/shard_map/ppermute | solution.py:602
  37.0 5.2 %collective-permute-start.13 = (s16[208,128]{1,0:T(8,128)(2,1)S(1)}, s16[208,128]{1,0:T(8,128)(2,1)S(1)}, u32[]{:S(2)}, u32[]{:S(2)}) collective-permute-start(s16[208,128]{1,0:T(8,128)(2,1)S(1)} %sum_lon.1.refs_0_), channel_id=1, source_target_pairs={{0,24},{8,16},{16,8},{24,0},{1,25},{9,17},{17,9},{25,1},{2,26},{10... | collective-permute-start | bytes 159752 | tf_op jit(solution)/shard_map/ppermute | solution.py:602
  37.7 4.7 %collective-permute-start.12 = (s16[208,128]{1,0:T(8,128)(2,1)S(1)}, s16[208,128]{1,0:T(8,128)(2,1)S(1)}, u32[]{:S(2)}, u32[]{:S(2)}) collective-permute-start(s16[208,128]{1,0:T(8,128)(2,1)S(1)} %sum_lon.1.refs_0_), channel_id=1, source_target_pairs={{0,16},{8,24},{16,0},{24,8},{1,17},{9,25},{17,1},{25,9},{2,18},{10... | collective-permute-start | bytes 159752 | tf_op jit(solution)/shard_map/ppermute | solution.py:602
  39.1 4.1 %collective-permute-start.11 = (s16[208,128]{1,0:T(8,128)(2,1)S(1)}, s16[208,128]{1,0:T(8,128)(2,1)S(1)}, u32[]{:S(2)}, u32[]{:S(2)}) collective-permute-start(s16[208,128]{1,0:T(8,128)(2,1)S(1)} %sum_lon.1.refs_0_), channel_id=1, source_target_pairs={{0,8},{8,0},{16,24},{24,16},{1,9},{9,1},{17,25},{25,17},{2,10},{10... | collective-permute-start | bytes 159752 | tf_op jit(solution)/shard_map/ppermute | solution.py:602

commit v4 on v3

--- a/solution.py
+++ b/solution.py
@@ -18,7 +18,6 @@
 SIDE = 16
 F32 = jnp.float32
 BF16 = jnp.bfloat16
-HIGH = lax.Precision.HIGHEST
 VMEM_LIMIT = 32 * 1024 * 1024
 COARSE_LIMIT = 60 * 1024 * 1024
 
@@ -74,45 +73,83 @@
     return jnp.concatenate(pieces, 0)
 
 
-def coarse_kernel(
-    velo_hbm, temp_hbm, target_hbm, *refs
-):
-    from_hbm, (own, to_lon, edges, *weights), (velo, temp, target, fine, sems) = refs[:3], refs[3:9], refs[9:]
-    copies = [
-        pltpu.make_async_copy(velo_hbm.at[0], velo.at[0], sems.at[0]),
-        pltpu.make_async_copy(velo_hbm.at[1], velo.at[1], sems.at[1]),
-        pltpu.make_async_copy(temp_hbm, temp, sems.at[2]),
-        pltpu.make_async_copy(target_hbm, target, sems.at[3]),
-        *(pltpu.make_async_copy(*pair, sems.at[4 + i]) for i, pair in enumerate(zip(from_hbm, weights))),
+def row_sums(ref, fine, spans):
+    levels, rows, _ = ref.shape
+    for j, span in enumerate(spans):
+        fine[j] = ref[:, :, span].reshape(levels * rows, 128)
+    step = levels * rows // COARSE
+    return [
+        sum(fine[j, pl.ds(s, step, stride=COARSE), :] for s in range(COARSE)) for j in range(len(spans))
     ]
+
+
+def pool_columns(x):
+    cols = x.shape[1]
+    here = subs_of((cols, 128)) // COARSE == lanes_of((cols, 128))
+    pool = jnp.where(here, F32(1.0 / COARSE**2), F32(0.0)).astype(BF16)
+    high, rest = halves(x)
+    terms = jnp.concatenate([high] + halves(rest), 0).astype(BF16)
+    y = dot(terms, pool)
+    size = x.shape[0]
+    return ((y[2 * size :] + y[size : 2 * size]) + y[:size]).astype(BF16).astype(F32)
+
+
+def edge_kernel(velo_hbm, temp_hbm, target_hbm, *refs):
+    from_hbm, (to_lon, velo, temp, target, *weights), (fine, cells, sems) = refs[:3], refs[3:10], refs[10:]
+    levels, rows, cols = temp.shape
+    height = rows // COARSE
+    pairs = [(velo_hbm.at[0], velo.at[0]), (velo_hbm.at[1], velo.at[1]), (temp_hbm, temp), (target_hbm, target)]
+    pairs += zip(from_hbm, weights)
+    copies = [pltpu.make_async_copy(*pair, sems.at[i]) for i, pair in enumerate(pairs)]
     for copy in copies:
         copy.start()
+    spans = (slice(0, 128), slice(cols - 128, cols))
+    sums = []
+    for f in range(3):
+        copies[f].wait()
+        sums += row_sums(temp if f == 2 else velo.at[f], fine, spans)
+    mean = pool_columns(jnp.concatenate(sums, 0))
+    copies[3].wait()
+    lane = lanes_of((height, 128))
+    cells[...] = jnp.zeros_like(cells)
+    for side in range(2):
+        begin = SIDE - HALO * side
+        for ch in range(7):
+            total = jnp.zeros((height, 128), F32)
+            for l in range(levels):
+                if ch < 4:
+                    x, shift = target[ch % 2, l].astype(F32), SIDE
+                else:
+                    at = ((2 * (ch - 4) + side) * levels + l) * height
+                    x, shift = mean[at : at + height], SIDE if side == 0 else SIDE - 128 // COARSE
+                at = 32 * l + begin
+                total = jnp.where((lane >= at) & (lane < at + HALO), pltpu.roll(x, (32 * l + shift) % 128, 1), total)
+            cells[side, pl.ds(ch, height, stride=8), :] = total
+    lane = lanes_of((rows, 128))
+    first = jnp.zeros((rows, 128), F32)
+    last = jnp.zeros((rows, 128), F32)
+    for f in range(3):
+        ref = temp if f == 2 else velo.at[f]
+        for l in range(levels):
+            n = f * levels + l
+            first = jnp.where(lane == n, pltpu.roll(ref[l, :, 0:128], n, 1), first)
+            last = jnp.where(lane == n, pltpu.roll(ref[l, :, cols - 128 :], n + 1, 1), last)
+    west, east = (jnp.concatenate([cells[i]] + halves(x), 0) for i, x in enumerate((first, last)))
+    to_lon[...] = jnp.where(heads_up("lon"), east, west).astype(BF16)
+    for copy in copies[4:]:
+        copy.wait()
+
+
+def coarse_kernel(velo, temp, target, own, edges, fine):
     levels, rows, cols = temp.shape
     height, width = rows // COARSE, cols // COARSE
     vregs = levels + 1
-    pool_r = subs_of((cols, width)) // COARSE
-    pool = jnp.where(pool_r == lanes_of((cols, width)), F32(1.0 / COARSE**2), F32(0.0))
+    spans = [slice(128 * j, 128 * (j + 1)) for j in range(cols // 128)]
 
     def field(f):
         return temp if f == 2 else velo.at[f]
 
-    means = []
-    for f in range(3):
-        copies[f].wait()
-        ref = field(f)
-        pieces = []
-        for j in range(cols // 128):
-            fine[j] = ref[:, :, 128 * j : 128 * (j + 1)].reshape(levels * rows, 128)
-            part = None
-            for s in range(COARSE):
-                piece = fine[j, pl.ds(s, levels * height, stride=COARSE), :]
-                part = piece if part is None else part + piece
-            pieces.append(part)
-        means.append(jnp.concatenate(pieces, 1))
-    mean = dot(jnp.concatenate(means, 0), pool, precision=HIGH)
-    mean = mean.astype(BF16).astype(F32)
-
-    copies[3].wait()
+    mean = pool_columns(jnp.concatenate([jnp.concatenate(row_sums(field(f), fine, spans), 1) for f in range(3)], 0))
     lane = lanes_of((height, 128))
 
     def place(tiles):
@@ -140,31 +177,9 @@
             pieces = [jnp.zeros((height, 128), F32)] * vregs
         for j in range(vregs):
             own[j, pl.ds(ch, height, stride=8), :] = pieces[j]
-    lane = lanes_of((8 * height, 128))
-    to_west = jnp.zeros((8 * height, 128), F32)
-    to_east = jnp.zeros((8 * height, 128), F32)
-    for l in range(levels):
-        here = (lane >= 32 * l) & (lane < 32 * (l + 1))
-        to_west = jnp.where(here, own[l], to_west)
-        to_east = jnp.where(here, own[l + 1], to_east)
-    lane = lanes_of((rows, 128))
-    first = jnp.zeros((rows, 128), F32)
-    last = jnp.zeros((rows, 128), F32)
-    for f in range(3):
-        ref = field(f)
-        for l in range(levels):
-            n = f * levels + l
-            first = jnp.where(lane == n, pltpu.roll(ref[l, :, 0:128], n, 1), first)
-            last = jnp.where(lane == n, pltpu.roll(ref[l, :, cols - 128 :], n + 1, 1), last)
-    tall = 8 * height
-    east = heads_up("lon")
-    cells = jnp.where(east, to_east, to_west)
-    to_lon[...] = jnp.concatenate([cells] + halves(jnp.where(east, last, first)), 0).astype(BF16)
     for i, row in enumerate((rows - 1, 0)):
         line = [field(f)[:, row, 128 * j : 128 * (j + 1)] for j in range(cols // 128) for f in range(3)]
         edges[i] = jnp.concatenate(line, 0)
-    for copy in copies[4:]:
-        copy.wait()
 
 
 def merge_kernel(own, got, other, edges, full, message):
@@ -625,27 +640,35 @@
     tall = 8 * height
     core = (0, 1)
     raw = (jnp.transpose(w_first, (1, 3, 0, 2)), w_middle, w_last)
-    own, to_lon, edges, *raw = pl.pallas_call(
-        coarse_kernel,
+    to_lon, velo, temp, target, *raw = pl.pallas_call(
+        edge_kernel,
         in_specs=[hbm] * 6,
         out_shape=(
-            vm((vregs, tall, 128), F32),
             vm((tall + 2 * rows, 128), BF16),
-            vm((2, 3 * levels * (cols // 128), 128), F32),
+            vm(velo.shape, F32),
+            vm(temp.shape, F32),
+            vm(target.shape, BF16),
             *(vm(w.shape, BF16) for w in raw),
         ),
         scratch_shapes=[
-            vm(velo.shape, F32),
-            vm(temp.shape, F32),
-            vm(target.shape, BF16),
-            vm((cols // 128, levels * rows, 128), F32),
+            vm((2, levels * rows, 128), F32),
+            vm((2, tall, 128), F32),
             pltpu.SemaphoreType.DMA((7,)),
         ],
         compiler_params=pltpu.CompilerParams(vmem_limit_bytes=COARSE_LIMIT),
-        name="coarse",
+        name="edge",
     )(velo, temp, target, *raw)
     everywhere = ("lat", "lon", "mem")
     got_lon = lax.ppermute(to_lon, everywhere, pairs_of(lon=core))
+    own, edges = pl.pallas_call(
+        coarse_kernel,
+        out_shape=(vm((vregs, tall, 128), F32), vm((2, 3 * levels * (cols // 128), 128), F32)),
+        scratch_shapes=[vm((cols // 128, levels * rows, 128), F32)],
+        cost_estimate=pl.CostEstimate(flops=5 * 10**8, bytes_accessed=2 * 10**6, transcendentals=0),
+        compiler_params=params,
+        name="coarse",
+    )(velo, temp, target)
+    got_lon, own, edges = lax.optimization_barrier((got_lon, own, edges))
     weights = pl.pallas_call(
         weights_kernel,
         out_shape=(

time: 44.4 us -> 44.2 us (level)
    pallas_call x1 -> x2, Pallas kernels: 1.71 us -> 1.95 us  [the longest x1 1.57 us: per_device(): pl.pallas_call(edge_kernel, in_specs=[hbm] * 6, out_shape=(vm((tall + 2 *...]
where the time goes in v4:
time: 44.2 us; the launch traced here: 44.1 us
  starting transfers between devices  17.4 us (39%)
  Pallas kernels  14.4 us (33%)
  waiting for transfers between devices  11.6 us (26%)
  between operations  0.72 us (2%)
    ppermute x9, starting transfers between devices, partner(): lax.ppermute(value, axis, [(i, i ^ k) for i in range(lax.axis_size(axis))])  11.5 us
    ppermute x9, waiting for transfers between devices, partner(): lax.ppermute(value, axis, [(i, i ^ k) for i in range(lax.axis_size(axis))])  7.02 us
    pallas_call x1, Pallas kernels, per_device(): pl.pallas_call(functools.partial(closure_kernel, 2.0 / count, total_coars...  5.25 us
    ppermute x1, starting transfers between devices, per_device(): got_lon = lax.ppermute(to_lon, everywhere, pairs_of(lon=core))  3.09 us
    pallas_call x1, Pallas kernels, per_device(): pl.pallas_call(outer_grads_kernel, out_shape=f32(48, 128), cost_estimate=...  2.27 us
    pallas_call x1, Pallas kernels, per_device(): pl.pallas_call(functools.partial(ocean_kernel, rows * nlat, members), out...  1.88 us
    pallas_call x1, Pallas kernels, per_device(): pl.pallas_call(edge_kernel, in_specs=[hbm] * 6, out_shape=(vm((tall + 2 *...  1.57 us
    ppermute x1, starting transfers between devices, per_device(): got_lat = lax.ppermute(to_lat, everywhere, pairs_of(lat=core))  1.56 us
  transfers between devices with their start and end apart: 14, of which 9 were waited for; matrix products, arithmetic and copies ran while one was open for 0% of the time, Pallas kernels for 14%

profile of v4, /device:TPU:0, one launch (start us, length us, event | category | flops | bytes accessed | tf_op | source)
XLA Modules:
  0.0 44.1 jit_solution(9299824529181446068)
XLA Ops:
  0.6 1.6 %edge.1 = (bf16[128,128]{1,0:T(8,128)(2,1)S(1)}, f32[2,4,32,512]{3,2,1,0:T(8,128)S(1)}, f32[4,32,512]{2,1,0:T(8,128)S(1)}, bf16[2,4,8,128]{3,2,1,0:T(8,128)(2,1)...) custom-call(f32[2,4,32,512]{3,2,1,0:T(8,128)} %velo_hbm.1, ...), custom_call_target="tpu_custom_call" | custom-call | tf_op jit(solution)/shard_map/edge/pallas_call | solution.py:643
  2.2 3.1 %collective-permute-start = (bf16[128,128]{1,0:T(8,128)(2,1)S(1)}, bf16[128,128]{1,0:T(8,128)(2,1)S(1)}, u32[]{:S(2)}, u32[]{:S(2)}) collective-permute-start(bf16[128,128]{1,0:T(8,128)(2,1)S(1)} %get-tuple-element.59), channel_id=1, source_target_pairs={{0,2},{1,7},{2,0},{3,5},{4,6},{5,3},{6,4},{7,1},{8,10},{9,15},{10,... | collective-permute-start | bytes 98312 | tf_op jit(solution)/shard_map/ppermute | solution.py:662
  5.3 0.4 coarse.1
  5.7 1.5 %collective-permute-done.got.got_lon = bf16[128,128]{1,0:T(8,128)(2,1)S(1)} collective-permute-done((bf16[128,128]{1,0:T(8,128)(2,1)S(1)}, bf16[128,128]{1,0:T(8,128)(2,1)S(1)}, u32[]{:S(2)}, u32[]{:S(2)}) %collective-permute-start) | collective-permute-done | bytes 32800 | tf_op jit(solution)/shard_map/ppermute | solution.py:662
  7.2 1.0 %collective-permute-start.1 = (bf16[128,128]{1,0:T(8,128)(2,1)S(1)}, bf16[128,128]{1,0:T(8,128)(2,1)S(1)}, u32[]{:S(2)}, u32[]{:S(2)}) collective-permute-start(bf16[128,128]{1,0:T(8,128)(2,1)S(1)} %collective-permute-done.got.got_lon), channel_id=1, source_target_pairs={{0,1},{1,0},{2,3},{3,2},{4,5},{5,4},{6,7},{7,6},{8,9},{9,8},{10,11... | collective-permute-start | bytes 98312 | tf_op jit(solution)/shard_map/ppermute | solution.py:613
  8.2 0.5 %weights.1 = (bf16[512,96]{1,0:T(8,128)(2,1)S(1)}, bf16[2,128,768]{2,1,0:T(8,128)(2,1)S(1)}, bf16[2,128,768]{2,1,0:T(8,128)(2,1)S(1)}, bf16[64,256]{1,0:T(8,128)(2,1)S(1)}, bf16[128,48]{1,0:T(8,128)(2,1)S(1)}) custom-call(bf16[9,3,2,64]{3,2,1,0:T(2,128)(2,1)S(1)} %get-tuple-element.70.first, bf16[2,9,64,64]{3,2,1,0:T(8,128)(2,1)S(1)} %get-tuple-element.71.middle, ...), custom_call_target="tpu_custom_call" | custom-call | flops 100000000 | bytes 4000000 | tf_op jit(solution)/shard_map/weights/pallas_call | solution.py:672
  8.7 0.3 collective-permute-done.1.other.other_lon
  9.0 0.1 merge.1
  9.1 1.6 %collective-permute-start.2 = (bf16[192,128]{1,0:T(8,128)(2,1)S(1)}, bf16[192,128]{1,0:T(8,128)(2,1)S(1)}, u32[]{:S(2)}, u32[]{:S(2)}) collective-permute-start(bf16[192,128]{1,0:T(8,128)(2,1)S(1)} %get-tuple-element.69), channel_id=1, source_target_pairs={{0,8},{1,25},{2,10},{3,27},{4,12},{5,29},{6,14},{7,31},{8,0},{9,17... | collective-permute-start | bytes 147464 | tf_op jit(solution)/shard_map/ppermute | solution.py:693
  10.7 1.2 %inner.1 = (bf16[3,2,384,640]{3,2,1,0:T(8,128)(2,1)S(1)}, bf16[512,640]{1,0:T(8,128)(2,1)S(1)}) custom-call(f32[5,64,128]{2,1,0:T(8,128)S(1)} %get-tuple-element.68.full, bf16[512,96]{1,0:T(8,128)(2,1)S(1)} %get-tuple-element.83.wf, bf16[2,128,768]{2,1,0:T(8,128)(2,1)S(1)} %get-tuple-element.84.wm), custom_call_target="tpu_custom_call" | custom-call | flops 1000000000 | bytes 4000000 | tf_op jit(solution)/shard_map/inner/pallas_call | solution.py:695
  11.9 1.5 %collective-permute-done.2.got.got_lat = bf16[192,128]{1,0:T(8,128)(2,1)S(1)} collective-permute-done((bf16[192,128]{1,0:T(8,128)(2,1)S(1)}, bf16[192,128]{1,0:T(8,128)(2,1)S(1)}, u32[]{:S(2)}, u32[]{:S(2)}) %collective-permute-start.2) | collective-permute-done | bytes 49184 | tf_op jit(solution)/shard_map/ppermute | solution.py:693
  13.4 0.0 collective-permute-start.3
  13.4 1.2 %collective-permute-done.3.other.other_lat = bf16[192,128]{1,0:T(8,128)(2,1)S(1)} collective-permute-done((bf16[192,128]{1,0:T(8,128)(2,1)S(1)}, bf16[192,128]{1,0:T(8,128)(2,1)S(1)}, u32[]{:S(2)}, u32[]{:S(2)}) %collective-permute-start.3) | collective-permute-done | bytes 49184 | tf_op jit(solution)/shard_map/ppermute | solution.py:613
  14.7 5.3 %closure.1 = (bf16[16,640]{1,0:T(8,128)(2,1)S(1)}, s16[160,128]{1,0:T(8,128)(2,1)S(1)}, s16[160,128]{1,0:T(8,128)(2,1)S(1)}, s16[160,128]{1,0:T(8,128)(2,1)S(1)}...) custom-call(f32[5,64,128]{2,1,0:T(8,128)S(1)} %get-tuple-element.68., ...), custom_call_target="tpu_custom_call" | custom-call | tf_op jit(solution)/shard_map/closure/pallas_call | solution.py:710
  19.9 0.2 collective-permute-start.7
  20.2 1.5 %collective-permute-start.4 = (s16[160,128]{1,0:T(8,128)(2,1)S(1)}, s16[160,128]{1,0:T(8,128)(2,1)S(1)}, u32[]{:S(2)}, u32[]{:S(2)}) collective-permute-start(s16[160,128]{1,0:T(8,128)(2,1)S(1)} %get-tuple-element.94), channel_id=1, source_target_pairs={{0,8},{8,0},{16,24},{24,16},{1,9},{9,1},{17,25},{25,17},{2,10},{10... | collective-permute-start | bytes 122888 | tf_op jit(solution)/shard_map/ppermute | solution.py:617
  21.7 1.5 %collective-permute-start.5 = (s16[160,128]{1,0:T(8,128)(2,1)S(1)}, s16[160,128]{1,0:T(8,128)(2,1)S(1)}, u32[]{:S(2)}, u32[]{:S(2)}) collective-permute-start(s16[160,128]{1,0:T(8,128)(2,1)S(1)} %get-tuple-element.95), channel_id=1, source_target_pairs={{0,16},{8,24},{16,0},{24,8},{1,17},{9,25},{17,1},{25,9},{2,18},{10... | collective-permute-start | bytes 122888 | tf_op jit(solution)/shard_map/ppermute | solution.py:617
  23.1 0.5 %collective-permute-start.6 = (s16[160,128]{1,0:T(8,128)(2,1)S(1)}, s16[160,128]{1,0:T(8,128)(2,1)S(1)}, u32[]{:S(2)}, u32[]{:S(2)}) collective-permute-start(s16[160,128]{1,0:T(8,128)(2,1)S(1)} %get-tuple-element.96), channel_id=1, source_target_pairs={{0,24},{8,16},{16,8},{24,0},{1,25},{9,17},{17,9},{25,1},{2,26},{10... | collective-permute-start | bytes 122888 | tf_op jit(solution)/shard_map/ppermute | solution.py:617
  23.6 0.0 copy-start
  23.7 2.3 %outer_grads.1.outer = f32[48,128]{1,0:T(8,128)S(1)} custom-call(bf16[288,640]{1,0:T(8,128)(2,1)S(1)} %get-tuple-element.88.xb, bf16[2,512,640]{2,1,0:T(8,128)(2,1)S(1)} %get-tuple-element.89.inner, bf16[1792,640]{1,0:T(8,128)(2,1)S(1)} %get-tuple-element.90.h2, bf16[192,640]{1,0:T(8,128)(2,1)S(1)} %get-tuple-element.91.gb, ...), custom_call_target="tpu_custom_call" | custom-call | flops 2000000000 | bytes 4000000 | tf_op jit(solution)/shard_map/outer_grads/pallas_call | solution.py:736
  25.9 0.0 collective-permute-done.7.other
  25.9 0.0 collective-permute-done.4.refs_0_
  25.9 0.0 collective-permute-done.5.refs_1_
  26.0 2.1 %collective-permute-done.6.refs_2_ = s16[160,128]{1,0:T(8,128)(2,1)S(1)} collective-permute-done((s16[160,128]{1,0:T(8,128)(2,1)S(1)}, s16[160,128]{1,0:T(8,128)(2,1)S(1)}, u32[]{:S(2)}, u32[]{:S(2)}) %collective-permute-start.6) | collective-permute-done | bytes 40992 | tf_op jit(solution)/shard_map/ppermute | solution.py:617
  28.0 0.1 sum_lat.1.refs_0_
  28.1 3.6 %collective-permute-start.10 = (s16[208,128]{1,0:T(8,128)(2,1)S(1)}, s16[208,128]{1,0:T(8,128)(2,1)S(1)}, u32[]{:S(2)}, u32[]{:S(2)}) collective-permute-start(s16[208,128]{1,0:T(8,128)(2,1)S(1)} %sum_lat.1.refs_0_), channel_id=1, source_target_pairs={{0,6},{2,4},{4,2},{6,0},{1,7},{3,5},{5,3},{7,1},{8,14},{10,12},{12... | collective-permute-start | bytes 159752 | tf_op jit(solution)/shard_map/ppermute | solution.py:617
  31.7 0.0 collective-permute-start.9
  31.7 0.8 %collective-permute-start.8 = (s16[208,128]{1,0:T(8,128)(2,1)S(1)}, s16[208,128]{1,0:T(8,128)(2,1)S(1)}, u32[]{:S(2)}, u32[]{:S(2)}) collective-permute-start(s16[208,128]{1,0:T(8,128)(2,1)S(1)} %sum_lat.1.refs_0_), channel_id=1, source_target_pairs={{0,2},{2,0},{4,6},{6,4},{1,3},{3,1},{5,7},{7,5},{8,10},{10,8},{12,... | collective-permute-start | bytes 159752 | tf_op jit(solution)/shard_map/ppermute | solution.py:617
  32.6 0.0 copy-done
  32.6 1.9 %ocean.1 = (f32[2,4,32,512]{3,2,1,0:T(8,128)}, f32[4,32,512]{2,1,0:T(8,128)}) custom-call(f32[2,4,32,512]{3,2,1,0:T(8,128)S(1)} %get-tuple-element.60.velo, f32[4,32,512]{2,1,0:T(8,128)S(1)} %get-tuple-element.61.temp, s32[32,512]{1,0:T(8,128)S(1)} %copy-done, bf16[16,640]{1,0:T(8,128)(2,1)S(1)} %get-tuple-element.97.mine, ...), custom_call_target="tpu_custom_call" | custom-call | flops 100000000 | bytes 4000000 | tf_op jit(solution)/shard_map/ocean/pallas_call | solution.py:753
  34.4 0.0 collective-permute-done.10.refs_3_
  34.5 2.3 %collective-permute-done.9.refs_2_ = s16[208,128]{1,0:T(8,128)(2,1)S(1)} collective-permute-done((s16[208,128]{1,0:T(8,128)(2,1)S(1)}, s16[208,128]{1,0:T(8,128)(2,1)S(1)}, u32[]{:S(2)}, u32[]{:S(2)}) %collective-permute-start.9) | collective-permute-done | bytes 53280 | tf_op jit(solution)/shard_map/ppermute | solution.py:617
  36.8 0.0 collective-permute-done.8.refs_1_
  36.8 0.1 sum_lon.1.refs_0_
  36.9 0.6 %collective-permute-start.13 = (s16[208,128]{1,0:T(8,128)(2,1)S(1)}, s16[208,128]{1,0:T(8,128)(2,1)S(1)}, u32[]{:S(2)}, u32[]{:S(2)}) collective-permute-start(s16[208,128]{1,0:T(8,128)(2,1)S(1)} %sum_lon.1.refs_0_), channel_id=1, source_target_pairs={{0,24},{8,16},{16,8},{24,0},{1,25},{9,17},{17,9},{25,1},{2,26},{10... | collective-permute-start | bytes 159752 | tf_op jit(solution)/shard_map/ppermute | solution.py:617
  37.5 1.4 %collective-permute-start.12 = (s16[208,128]{1,0:T(8,128)(2,1)S(1)}, s16[208,128]{1,0:T(8,128)(2,1)S(1)}, u32[]{:S(2)}, u32[]{:S(2)}) collective-permute-start(s16[208,128]{1,0:T(8,128)(2,1)S(1)} %sum_lon.1.refs_0_), channel_id=1, source_target_pairs={{0,16},{8,24},{16,0},{24,8},{1,17},{9,25},{17,1},{25,9},{2,18},{10... | collective-permute-start | bytes 159752 | tf_op jit(solution)/shard_map/ppermute | solution.py:617
  38.9 1.5 %collective-permute-start.11 = (s16[208,128]{1,0:T(8,128)(2,1)S(1)}, s16[208,128]{1,0:T(8,128)(2,1)S(1)}, u32[]{:S(2)}, u32[]{:S(2)}) collective-permute-start(s16[208,128]{1,0:T(8,128)(2,1)S(1)} %sum_lon.1.refs_0_), channel_id=1, source_target_pairs={{0,8},{8,0},{16,24},{24,16},{1,9},{9,1},{17,25},{25,17},{2,10},{10... | collective-permute-start | bytes 159752 | tf_op jit(solution)/shard_map/ppermute | solution.py:617
  40.4 1.7 %collective-permute-done.13.refs_3_ = s16[208,128]{1,0:T(8,128)(2,1)S(1)} collective-permute-done((s16[208,128]{1,0:T(8,128)(2,1)S(1)}, s16[208,128]{1,0:T(8,128)(2,1)S(1)}, u32[]{:S(2)}, u32[]{:S(2)}) %collective-permute-start.13) | collective-permute-done | bytes 53280 | tf_op jit(solution)/shard_map/ppermute | solution.py:617
  42.1 0.1 collective-permute-done.12.refs_2_
  42.2 0.8 %collective-permute-done.11.refs_1_ = s16[208,128]{1,0:T(8,128)(2,1)S(1)} collective-permute-done((s16[208,128]{1,0:T(8,128)(2,1)S(1)}, s16[208,128]{1,0:T(8,128)(2,1)S(1)}, u32[]{:S(2)}, u32[]{:S(2)}) %collective-permute-start.11) | collective-permute-done | bytes 53280 | tf_op jit(solution)/shard_map/ppermute | solution.py:617
  43.1 1.0 %finish.1 = (f32[9,3,2,64]{3,2,1,0:T(2,128)}, f32[2,9,64,64]{3,2,1,0:T(8,128)}, f32[2,9,2,64]{3,2,1,0:T(2,128)}) custom-call(s16[208,128]{1,0:T(8,128)(2,1)S(1)} %sum_lon.1.refs_0_, s16[208,128]{1,0:T(8,128)(2,1)S(1)} %collective-permute-done.11.refs_1_, s16[208,128]{1,0:T(8,128)(2,1)S(1)} %collective-permute-done.12.refs_2_, ...), custom_call_target="tpu_custom_call" | custom-call | tf_op jit(solution)/shard_map/finish/pallas_call | solution.py:765
Async XLA Ops:
  2.2 5.0 %collective-permute-start = (bf16[128,128]{1,0:T(8,128)(2,1)S(1)}, bf16[128,128]{1,0:T(8,128)(2,1)S(1)}, u32[]{:S(2)}, u32[]{:S(2)}) collective-permute-start(bf16[128,128]{1,0:T(8,128)(2,1)S(1)} %get-tuple-element.59), channel_id=1, source_target_pairs={{0,2},{1,7},{2,0},{3,5},{4,6},{5,3},{6,4},{7,1},{8,10},{9,15},{10,... | collective-permute-start | bytes 98312 | tf_op jit(solution)/shard_map/ppermute | solution.py:662
  7.2 1.9 %collective-permute-start.1 = (bf16[128,128]{1,0:T(8,128)(2,1)S(1)}, bf16[128,128]{1,0:T(8,128)(2,1)S(1)}, u32[]{:S(2)}, u32[]{:S(2)}) collective-permute-start(bf16[128,128]{1,0:T(8,128)(2,1)S(1)} %collective-permute-done.got.got_lon), channel_id=1, source_target_pairs={{0,1},{1,0},{2,3},{3,2},{4,5},{5,4},{6,7},{7,6},{8,9},{9,8},{10,11... | collective-permute-start | bytes 98312 | tf_op jit(solution)/shard_map/ppermute | solution.py:613
  9.1 4.3 %collective-permute-start.2 = (bf16[192,128]{1,0:T(8,128)(2,1)S(1)}, bf16[192,128]{1,0:T(8,128)(2,1)S(1)}, u32[]{:S(2)}, u32[]{:S(2)}) collective-permute-start(bf16[192,128]{1,0:T(8,128)(2,1)S(1)} %get-tuple-element.69), channel_id=1, source_target_pairs={{0,8},{1,25},{2,10},{3,27},{4,12},{5,29},{6,14},{7,31},{8,0},{9,17... | collective-permute-start | bytes 147464 | tf_op jit(solution)/shard_map/ppermute | solution.py:693
  13.4 1.2 %collective-permute-start.3 = (bf16[192,128]{1,0:T(8,128)(2,1)S(1)}, bf16[192,128]{1,0:T(8,128)(2,1)S(1)}, u32[]{:S(2)}, u32[]{:S(2)}) collective-permute-start(bf16[192,128]{1,0:T(8,128)(2,1)S(1)} %collective-permute-done.2.got.got_lat), channel_id=1, source_target_pairs={{0,1},{1,0},{2,3},{3,2},{4,5},{5,4},{6,7},{7,6},{8,9},{9,8},{10,11... | collective-permute-start | bytes 147464 | tf_op jit(solution)/shard_map/ppermute | solution.py:613
  19.9 6.0 %collective-permute-start.7 = (bf16[16,640]{1,0:T(8,128)(2,1)S(1)}, bf16[16,640]{1,0:T(8,128)(2,1)S(1)}, u32[]{:S(2)}, u32[]{:S(2)}) collective-permute-start(bf16[16,640]{1,0:T(8,128)(2,1)S(1)} %get-tuple-element.97.mine), channel_id=1, source_target_pairs={{0,1},{1,0},{2,3},{3,2},{4,5},{5,4},{6,7},{7,6},{8,9},{9,8},{10,11... | collective-permute-start | bytes 61448 | tf_op jit(solution)/shard_map/ppermute | solution.py:613
  20.2 5.8 %collective-permute-start.4 = (s16[160,128]{1,0:T(8,128)(2,1)S(1)}, s16[160,128]{1,0:T(8,128)(2,1)S(1)}, u32[]{:S(2)}, u32[]{:S(2)}) collective-permute-start(s16[160,128]{1,0:T(8,128)(2,1)S(1)} %get-tuple-element.94), channel_id=1, source_target_pairs={{0,8},{8,0},{16,24},{24,16},{1,9},{9,1},{17,25},{25,17},{2,10},{10... | collective-permute-start | bytes 122888 | tf_op jit(solution)/shard_map/ppermute | solution.py:617
  21.7 4.3 %collective-permute-start.5 = (s16[160,128]{1,0:T(8,128)(2,1)S(1)}, s16[160,128]{1,0:T(8,128)(2,1)S(1)}, u32[]{:S(2)}, u32[]{:S(2)}) collective-permute-start(s16[160,128]{1,0:T(8,128)(2,1)S(1)} %get-tuple-element.95), channel_id=1, source_target_pairs={{0,16},{8,24},{16,0},{24,8},{1,17},{9,25},{17,1},{25,9},{2,18},{10... | collective-permute-start | bytes 122888 | tf_op jit(solution)/shard_map/ppermute | solution.py:617
  23.1 4.9 %collective-permute-start.6 = (s16[160,128]{1,0:T(8,128)(2,1)S(1)}, s16[160,128]{1,0:T(8,128)(2,1)S(1)}, u32[]{:S(2)}, u32[]{:S(2)}) collective-permute-start(s16[160,128]{1,0:T(8,128)(2,1)S(1)} %get-tuple-element.96), channel_id=1, source_target_pairs={{0,24},{8,16},{16,8},{24,0},{1,25},{9,17},{17,9},{25,1},{2,26},{10... | collective-permute-start | bytes 122888 | tf_op jit(solution)/shard_map/ppermute | solution.py:617
  23.6 8.9 %copy-start = (s32[32,512]{1,0:T(8,128)S(1)}, s32[32,512]{1,0:T(8,128)}, u32[]{:S(2)}) copy-start(s32[32,512]{1,0:T(8,128)} %land.1) | copy-start | bytes 196612
  28.1 6.3 %collective-permute-start.10 = (s16[208,128]{1,0:T(8,128)(2,1)S(1)}, s16[208,128]{1,0:T(8,128)(2,1)S(1)}, u32[]{:S(2)}, u32[]{:S(2)}) collective-permute-start(s16[208,128]{1,0:T(8,128)(2,1)S(1)} %sum_lat.1.refs_0_), channel_id=1, source_target_pairs={{0,6},{2,4},{4,2},{6,0},{1,7},{3,5},{5,3},{7,1},{8,14},{10,12},{12... | collective-permute-start | bytes 159752 | tf_op jit(solution)/shard_map/ppermute | solution.py:617
  31.7 5.0 %collective-permute-start.9 = (s16[208,128]{1,0:T(8,128)(2,1)S(1)}, s16[208,128]{1,0:T(8,128)(2,1)S(1)}, u32[]{:S(2)}, u32[]{:S(2)}) collective-permute-start(s16[208,128]{1,0:T(8,128)(2,1)S(1)} %sum_lat.1.refs_0_), channel_id=1, source_target_pairs={{0,4},{2,6},{4,0},{6,2},{1,5},{3,7},{5,1},{7,3},{8,12},{10,14},{12... | collective-permute-start | bytes 159752 | tf_op jit(solution)/shard_map/ppermute | solution.py:617
  31.7 5.0 %collective-permute-start.8 = (s16[208,128]{1,0:T(8,128)(2,1)S(1)}, s16[208,128]{1,0:T(8,128)(2,1)S(1)}, u32[]{:S(2)}, u32[]{:S(2)}) collective-permute-start(s16[208,128]{1,0:T(8,128)(2,1)S(1)} %sum_lat.1.refs_0_), channel_id=1, source_target_pairs={{0,2},{2,0},{4,6},{6,4},{1,3},{3,1},{5,7},{7,5},{8,10},{10,8},{12,... | collective-permute-start | bytes 159752 | tf_op jit(solution)/shard_map/ppermute | solution.py:617
  36.9 5.2 %collective-permute-start.13 = (s16[208,128]{1,0:T(8,128)(2,1)S(1)}, s16[208,128]{1,0:T(8,128)(2,1)S(1)}, u32[]{:S(2)}, u32[]{:S(2)}) collective-permute-start(s16[208,128]{1,0:T(8,128)(2,1)S(1)} %sum_lon.1.refs_0_), channel_id=1, source_target_pairs={{0,24},{8,16},{16,8},{24,0},{1,25},{9,17},{17,9},{25,1},{2,26},{10... | collective-permute-start | bytes 159752 | tf_op jit(solution)/shard_map/ppermute | solution.py:617
  37.5 4.7 %collective-permute-start.12 = (s16[208,128]{1,0:T(8,128)(2,1)S(1)}, s16[208,128]{1,0:T(8,128)(2,1)S(1)}, u32[]{:S(2)}, u32[]{:S(2)}) collective-permute-start(s16[208,128]{1,0:T(8,128)(2,1)S(1)} %sum_lon.1.refs_0_), channel_id=1, source_target_pairs={{0,16},{8,24},{16,0},{24,8},{1,17},{9,25},{17,1},{25,9},{2,18},{10... | collective-permute-start | bytes 159752 | tf_op jit(solution)/shard_map/ppermute | solution.py:617
  38.9 4.1 %collective-permute-start.11 = (s16[208,128]{1,0:T(8,128)(2,1)S(1)}, s16[208,128]{1,0:T(8,128)(2,1)S(1)}, u32[]{:S(2)}, u32[]{:S(2)}) collective-permute-start(s16[208,128]{1,0:T(8,128)(2,1)S(1)} %sum_lon.1.refs_0_), channel_id=1, source_target_pairs={{0,8},{8,0},{16,24},{24,16},{1,9},{9,1},{17,25},{25,17},{2,10},{10... | collective-permute-start | bytes 159752 | tf_op jit(solution)/shard_map/ppermute | solution.py:617

commit v5 on v4

--- a/solution.py
+++ b/solution.py
@@ -278,7 +278,7 @@
 
 def closure_kernel(
     scale, total_rows,
-    full, got, other, h1_inner, h2_inner, wf, wm, wl, wlt,
+    full, got, other, h1_inner, h2_inner, xb_inner, wf, wm, wl, wlt,
     force, *rest,
 ):
     nlat = lax.axis_size("lat")
@@ -301,7 +301,8 @@
     sub = subs_of((8, wide))
     tile_b = inner_lanes(wide).astype(BF16)
 
-    for r in range(span):
+    xb[16 * HALO : 16 * (HALO + height), :] = xb_inner[...]
+    for r in (*range(HALO), *range(HALO + height, span)):
         xb[16 * r : 16 * (r + 1), :] = spread_columns(window(xf, r, 1, 8))
 
     known = range(5, height + 3)
@@ -694,8 +695,11 @@
     wf, wm, wb, wl, wlt = weights
     tops = pl.pallas_call(
         inner_kernel,
-        out_shape=(vm((3, 2, 64 * (height - 2), wide), BF16), vm((128 * (height - 4), wide), BF16)),
-        scratch_shapes=[vm((16 * height, wide), BF16)],
+        out_shape=(
+            vm((3, 2, 64 * (height - 2), wide), BF16),
+            vm((128 * (height - 4), wide), BF16),
+            vm((16 * height, wide), BF16),
+        ),
         cost_estimate=pl.CostEstimate(flops=10**9, bytes_accessed=4 * 10**6, transcendentals=0),
         compiler_params=params,
         name="inner",

time: 44.2 us -> 44.1 us (level)
  no operation moved by 1% of the time
where the time goes in v5:
time: 44.1 us; the launch traced here: 44 us
  starting transfers between devices  17.4 us (39%)
  Pallas kernels  14.2 us (32%)
  waiting for transfers between devices  11.7 us (27%)
  between operations  0.72 us (2%)
    ppermute x9, starting transfers between devices, partner(): lax.ppermute(value, axis, [(i, i ^ k) for i in range(lax.axis_size(axis))])  11.5 us
    ppermute x9, waiting for transfers between devices, partner(): lax.ppermute(value, axis, [(i, i ^ k) for i in range(lax.axis_size(axis))])  7.01 us
    pallas_call x1, Pallas kernels, per_device(): pl.pallas_call(functools.partial(closure_kernel, 2.0 / count, total_coars...  5.15 us
    ppermute x1, starting transfers between devices, per_device(): got_lon = lax.ppermute(to_lon, everywhere, pairs_of(lon=core))  3.09 us
    pallas_call x1, Pallas kernels, per_device(): pl.pallas_call(outer_grads_kernel, out_shape=f32(48, 128), cost_estimate=...  2.27 us
    pallas_call x1, Pallas kernels, per_device(): pl.pallas_call(functools.partial(ocean_kernel, rows * nlat, members), out...  1.88 us
    ppermute x1, waiting for transfers between devices, per_device(): got_lat = lax.ppermute(to_lat, everywhere, pairs_of(lat=core))  1.59 us
    pallas_call x1, Pallas kernels, per_device(): pl.pallas_call(edge_kernel, in_specs=[hbm] * 6, out_shape=(vm((tall + 2 *...  1.57 us
  transfers between devices with their start and end apart: 14, of which 9 were waited for; matrix products, arithmetic and copies ran while one was open for 0% of the time, Pallas kernels for 14%

profile of v5, /device:TPU:0, one launch (start us, length us, event | category | flops | bytes accessed | tf_op | source)
XLA Modules:
  0.0 44.0 jit_solution(8501168577525999649)
XLA Ops:
  0.6 1.6 %edge.1 = (bf16[128,128]{1,0:T(8,128)(2,1)S(1)}, f32[2,4,32,512]{3,2,1,0:T(8,128)S(1)}, f32[4,32,512]{2,1,0:T(8,128)S(1)}, bf16[2,4,8,128]{3,2,1,0:T(8,128)(2,1)...) custom-call(f32[2,4,32,512]{3,2,1,0:T(8,128)} %velo_hbm.1, ...), custom_call_target="tpu_custom_call" | custom-call | tf_op jit(solution)/shard_map/edge/pallas_call | solution.py:644
  2.2 3.1 %collective-permute-start = (bf16[128,128]{1,0:T(8,128)(2,1)S(1)}, bf16[128,128]{1,0:T(8,128)(2,1)S(1)}, u32[]{:S(2)}, u32[]{:S(2)}) collective-permute-start(bf16[128,128]{1,0:T(8,128)(2,1)S(1)} %get-tuple-element.61), channel_id=1, source_target_pairs={{0,2},{1,7},{2,0},{3,5},{4,6},{5,3},{6,4},{7,1},{8,10},{9,15},{10,... | collective-permute-start | bytes 98312 | tf_op jit(solution)/shard_map/ppermute | solution.py:663
  5.3 0.4 coarse.1
  5.7 1.5 %collective-permute-done.got.got_lon = bf16[128,128]{1,0:T(8,128)(2,1)S(1)} collective-permute-done((bf16[128,128]{1,0:T(8,128)(2,1)S(1)}, bf16[128,128]{1,0:T(8,128)(2,1)S(1)}, u32[]{:S(2)}, u32[]{:S(2)}) %collective-permute-start) | collective-permute-done | bytes 32800 | tf_op jit(solution)/shard_map/ppermute | solution.py:663
  7.2 1.0 %collective-permute-start.1 = (bf16[128,128]{1,0:T(8,128)(2,1)S(1)}, bf16[128,128]{1,0:T(8,128)(2,1)S(1)}, u32[]{:S(2)}, u32[]{:S(2)}) collective-permute-start(bf16[128,128]{1,0:T(8,128)(2,1)S(1)} %collective-permute-done.got.got_lon), channel_id=1, source_target_pairs={{0,1},{1,0},{2,3},{3,2},{4,5},{5,4},{6,7},{7,6},{8,9},{9,8},{10,11... | collective-permute-start | bytes 98312 | tf_op jit(solution)/shard_map/ppermute | solution.py:614
  8.2 0.5 %weights.1 = (bf16[512,96]{1,0:T(8,128)(2,1)S(1)}, bf16[2,128,768]{2,1,0:T(8,128)(2,1)S(1)}, bf16[2,128,768]{2,1,0:T(8,128)(2,1)S(1)}, bf16[64,256]{1,0:T(8,128)(2,1)S(1)}, bf16[128,48]{1,0:T(8,128)(2,1)S(1)}) custom-call(bf16[9,3,2,64]{3,2,1,0:T(2,128)(2,1)S(1)} %get-tuple-element.72.first, bf16[2,9,64,64]{3,2,1,0:T(8,128)(2,1)S(1)} %get-tuple-element.73.middle, ...), custom_call_target="tpu_custom_call" | custom-call | flops 100000000 | bytes 4000000 | tf_op jit(solution)/shard_map/weights/pallas_call | solution.py:673
  8.7 0.3 collective-permute-done.1.other.other_lon
  9.0 0.1 merge.1
  9.1 1.6 %collective-permute-start.2 = (bf16[192,128]{1,0:T(8,128)(2,1)S(1)}, bf16[192,128]{1,0:T(8,128)(2,1)S(1)}, u32[]{:S(2)}, u32[]{:S(2)}) collective-permute-start(bf16[192,128]{1,0:T(8,128)(2,1)S(1)} %get-tuple-element.71), channel_id=1, source_target_pairs={{0,8},{1,25},{2,10},{3,27},{4,12},{5,29},{6,14},{7,31},{8,0},{9,17... | collective-permute-start | bytes 147464 | tf_op jit(solution)/shard_map/ppermute | solution.py:694
  10.7 1.2 %inner.1 = (bf16[3,2,384,640]{3,2,1,0:T(8,128)(2,1)S(1)}, bf16[512,640]{1,0:T(8,128)(2,1)S(1)}, bf16[128,640]{1,0:T(8,128)(2,1)S(1)}) custom-call(f32[5,64,128]{2,1,0:T(8,128)S(1)} %get-tuple-element.70.full, bf16[512,96]{1,0:T(8,128)(2,1)S(1)} %get-tuple-element.87.wf, bf16[2,128,768]{2,1,0:T(8,128)(2,1)S(1)} %get-tuple-element.88.wm), custom_call_target="tpu_custom_call" | custom-call | flops 1000000000 | bytes 4000000 | tf_op jit(solution)/shard_map/inner/pallas_call | solution.py:696
  11.9 1.6 %collective-permute-done.2.got.got_lat = bf16[192,128]{1,0:T(8,128)(2,1)S(1)} collective-permute-done((bf16[192,128]{1,0:T(8,128)(2,1)S(1)}, bf16[192,128]{1,0:T(8,128)(2,1)S(1)}, u32[]{:S(2)}, u32[]{:S(2)}) %collective-permute-start.2) | collective-permute-done | bytes 49184 | tf_op jit(solution)/shard_map/ppermute | solution.py:694
  13.4 0.0 collective-permute-start.3
  13.4 1.2 %collective-permute-done.3.other.other_lat = bf16[192,128]{1,0:T(8,128)(2,1)S(1)} collective-permute-done((bf16[192,128]{1,0:T(8,128)(2,1)S(1)}, bf16[192,128]{1,0:T(8,128)(2,1)S(1)}, u32[]{:S(2)}, u32[]{:S(2)}) %collective-permute-start.3) | collective-permute-done | bytes 49184 | tf_op jit(solution)/shard_map/ppermute | solution.py:614
  14.7 5.1 %closure.1 = (bf16[16,640]{1,0:T(8,128)(2,1)S(1)}, s16[160,128]{1,0:T(8,128)(2,1)S(1)}, s16[160,128]{1,0:T(8,128)(2,1)S(1)}, s16[160,128]{1,0:T(8,128)(2,1)S(1)}...) custom-call(f32[5,64,128]{2,1,0:T(8,128)S(1)} %get-tuple-element.70., ...), custom_call_target="tpu_custom_call" | custom-call | tf_op jit(solution)/shard_map/closure/pallas_call | solution.py:714
  19.8 0.2 collective-permute-start.7
  20.1 1.5 %collective-permute-start.4 = (s16[160,128]{1,0:T(8,128)(2,1)S(1)}, s16[160,128]{1,0:T(8,128)(2,1)S(1)}, u32[]{:S(2)}, u32[]{:S(2)}) collective-permute-start(s16[160,128]{1,0:T(8,128)(2,1)S(1)} %get-tuple-element.98), channel_id=1, source_target_pairs={{0,8},{8,0},{16,24},{24,16},{1,9},{9,1},{17,25},{25,17},{2,10},{10... | collective-permute-start | bytes 122888 | tf_op jit(solution)/shard_map/ppermute | solution.py:618
  21.6 1.5 %collective-permute-start.5 = (s16[160,128]{1,0:T(8,128)(2,1)S(1)}, s16[160,128]{1,0:T(8,128)(2,1)S(1)}, u32[]{:S(2)}, u32[]{:S(2)}) collective-permute-start(s16[160,128]{1,0:T(8,128)(2,1)S(1)} %get-tuple-element.99), channel_id=1, source_target_pairs={{0,16},{8,24},{16,0},{24,8},{1,17},{9,25},{17,1},{25,9},{2,18},{10... | collective-permute-start | bytes 122888 | tf_op jit(solution)/shard_map/ppermute | solution.py:618
  23.0 0.5 %collective-permute-start.6 = (s16[160,128]{1,0:T(8,128)(2,1)S(1)}, s16[160,128]{1,0:T(8,128)(2,1)S(1)}, u32[]{:S(2)}, u32[]{:S(2)}) collective-permute-start(s16[160,128]{1,0:T(8,128)(2,1)S(1)} %get-tuple-element.100), channel_id=1, source_target_pairs={{0,24},{8,16},{16,8},{24,0},{1,25},{9,17},{17,9},{25,1},{2,26},{10... | collective-permute-start | bytes 122888 | tf_op jit(solution)/shard_map/ppermute | solution.py:618
  23.5 0.0 copy-start
  23.5 2.3 %outer_grads.1.outer = f32[48,128]{1,0:T(8,128)S(1)} custom-call(bf16[288,640]{1,0:T(8,128)(2,1)S(1)} %get-tuple-element.92.xb, bf16[2,512,640]{2,1,0:T(8,128)(2,1)S(1)} %get-tuple-element.93.inner, bf16[1792,640]{1,0:T(8,128)(2,1)S(1)} %get-tuple-element.94.h2, bf16[192,640]{1,0:T(8,128)(2,1)S(1)} %get-tuple-element.95.gb, ...), custom_call_target="tpu_custom_call" | custom-call | flops 2000000000 | bytes 4000000 | tf_op jit(solution)/shard_map/outer_grads/pallas_call | solution.py:740
  25.8 0.0 collective-permute-done.7.other
  25.8 0.0 collective-permute-done.4.refs_0_
  25.8 0.0 collective-permute-done.5.refs_1_
  25.9 2.1 %collective-permute-done.6.refs_2_ = s16[160,128]{1,0:T(8,128)(2,1)S(1)} collective-permute-done((s16[160,128]{1,0:T(8,128)(2,1)S(1)}, s16[160,128]{1,0:T(8,128)(2,1)S(1)}, u32[]{:S(2)}, u32[]{:S(2)}) %collective-permute-start.6) | collective-permute-done | bytes 40992 | tf_op jit(solution)/shard_map/ppermute | solution.py:618
  27.9 0.1 sum_lat.1.refs_0_
  28.0 3.6 %collective-permute-start.10 = (s16[208,128]{1,0:T(8,128)(2,1)S(1)}, s16[208,128]{1,0:T(8,128)(2,1)S(1)}, u32[]{:S(2)}, u32[]{:S(2)}) collective-permute-start(s16[208,128]{1,0:T(8,128)(2,1)S(1)} %sum_lat.1.refs_0_), channel_id=1, source_target_pairs={{0,6},{2,4},{4,2},{6,0},{1,7},{3,5},{5,3},{7,1},{8,14},{10,12},{12... | collective-permute-start | bytes 159752 | tf_op jit(solution)/shard_map/ppermute | solution.py:618
  31.6 0.0 collective-permute-start.9
  31.6 0.8 %collective-permute-start.8 = (s16[208,128]{1,0:T(8,128)(2,1)S(1)}, s16[208,128]{1,0:T(8,128)(2,1)S(1)}, u32[]{:S(2)}, u32[]{:S(2)}) collective-permute-start(s16[208,128]{1,0:T(8,128)(2,1)S(1)} %sum_lat.1.refs_0_), channel_id=1, source_target_pairs={{0,2},{2,0},{4,6},{6,4},{1,3},{3,1},{5,7},{7,5},{8,10},{10,8},{12,... | collective-permute-start | bytes 159752 | tf_op jit(solution)/shard_map/ppermute | solution.py:618
  32.5 0.0 copy-done
  32.5 1.9 %ocean.1 = (f32[2,4,32,512]{3,2,1,0:T(8,128)}, f32[4,32,512]{2,1,0:T(8,128)}) custom-call(f32[2,4,32,512]{3,2,1,0:T(8,128)S(1)} %get-tuple-element.62.velo, f32[4,32,512]{2,1,0:T(8,128)S(1)} %get-tuple-element.63.temp, s32[32,512]{1,0:T(8,128)S(1)} %copy-done, bf16[16,640]{1,0:T(8,128)(2,1)S(1)} %get-tuple-element.101.mine, ...), custom_call_target="tpu_custom_call" | custom-call | flops 100000000 | bytes 4000000 | tf_op jit(solution)/shard_map/ocean/pallas_call | solution.py:757
  34.3 0.0 collective-permute-done.10.refs_3_
  34.3 2.3 %collective-permute-done.9.refs_2_ = s16[208,128]{1,0:T(8,128)(2,1)S(1)} collective-permute-done((s16[208,128]{1,0:T(8,128)(2,1)S(1)}, s16[208,128]{1,0:T(8,128)(2,1)S(1)}, u32[]{:S(2)}, u32[]{:S(2)}) %collective-permute-start.9) | collective-permute-done | bytes 53280 | tf_op jit(solution)/shard_map/ppermute | solution.py:618
  36.6 0.0 collective-permute-done.8.refs_1_
  36.6 0.1 sum_lon.1.refs_0_
  36.8 0.6 %collective-permute-start.13 = (s16[208,128]{1,0:T(8,128)(2,1)S(1)}, s16[208,128]{1,0:T(8,128)(2,1)S(1)}, u32[]{:S(2)}, u32[]{:S(2)}) collective-permute-start(s16[208,128]{1,0:T(8,128)(2,1)S(1)} %sum_lon.1.refs_0_), channel_id=1, source_target_pairs={{0,24},{8,16},{16,8},{24,0},{1,25},{9,17},{17,9},{25,1},{2,26},{10... | collective-permute-start | bytes 159752 | tf_op jit(solution)/shard_map/ppermute | solution.py:618
  37.4 1.4 %collective-permute-start.12 = (s16[208,128]{1,0:T(8,128)(2,1)S(1)}, s16[208,128]{1,0:T(8,128)(2,1)S(1)}, u32[]{:S(2)}, u32[]{:S(2)}) collective-permute-start(s16[208,128]{1,0:T(8,128)(2,1)S(1)} %sum_lon.1.refs_0_), channel_id=1, source_target_pairs={{0,16},{8,24},{16,0},{24,8},{1,17},{9,25},{17,1},{25,9},{2,18},{10... | collective-permute-start | bytes 159752 | tf_op jit(solution)/shard_map/ppermute | solution.py:618
  38.8 1.5 %collective-permute-start.11 = (s16[208,128]{1,0:T(8,128)(2,1)S(1)}, s16[208,128]{1,0:T(8,128)(2,1)S(1)}, u32[]{:S(2)}, u32[]{:S(2)}) collective-permute-start(s16[208,128]{1,0:T(8,128)(2,1)S(1)} %sum_lon.1.refs_0_), channel_id=1, source_target_pairs={{0,8},{8,0},{16,24},{24,16},{1,9},{9,1},{17,25},{25,17},{2,10},{10... | collective-permute-start | bytes 159752 | tf_op jit(solution)/shard_map/ppermute | solution.py:618
  40.3 1.6 %collective-permute-done.13.refs_3_ = s16[208,128]{1,0:T(8,128)(2,1)S(1)} collective-permute-done((s16[208,128]{1,0:T(8,128)(2,1)S(1)}, s16[208,128]{1,0:T(8,128)(2,1)S(1)}, u32[]{:S(2)}, u32[]{:S(2)}) %collective-permute-start.13) | collective-permute-done | bytes 53280 | tf_op jit(solution)/shard_map/ppermute | solution.py:618
  42.0 0.1 collective-permute-done.12.refs_2_
  42.1 0.8 %collective-permute-done.11.refs_1_ = s16[208,128]{1,0:T(8,128)(2,1)S(1)} collective-permute-done((s16[208,128]{1,0:T(8,128)(2,1)S(1)}, s16[208,128]{1,0:T(8,128)(2,1)S(1)}, u32[]{:S(2)}, u32[]{:S(2)}) %collective-permute-start.11) | collective-permute-done | bytes 53280 | tf_op jit(solution)/shard_map/ppermute | solution.py:618
  43.0 1.0 %finish.1 = (f32[9,3,2,64]{3,2,1,0:T(2,128)}, f32[2,9,64,64]{3,2,1,0:T(8,128)}, f32[2,9,2,64]{3,2,1,0:T(2,128)}) custom-call(s16[208,128]{1,0:T(8,128)(2,1)S(1)} %sum_lon.1.refs_0_, s16[208,128]{1,0:T(8,128)(2,1)S(1)} %collective-permute-done.11.refs_1_, s16[208,128]{1,0:T(8,128)(2,1)S(1)} %collective-permute-done.12.refs_2_, ...), custom_call_target="tpu_custom_call" | custom-call | tf_op jit(solution)/shard_map/finish/pallas_call | solution.py:769
Async XLA Ops:
  2.2 5.0 %collective-permute-start = (bf16[128,128]{1,0:T(8,128)(2,1)S(1)}, bf16[128,128]{1,0:T(8,128)(2,1)S(1)}, u32[]{:S(2)}, u32[]{:S(2)}) collective-permute-start(bf16[128,128]{1,0:T(8,128)(2,1)S(1)} %get-tuple-element.61), channel_id=1, source_target_pairs={{0,2},{1,7},{2,0},{3,5},{4,6},{5,3},{6,4},{7,1},{8,10},{9,15},{10,... | collective-permute-start | bytes 98312 | tf_op jit(solution)/shard_map/ppermute | solution.py:663
  7.2 1.9 %collective-permute-start.1 = (bf16[128,128]{1,0:T(8,128)(2,1)S(1)}, bf16[128,128]{1,0:T(8,128)(2,1)S(1)}, u32[]{:S(2)}, u32[]{:S(2)}) collective-permute-start(bf16[128,128]{1,0:T(8,128)(2,1)S(1)} %collective-permute-done.got.got_lon), channel_id=1, source_target_pairs={{0,1},{1,0},{2,3},{3,2},{4,5},{5,4},{6,7},{7,6},{8,9},{9,8},{10,11... | collective-permute-start | bytes 98312 | tf_op jit(solution)/shard_map/ppermute | solution.py:614
  9.1 4.3 %collective-permute-start.2 = (bf16[192,128]{1,0:T(8,128)(2,1)S(1)}, bf16[192,128]{1,0:T(8,128)(2,1)S(1)}, u32[]{:S(2)}, u32[]{:S(2)}) collective-permute-start(bf16[192,128]{1,0:T(8,128)(2,1)S(1)} %get-tuple-element.71), channel_id=1, source_target_pairs={{0,8},{1,25},{2,10},{3,27},{4,12},{5,29},{6,14},{7,31},{8,0},{9,17... | collective-permute-start | bytes 147464 | tf_op jit(solution)/shard_map/ppermute | solution.py:694
  13.4 1.2 %collective-permute-start.3 = (bf16[192,128]{1,0:T(8,128)(2,1)S(1)}, bf16[192,128]{1,0:T(8,128)(2,1)S(1)}, u32[]{:S(2)}, u32[]{:S(2)}) collective-permute-start(bf16[192,128]{1,0:T(8,128)(2,1)S(1)} %collective-permute-done.2.got.got_lat), channel_id=1, source_target_pairs={{0,1},{1,0},{2,3},{3,2},{4,5},{5,4},{6,7},{7,6},{8,9},{9,8},{10,11... | collective-permute-start | bytes 147464 | tf_op jit(solution)/shard_map/ppermute | solution.py:614
  19.8 6.0 %collective-permute-start.7 = (bf16[16,640]{1,0:T(8,128)(2,1)S(1)}, bf16[16,640]{1,0:T(8,128)(2,1)S(1)}, u32[]{:S(2)}, u32[]{:S(2)}) collective-permute-start(bf16[16,640]{1,0:T(8,128)(2,1)S(1)} %get-tuple-element.101.mine), channel_id=1, source_target_pairs={{0,1},{1,0},{2,3},{3,2},{4,5},{5,4},{6,7},{7,6},{8,9},{9,8},{10,11... | collective-permute-start | bytes 61448 | tf_op jit(solution)/shard_map/ppermute | solution.py:614
  20.1 5.8 %collective-permute-start.4 = (s16[160,128]{1,0:T(8,128)(2,1)S(1)}, s16[160,128]{1,0:T(8,128)(2,1)S(1)}, u32[]{:S(2)}, u32[]{:S(2)}) collective-permute-start(s16[160,128]{1,0:T(8,128)(2,1)S(1)} %get-tuple-element.98), channel_id=1, source_target_pairs={{0,8},{8,0},{16,24},{24,16},{1,9},{9,1},{17,25},{25,17},{2,10},{10... | collective-permute-start | bytes 122888 | tf_op jit(solution)/shard_map/ppermute | solution.py:618
  21.6 4.3 %collective-permute-start.5 = (s16[160,128]{1,0:T(8,128)(2,1)S(1)}, s16[160,128]{1,0:T(8,128)(2,1)S(1)}, u32[]{:S(2)}, u32[]{:S(2)}) collective-permute-start(s16[160,128]{1,0:T(8,128)(2,1)S(1)} %get-tuple-element.99), channel_id=1, source_target_pairs={{0,16},{8,24},{16,0},{24,8},{1,17},{9,25},{17,1},{25,9},{2,18},{10... | collective-permute-start | bytes 122888 | tf_op jit(solution)/shard_map/ppermute | solution.py:618
  23.0 4.9 %collective-permute-start.6 = (s16[160,128]{1,0:T(8,128)(2,1)S(1)}, s16[160,128]{1,0:T(8,128)(2,1)S(1)}, u32[]{:S(2)}, u32[]{:S(2)}) collective-permute-start(s16[160,128]{1,0:T(8,128)(2,1)S(1)} %get-tuple-element.100), channel_id=1, source_target_pairs={{0,24},{8,16},{16,8},{24,0},{1,25},{9,17},{17,9},{25,1},{2,26},{10... | collective-permute-start | bytes 122888 | tf_op jit(solution)/shard_map/ppermute | solution.py:618
  23.5 8.9 %copy-start = (s32[32,512]{1,0:T(8,128)S(1)}, s32[32,512]{1,0:T(8,128)}, u32[]{:S(2)}) copy-start(s32[32,512]{1,0:T(8,128)} %land.1) | copy-start | bytes 196612
  28.0 6.3 %collective-permute-start.10 = (s16[208,128]{1,0:T(8,128)(2,1)S(1)}, s16[208,128]{1,0:T(8,128)(2,1)S(1)}, u32[]{:S(2)}, u32[]{:S(2)}) collective-permute-start(s16[208,128]{1,0:T(8,128)(2,1)S(1)} %sum_lat.1.refs_0_), channel_id=1, source_target_pairs={{0,6},{2,4},{4,2},{6,0},{1,7},{3,5},{5,3},{7,1},{8,14},{10,12},{12... | collective-permute-start | bytes 159752 | tf_op jit(solution)/shard_map/ppermute | solution.py:618
  31.6 5.0 %collective-permute-start.9 = (s16[208,128]{1,0:T(8,128)(2,1)S(1)}, s16[208,128]{1,0:T(8,128)(2,1)S(1)}, u32[]{:S(2)}, u32[]{:S(2)}) collective-permute-start(s16[208,128]{1,0:T(8,128)(2,1)S(1)} %sum_lat.1.refs_0_), channel_id=1, source_target_pairs={{0,4},{2,6},{4,0},{6,2},{1,5},{3,7},{5,1},{7,3},{8,12},{10,14},{12... | collective-permute-start | bytes 159752 | tf_op jit(solution)/shard_map/ppermute | solution.py:618
  31.6 5.0 %collective-permute-start.8 = (s16[208,128]{1,0:T(8,128)(2,1)S(1)}, s16[208,128]{1,0:T(8,128)(2,1)S(1)}, u32[]{:S(2)}, u32[]{:S(2)}) collective-permute-start(s16[208,128]{1,0:T(8,128)(2,1)S(1)} %sum_lat.1.refs_0_), channel_id=1, source_target_pairs={{0,2},{2,0},{4,6},{6,4},{1,3},{3,1},{5,7},{7,5},{8,10},{10,8},{12,... | collective-permute-start | bytes 159752 | tf_op jit(solution)/shard_map/ppermute | solution.py:618
  36.8 5.2 %collective-permute-start.13 = (s16[208,128]{1,0:T(8,128)(2,1)S(1)}, s16[208,128]{1,0:T(8,128)(2,1)S(1)}, u32[]{:S(2)}, u32[]{:S(2)}) collective-permute-start(s16[208,128]{1,0:T(8,128)(2,1)S(1)} %sum_lon.1.refs_0_), channel_id=1, source_target_pairs={{0,24},{8,16},{16,8},{24,0},{1,25},{9,17},{17,9},{25,1},{2,26},{10... | collective-permute-start | bytes 159752 | tf_op jit(solution)/shard_map/ppermute | solution.py:618
  37.4 4.7 %collective-permute-start.12 = (s16[208,128]{1,0:T(8,128)(2,1)S(1)}, s16[208,128]{1,0:T(8,128)(2,1)S(1)}, u32[]{:S(2)}, u32[]{:S(2)}) collective-permute-start(s16[208,128]{1,0:T(8,128)(2,1)S(1)} %sum_lon.1.refs_0_), channel_id=1, source_target_pairs={{0,16},{8,24},{16,0},{24,8},{1,17},{9,25},{17,1},{25,9},{2,18},{10... | collective-permute-start | bytes 159752 | tf_op jit(solution)/shard_map/ppermute | solution.py:618
  38.8 4.1 %collective-permute-start.11 = (s16[208,128]{1,0:T(8,128)(2,1)S(1)}, s16[208,128]{1,0:T(8,128)(2,1)S(1)}, u32[]{:S(2)}, u32[]{:S(2)}) collective-permute-start(s16[208,128]{1,0:T(8,128)(2,1)S(1)} %sum_lon.1.refs_0_), channel_id=1, source_target_pairs={{0,8},{8,0},{16,24},{24,16},{1,9},{9,1},{17,25},{25,17},{2,10},{10... | collective-permute-start | bytes 159752 | tf_op jit(solution)/shard_map/ppermute | solution.py:618
